TPU v7x, 32 devices: a whole 2x2x4 slice. The times are simulated.
32 devices in a mesh: sec: 4 (over z), band: 4 (over y, x), ch: 2 (over core).
Axes of the slice: x: 2, y: 2, z: 4, core: 2. Of those that a mesh axis runs over, the one named last changes fastest.
Arguments:
- air_field_lattice: bfloat16 [64, 1024, 768], P(('sec', 'band', 'ch')), may hold values from -6 to 6
- associated_polynomial_matrix: bfloat16 [512, 64, 64], P(('sec', 'band', 'ch')), may hold values from -0.75 to 0.75
- harmonic_damping_factor: float32 [64, 768], replicated, may hold values from 0.5 to 2
- boundary_exchange_projector: bfloat16 [768, 8], replicated, may hold values from -0.21875 to 0.21875
- warmth_response_factor: float32 [768], replicated, may hold values from -4 to 4
- water_patch_fields: bfloat16 [192, 128, 4, 258], P(('sec', 'band', 'ch')), may hold values from -6 to 6
- kernel_coefficients: bfloat16 [3, 3, 128, 128], replicated, may hold values from -0.1875 to 0.1875
- local_exchange_matrix: bfloat16 [8, 128], replicated, may hold values from -2 to 2
- patch_average_matrix: float32 [8, 128], replicated, may hold values from -15 to 15
- water_kernel_offset: float32 [128], replicated, may hold values from -3 to 3
- water_readout_matrix: bfloat16 [128, 128], replicated, may hold values from -0.5 to 0.5
- patch_holder_index: int32 [32, 4], replicated, may hold values from 0 to 3, as said below
- water_point_indicator: int32 [192, 2, 256], P(('sec', 'band', 'ch')), may hold values from 0 to 1, as said below
- water_point_totals: int32 [192], P(('sec', 'band', 'ch')), may hold values from 0 to 512, as said below
Outputs:
- advanced_air_field: bfloat16 [64, 1024, 768], P(('sec', 'band', 'ch'))
- ocean_next: bfloat16 [192, 128, 2, 256], P(('sec', 'band', 'ch'))
Inputs may be any that keep to these rules, and one draw needn't show every extreme that they name: `patch_holder_index`: within each group of equal s and c, every band index owns either 6 or 2 of the group's tiles, half of them each way, so no device owns more than 6. `water_point_indicator`: empty slots are all zeros. `water_point_totals`: the number of ones of the slot in water_point_indicator.
All inputs are finite; a program needn't handle non-finite values.
Results may differ from a plain program's by a relative error of at most 0.0058.
Values may be sent and summed in bfloat16 or wider, within the bound.
No kernel may reach another device: no remote copies, remote signals or barrier semaphores. Data moves between devices by JAX's collectives and lax.ppermute only.
A program may use at most 128 MiB of HBM per device.

v0:
```python
import functools
import math

import jax
import jax.numpy as jnp
import numpy as np
from jax import lax
from jax.sharding import PartitionSpec as P

K = 512
AXES = ("sec", "band", "ch")
PARTS = (256, 512)


@functools.lru_cache(maxsize=None)
def dft_table(meridian_number):
    cell_index = np.arange(meridian_number, dtype=np.int64)[:, None]
    column = np.arange(2 * K, dtype=np.int64)[None, :]
    phase_angle = (cell_index * (column // 2) % meridian_number) * (2.0 * math.pi / meridian_number)
    table = np.where(column % 2 == 0, np.cos(phase_angle), -np.sin(phase_angle))
    return table.astype(np.float32).astype(jnp.bfloat16)


def ocean_update(
    state,
    tile_flux,
    mask_tile,
    count_tile,
    kernel_coefficients,
    local_exchange_matrix,
    patch_average_matrix,
    water_kernel_offset,
    water_readout_matrix,
):
    parallel_lines = mask_tile.shape[1]
    tile_width = mask_tile.shape[2]
    mask_f = mask_tile.astype(jnp.float32)
    masked = tile_flux * mask_tile[:, None].astype(jnp.bfloat16)
    fmean = (
        jnp.sum(masked.astype(jnp.float32), axis=(2, 3))
        / jnp.maximum(count_tile.astype(jnp.float32), 1.0)[:, None]
    )
    total = jnp.einsum(
        "fo,sfrw->sorw", local_exchange_matrix, masked, preferred_element_type=jnp.float32
    )
    for shift_row in range(3):
        for shift_col in range(3):
            window = state[
                :, :, shift_row : shift_row + parallel_lines, shift_col : shift_col + tile_width
            ]
            total = total + jnp.einsum(
                "io,sirw->sorw",
                kernel_coefficients[shift_row, shift_col],
                window,
                preferred_element_type=jnp.float32,
            )
    mean_term = jnp.sum(fmean[:, :, None] * patch_average_matrix[None], axis=1)
    total = total + mean_term[:, :, None, None] + water_kernel_offset[None, :, None, None]
    hidden = jax.nn.gelu(total, approximate=True).astype(jnp.bfloat16)
    update = jnp.einsum(
        "io,sirw->sorw", water_readout_matrix, hidden, preferred_element_type=jnp.float32
    )
    fresh = (
        state[:, :, 1 : 1 + parallel_lines, 1 : 1 + tile_width].astype(jnp.float32) + update
    ) * mask_f[:, None]
    return fresh.astype(jnp.bfloat16)


def shards(
    air_field_lattice,
    associated_polynomial_matrix,
    harmonic_damping_factor,
    boundary_exchange_projector,
    warmth_response_factor,
    water_patch_fields,
    kernel_coefficients,
    local_exchange_matrix,
    patch_average_matrix,
    water_kernel_offset,
    water_readout_matrix,
    patch_holder_index,
    water_point_indicator,
    water_point_totals,
):
    parallel_lines, meridian_number, channel_count = air_field_lattice.shape
    sec_count = lax.axis_size("sec")
    band_count = lax.axis_size("band")
    core_count = lax.axis_size("ch")
    device_count = sec_count * band_count * core_count
    total_cols = 2 * K
    per_device = total_cols // device_count
    slot_count = water_patch_fields.shape[0]
    mode_count = associated_polynomial_matrix.shape[0]
    lat_count = associated_polynomial_matrix.shape[1]
    table = dft_table(meridian_number)
    forward = jnp.asarray(np.ascontiguousarray(table.T))
    backward = jnp.asarray((table.astype(np.float32) * (2.0 / meridian_number)).astype(jnp.bfloat16))

    ends = np.cumsum((0,) + PARTS)
    spans = [slice(int(a), int(b)) for a, b in zip(ends[:-1], ends[1:])]
    collected = []
    for span in spans:
        fourier = jnp.einsum(
            "qn,anc->aqc", forward, air_field_lattice[:, :, span], preferred_element_type=jnp.float32
        ).astype(jnp.bfloat16)
        collected.append(lax.all_to_all(fourier, AXES, split_axis=1, concat_axis=0, tiled=True))
    returned = []
    for span, coeffs in zip(spans, collected):
        width = coeffs.shape[-1]
        pairs = coeffs.reshape(lat_count, mode_count, 2, width)
        spectrum = jnp.einsum(
            "mlt,tmpc->mlpc", associated_polynomial_matrix, pairs, preferred_element_type=jnp.float32
        )
        scaled = (spectrum * harmonic_damping_factor[None, :, None, span]).astype(jnp.bfloat16)
        damped = jnp.einsum(
            "mlt,mlpc->tmpc", associated_polynomial_matrix, scaled, preferred_element_type=jnp.float32
        ).astype(jnp.bfloat16).reshape(lat_count, per_device, width)
        returned.append(lax.all_to_all(damped, AXES, split_axis=0, concat_axis=1, tiled=True))

    flux_local = jnp.einsum(
        "anc,cf->fan",
        air_field_lattice,
        boundary_exchange_projector,
        preferred_element_type=jnp.float32,
    ).astype(jnp.bfloat16)
    gathered = lax.all_gather(flux_local, "band", axis=1, tiled=True)
    sec_id = lax.axis_index("sec")
    band_id = lax.axis_index("band")
    core_id = lax.axis_index("ch")
    owner_grid = patch_holder_index.reshape(sec_count, band_count, core_count, -1)
    tiles_per_row = owner_grid.shape[3]
    owner_group = lax.dynamic_index_in_dim(owner_grid, sec_id, 0, keepdims=False)
    owner_group = lax.dynamic_index_in_dim(owner_group, core_id, 1, keepdims=False)
    owner_flat = owner_group.reshape(-1)
    holders = jnp.arange(band_count, dtype=jnp.int32)
    mine_all = owner_flat[None, :] == holders[:, None]
    rank_all = jnp.cumsum(mine_all.astype(jnp.int32), axis=1) - 1
    slot_index = jnp.arange(slot_count, dtype=jnp.int32)
    pick_all = mine_all[:, None, :] & (rank_all[:, None, :] == slot_index[None, :, None])
    my_pick = lax.dynamic_index_in_dim(pick_all, band_id, 0, keepdims=False)
    flux_count = gathered.shape[0]
    tile_width = meridian_number // tiles_per_row
    pieces = gathered.reshape(flux_count, band_count, parallel_lines, tiles_per_row, tile_width)
    chooser = my_pick.reshape(slot_count, band_count, tiles_per_row).astype(jnp.bfloat16)
    tile_flux = jnp.einsum(
        "sbj,fbrjw->sfrw", chooser, pieces, preferred_element_type=jnp.float32
    ).astype(jnp.bfloat16)
    ocean_next = ocean_update(
        water_patch_fields,
        tile_flux,
        water_point_indicator,
        water_point_totals,
        kernel_coefficients,
        local_exchange_matrix,
        patch_average_matrix,
        water_kernel_offset,
        water_readout_matrix,
    )
    sea_slots = ocean_next[:, 0]
    sea_all = lax.all_gather(sea_slots, "band", axis=0, tiled=True)
    rank_tile = jnp.sum(jnp.where(mine_all, rank_all, 0), axis=0)
    my_owners = lax.dynamic_index_in_dim(owner_group, band_id, 0, keepdims=False)
    my_ranks = lax.dynamic_slice_in_dim(rank_tile, band_id * tiles_per_row, tiles_per_row)
    target = my_owners * slot_count + my_ranks
    selector = (
        target[:, None] == jnp.arange(band_count * slot_count, dtype=jnp.int32)[None, :]
    ).astype(jnp.bfloat16)
    water_patches = jnp.einsum(
        "jk,krw->rjw", selector, sea_all, preferred_element_type=jnp.float32
    ).astype(jnp.bfloat16)
    water_skin_warmth = water_patches.reshape(parallel_lines, meridian_number)
    pieces_out = []
    for span, coeffs in zip(spans, returned):
        rebuilt = jnp.einsum("nq,aqc->anc", backward, coeffs, preferred_element_type=jnp.float32)
        pieces_out.append(
            (
                air_field_lattice[:, :, span].astype(jnp.float32)
                + rebuilt
                + water_skin_warmth.astype(jnp.float32)[:, :, None]
                * warmth_response_factor[None, None, span]
            ).astype(jnp.bfloat16)
        )
    return (jnp.concatenate(pieces_out, axis=-1), ocean_next)


def solution(mesh):
    placed = (
        P(("sec", "band", "ch"), None, None),
        P(("sec", "band", "ch"), None, None),
        P(),
        P(),
        P(),
        P(("sec", "band", "ch"), None, None, None),
        P(),
        P(),
        P(),
        P(),
        P(),
        P(),
        P(("sec", "band", "ch"), None, None),
        P(("sec", "band", "ch")),
    )
    return jax.shard_map(
        shards,
        mesh=mesh,
        in_specs=placed,
        out_specs=(
            P(("sec", "band", "ch"), None, None),
            P(("sec", "band", "ch"), None, None, None),
        ),
        check_vma=False,
    )
```

profile of v0, /device:TPU:0, one launch (start us, length us, event | category | flops | bytes accessed | tf_op | source)
XLA Modules:
  0.0 183.1 jit_solution(2198496481197555965)
XLA Ops:
  0.6 0.0 copy-start
  0.6 3.1 %fusion.20 = bf16[2,1024,256]{2,1,0:T(8,128)(2,1)S(1)} fusion(bf16[1024,1024,1]{1,0,2:T(8,128)(2,1)} %constant.107, bf16[2,1024,768]{2,1,0:T(8,128)(2,1)} %param.16), kind=kOutput, calls=%fused_computation.30 | convolution fusion | flops 1074266112 | bytes 4194304 | tf_op jit(solution)/shard_map/qn,anc->aqc/dot_general | solution.py:103
  3.8 0.0 copy-start.24
  3.8 2.1 %copy.172 = bf16[2,1024,256]{2,0,1:T(2,128)(2,1)} copy(bf16[2,1024,256]{2,1,0:T(8,128)(2,1)S(1)} %fusion.20) | data formatting | bytes 2097152 | tf_op jit(solution)/shard_map/convert_element_type | solution.py:105
  5.9 7.3 %all-to-all-start = ((bf16[2,1024,256]{2,0,1:T(2,128)(2,1)}), bf16[2,1024,256]{2,0,1:T(2,128)(2,1)S(1)}, u32[]{:S(2)}, u32[]{:S(2)}) async-start(bf16[2,1024,256]{2,0,1:T(2,128)(2,1)} %copy.172), calls=%async_computation | async-start | bytes 2097152 | tf_op jit(solution)/shard_map/all_to_all | solution.py:106
  13.2 0.0 copy-done.24
  13.2 3.9 %convert_bitcast_fusion = bf16[2,1024,512]{2,1,0:T(8,128)(2,1)S(1)} fusion(bf16[1024,1024,1]{1,0,2:T(8,128)(2,1)S(1)} %copy-done.24, bf16[2,1024,768]{2,1,0:T(8,128)(2,1)} %param.16), kind=kOutput, calls=%fused_computation.14 | convolution fusion | flops 2148532224 | bytes 6291456 | tf_op jit(solution)/shard_map/qn,anc->aqc/dot_general | solution.py:103
  17.1 3.5 %copy.200 = bf16[2,1024,512]{2,0,1:T(2,128)(2,1)} copy(bf16[2,1024,512]{2,1,0:T(8,128)(2,1)S(1)} %convert_bitcast_fusion) | data formatting | bytes 4194304 | tf_op jit(solution)/shard_map/convert_element_type | solution.py:105
  20.6 18.8 %all-to-all-done = bf16[2,1024,256]{2,0,1:T(2,128)(2,1)S(1)} async-done(((bf16[2,1024,256]{2,0,1:T(2,128)(2,1)}), bf16[2,1024,256]{2,0,1:T(2,128)(2,1)S(1)}, u32[]{:S(2)}, u32[]{:S(2)}) %all-to-all-start) | async-done | bytes 1048608 | tf_op jit(solution)/shard_map/all_to_all | solution.py:106
  39.4 3.7 %all-to-all-start.2 = ((bf16[2,1024,512]{2,0,1:T(2,128)(2,1)}), bf16[2,1024,512]{2,0,1:T(2,128)(2,1)}, u32[]{:S(2)}, u32[]{:S(2)}) async-start(bf16[2,1024,512]{2,0,1:T(2,128)(2,1)} %copy.200), calls=%async_computation.2 | async-start | bytes 4194304 | tf_op jit(solution)/shard_map/all_to_all | solution.py:106
  43.2 0.0 copy-done.18
  43.2 0.0 copy-done.20
  43.2 0.1 copy.181
  43.3 0.1 eq.45
  43.4 0.2 reduce_window_sum.11
  43.7 2.8 %convolution_convert_fusion.3 = bf16[8,2,1024]{2,0,1:T(8,128)(2,1)S(1)} fusion(bf16[2,1024,768]{2,1,0:T(8,128)(2,1)} %param.16, bf16[768,8]{0,1:T(8,128)(2,1)S(1)} %copy-done.15), kind=kOutput, calls=%fused_computation.34 | convolution fusion | flops 25182208 | bytes 3190784 | tf_op jit(solution)/shard_map/anc,cf->fan/dot_general | solution.py:120
  46.5 15.8 %all_gather.6 = bf16[8,8,1024]{2,0,1:T(8,128)(2,1)S(1)} all-gather(bf16[8,2,1024]{2,0,1:T(8,128)(2,1)S(1)} %convolution_convert_fusion.3), channel_id=1, replica_groups=mesh['sec'=4,'band'=4,'ch'=2] {'band'}, dimensions={1}, use_global_device_ids=true | all-gather | bytes 163840 | tf_op jit(solution)/shard_map/all_gather | solution.py:126
  62.3 0.1 reshape.124
  62.4 0.1 fusion.82
  62.5 0.2 copy.288
  62.7 0.4 reshape.95
  63.2 0.2 slice-done
  63.3 1.2 convolution_convert_fusion.1
  64.6 0.0 copy-start.22
  64.6 0.0 copy-start.2
  64.6 1.6 copy.176
  66.2 25.9 %all-to-all-done.2 = bf16[2,1024,512]{2,0,1:T(2,128)(2,1)} async-done(((bf16[2,1024,512]{2,0,1:T(2,128)(2,1)}), bf16[2,1024,512]{2,0,1:T(2,128)(2,1)}, u32[]{:S(2)}, u32[]{:S(2)}) %all-to-all-start.2) | async-done | bytes 2097184 | tf_op jit(solution)/shard_map/all_to_all | solution.py:106
  92.1 4.3 %all-to-all-start.1 = ((bf16[64,32,256]{2,1,0:T(8,128)(2,1)}), bf16[64,32,256]{2,1,0:T(8,128)(2,1)}, u32[]{:S(2)}, u32[]{:S(2)}) async-start(bf16[64,32,256]{2,1,0:T(8,128)(2,1)} %copy.176), calls=%async_computation.1 | async-start | bytes 2097152 | tf_op jit(solution)/shard_map/all_to_all | solution.py:118
  96.4 0.3 convert_reduce_fusion
  96.7 0.1 copy.194
  96.8 8.6 %fusion.96 = (bf16[6,128,2,256]{1,2,3,0:T(2,128)(2,1)}, bf16[6,128,2,256]{1,2,3,0:T(2,128)(2,1)}, bf16[6,128,2,256]{1,2,3,0:T(2,128)(2,1)}, bf16[6,128,2,256]{1,...) fusion(bf16[6,128,4,258]{1,2,3,0:T(4,128)(2,1)S(1)} %copy-done.2), kind=kLoop, calls=%fused_computation.117 | loop fusion | bytes 14155776 | tf_op jit(solution)/shard_map/slice | solution.py:48
  105.4 3.4 %copy.287 = bf16[2,32,32,512]{3,2,0,1:T(8,128)(2,1)} copy(bf16[2,32,32,512]{3,0,2,1:T(2,128)(2,1)} %bitcast.59) | data formatting | bytes 4194304 | tf_op jit(solution)/shard_map/all_to_all | solution.py:106
  108.8 2.8 %reshape.100 = bf16[64,16,2,512]{3,2,1,0:T(2,128)(2,1)S(1)} reshape(bf16[32,2,32,512]{3,2,1,0:T(8,128)(2,1)} %bitcast.194) | data formatting | bytes 4194304 | tf_op jit(solution)/shard_map/reshape | solution.py:110
  111.6 4.9 %convolution_convert_fusion = bf16[16,2,512,64]{2,3,1,0:T(8,128)(2,1)} fusion(bf16[64,16,2,512]{3,2,1,0:T(2,128)(2,1)S(1)} %reshape.100, f32[64,512]{1,0:T(8,128)S(1)} %slice-done.1, bf16[16,64,64]{2,1,0:T(8,128)(2,1)S(1)} %copy-done), kind=kOutput, calls=%fused_computation.15 | convolution fusion | flops 271581184 | bytes 4456448 | tf_op jit(solution)/shard_map/mlt,mlpc->tmpc/dot_general | solution.py:115
  116.5 4.1 %copy.204 = bf16[64,32,512]{2,1,0:T(8,128)(2,1)} copy(bf16[64,32,512]{2,0,1:T(8,128)(2,1)} %bitcast.192) | data formatting | bytes 4194304 | tf_op jit(solution)/shard_map/reshape | solution.py:117
  120.6 1.8 all-to-all-done.1
  122.4 3.8 %all-to-all-start.3 = ((bf16[64,32,512]{2,1,0:T(8,128)(2,1)}), bf16[64,32,512]{2,1,0:T(8,128)(2,1)S(1)}, u32[]{:S(2)}, u32[]{:S(2)}) async-start(bf16[64,32,512]{2,1,0:T(8,128)(2,1)} %copy.204), calls=%async_computation.3 | async-start | bytes 4194304 | tf_op jit(solution)/shard_map/all_to_all | solution.py:118
  126.3 0.1 multiply_reduce_fusion
  126.3 0.0 copy-done.13
  126.4 0.0 copy-start.11
  126.4 1.5 fusion.51
  127.9 1.5 fusion.29
  129.4 1.5 fusion.31
  130.9 1.5 fusion.33
  132.5 1.6 fusion.35
  134.1 1.6 fusion.37
  135.6 0.0 copy-done.7
  135.7 1.5 fusion.39
  137.2 1.6 fusion.41
  138.8 1.5 fusion.43
  140.3 7.6 %fusion.19 = bf16[6,128,2,256]{1,3,2,0:T(8,128)(2,1)} fusion(f32[6,2,256,128]{3,2,1,0:T(8,128)} %fusion.29, f32[6,2,256,128]{3,2,1,0:T(8,128)} %fusion.31, f32[6,2,256,128]{3,2,1,0:T(8,128)} %fusion.33, f32[6,2,256,128]{3,2,1,0:T(8,128)} %fusion.35, f32[6,2,256,128]{3,2,1,0:T(8,128)} %fusion.51, f32[6,2,256,128]{3,2,1,0:T(8,128)} %fusion.37, ...), kind=kOutput, calls=%fused_computation.27 | convolution fusion | flops 116391936 | bytes 15828480 | tf_op jit(solution)/shard_map/io,sirw->sorw/dot_general | solution.py:60
  147.9 3.1 %copy.208 = bf16[6,128,2,256]{3,2,1,0:T(2,128)(2,1)} copy(bf16[6,128,2,256]{1,3,2,0:T(8,128)(2,1)} %fusion.19) | data formatting | bytes 1572864
  151.0 0.3 copy.198
  151.3 8.8 %all-gather = bf16[24,1,2,256]{3,2,1,0:T(2,128)(2,1)S(1)} all-gather(bf16[6,1,2,256]{3,2,1,0:T(2,128)(2,1)S(1)} %copy.198), channel_id=2, replica_groups=mesh['sec'=4,'band'=4,'ch'=2] {'band'}, dimensions={0}, use_global_device_ids=true | all-gather | bytes 30720 | tf_op jit(solution)/shard_map/all_gather | solution.py:160
  160.1 0.1 fusion.90
  160.2 0.2 fusion.24
  160.4 1.3 copy.177
  161.7 2.5 %fusion.4 = bf16[2,1024,256]{2,1,0:T(8,128)(2,1)S(1)} fusion(bf16[1024,1024,1]{1,0,2:T(8,128)(2,1)S(1)} %copy-done.23, bf16[2,1024,256]{2,1,0:T(8,128)(2,1)S(1)} %bitcast.200, f32[256]{0:T(256)S(1)} %slice-done.2, f32[2,1024]{1,0:T(2,128)S(1)} %bitcast.203, bf16[2,1024,768]{2,1,0:T(8,128)(2,1)} %param.16), kind=kOutput, calls=%fused_computation.9 | convolution fusion | flops 1076363264 | bytes 5252096 | tf_op jit(solution)/shard_map/nq,aqc->anc/dot_general | solution.py:174
  164.3 10.9 %all-to-all-done.3 = bf16[64,32,512]{2,1,0:T(8,128)(2,1)S(1)} async-done(((bf16[64,32,512]{2,1,0:T(8,128)(2,1)}), bf16[64,32,512]{2,1,0:T(8,128)(2,1)S(1)}, u32[]{:S(2)}, u32[]{:S(2)}) %all-to-all-start.3) | async-done | bytes 2097184 | tf_op jit(solution)/shard_map/all_to_all | solution.py:118
  175.1 0.1 copy.205
  175.3 1.7 copy-done.4
  177.0 4.2 %fusion.1 = bf16[2,1024,512]{2,1,0:T(8,128)(2,1)S(1)} fusion(bf16[1024,1024,1]{1,0,2:T(8,128)(2,1)} %constant.108, bf16[2,1024,512]{2,1,0:T(8,128)(2,1)S(1)} %bitcast.199, f32[512]{0:T(512)S(1)} %slice.102, f32[2,1024]{1,0:T(2,128)S(1)} %bitcast.204, bf16[2,1024,768]{2,1,0:T(8,128)(2,1)S(1)} %copy-done.4), kind=kOutput, calls=%fused_computation.2 | convolution fusion | flops 2152726528 | bytes 8398848 | tf_op jit(solution)/shard_map/nq,aqc->anc/dot_general | solution.py:174
  181.2 1.9 %pad_maximum_fusion = bf16[2,1024,768]{2,1,0:T(8,128)(2,1)} fusion(bf16[2,1024,512]{2,1,0:T(8,128)(2,1)S(1)} %fusion.1, bf16[2,1024,256]{2,1,0:T(8,128)(2,1)S(1)} %fusion.4), kind=kLoop, calls=%fused_computation.5 | loop fusion | flops 6291456 | bytes 6291456 | tf_op jit(solution)/shard_map/concatenate | solution.py:183
  183.1 0.0 copy-done.1
  (54 shorter events, 0.2 us)
Async XLA Ops:
  0.6 62.5 %copy-start = (bf16[16,64,64]{2,1,0:T(8,128)(2,1)S(1)}, bf16[16,64,64]{2,1,0:T(8,128)(2,1)}, u32[]{:S(2)}) copy-start(bf16[16,64,64]{2,1,0:T(8,128)(2,1)} %param.17) | copy-start | bytes 393220
  3.8 9.4 %copy-start.24 = (bf16[1024,1024,1]{1,0,2:T(8,128)(2,1)S(1)}, bf16[1024,1024,1]{1,0,2:T(8,128)(2,1)}, u32[]{:S(2)}) copy-start(bf16[1024,1024,1]{1,0,2:T(8,128)(2,1)} %constant.107) | copy-start | bytes 6291460
  5.9 33.5 %all-to-all-start = ((bf16[2,1024,256]{2,0,1:T(2,128)(2,1)}), bf16[2,1024,256]{2,0,1:T(2,128)(2,1)S(1)}, u32[]{:S(2)}, u32[]{:S(2)}) async-start(bf16[2,1024,256]{2,0,1:T(2,128)(2,1)} %copy.172), calls=%async_computation | async-start | bytes 2097152 | tf_op jit(solution)/shard_map/all_to_all | solution.py:106
  20.6 22.6 %copy-start.18 = (f32[768]{0:T(1024)S(1)}, f32[768]{0:T(1024)}, u32[]{:S(2)}) copy-start(f32[768]{0:T(1024)} %param.20) | copy-start | bytes 9220
  20.6 22.6 %copy-start.20 = (s32[32,4]{0,1:T(4,128)S(1)}, s32[32,4]{0,1:T(4,128)}, u32[]{:S(2)}) copy-start(s32[32,4]{0,1:T(4,128)} %param.27) | copy-start | bytes 1540
  20.6 23.0 %copy-start.16 = (s32[6,2,256]{2,1,0:T(2,128)S(1)}, s32[6,2,256]{2,1,0:T(2,128)}, u32[]{:S(2)}) copy-start(s32[6,2,256]{2,1,0:T(2,128)} %param.28) | copy-start | bytes 36868
  20.6 23.1 %copy-start.15 = (bf16[768,8]{0,1:T(8,128)(2,1)S(1)}, bf16[768,8]{0,1:T(8,128)(2,1)}, u32[]{:S(2)}) copy-start(bf16[768,8]{0,1:T(8,128)(2,1)} %param.19) | copy-start | bytes 36868
  39.4 52.6 %all-to-all-start.2 = ((bf16[2,1024,512]{2,0,1:T(2,128)(2,1)}), bf16[2,1024,512]{2,0,1:T(2,128)(2,1)}, u32[]{:S(2)}, u32[]{:S(2)}) async-start(bf16[2,1024,512]{2,0,1:T(2,128)(2,1)} %copy.200), calls=%async_computation.2 | async-start | bytes 4194304 | tf_op jit(solution)/shard_map/all_to_all | solution.py:106
  62.5 0.8 slice-start
  64.6 31.8 %copy-start.22 = (s32[6]{0:T(128)S(1)}, s32[6]{0:T(128)}, u32[]{:S(2)}) copy-start(s32[6]{0:T(128)} %param.29) | copy-start | bytes 76
  64.6 32.2 %copy-start.2 = (bf16[6,128,4,258]{1,2,3,0:T(4,128)(2,1)S(1)}, bf16[6,128,4,258]{1,2,3,0:T(4,128)(2,1)}, u32[]{:S(2)}) copy-start(bf16[6,128,4,258]{1,2,3,0:T(4,128)(2,1)} %param.21) | copy-start | bytes 4755460
  92.1 30.4 %all-to-all-start.1 = ((bf16[64,32,256]{2,1,0:T(8,128)(2,1)}), bf16[64,32,256]{2,1,0:T(8,128)(2,1)}, u32[]{:S(2)}, u32[]{:S(2)}) async-start(bf16[64,32,256]{2,1,0:T(8,128)(2,1)} %copy.176), calls=%async_computation.1 | async-start | bytes 2097152 | tf_op jit(solution)/shard_map/all_to_all | solution.py:118
  108.8 2.8 %slice-start.1 = ((f32[64,768]{1,0:T(8,128)}), f32[64,512]{1,0:T(8,128)S(1)}, s32[]{:S(2)}) async-start(f32[64,768]{1,0:T(8,128)} %param.18), calls=%async_computation.5 | async-start | bytes 262144 | tf_op jit(solution)/shard_map/slice | solution.py:114
  120.6 5.6 %copy-start.17 = (f32[8,128]{1,0:T(8,128)S(1)}, f32[8,128]{1,0:T(8,128)}, u32[]{:S(2)}) copy-start(f32[8,128]{1,0:T(8,128)} %param.24) | copy-start | bytes 12292
  120.6 5.7 %copy-start.13 = (bf16[3,3,128,128]{3,2,1,0:T(8,128)(2,1)S(1)}, bf16[3,3,128,128]{3,2,1,0:T(8,128)(2,1)}, u32[]{:S(2)}) copy-start(bf16[3,3,128,128]{3,2,1,0:T(8,128)(2,1)} %param.22) | copy-start | bytes 884740
  122.4 52.7 %all-to-all-start.3 = ((bf16[64,32,512]{2,1,0:T(8,128)(2,1)}), bf16[64,32,512]{2,1,0:T(8,128)(2,1)S(1)}, u32[]{:S(2)}, u32[]{:S(2)}) async-start(bf16[64,32,512]{2,1,0:T(8,128)(2,1)} %copy.204), calls=%async_computation.3 | async-start | bytes 4194304 | tf_op jit(solution)/shard_map/all_to_all | solution.py:118
  126.3 1.6 copy-start.12
  126.4 3.0 %copy-start.11 = (bf16[6,128,2,256]{1,2,3,0:T(2,128)(2,1)S(1)}, bf16[6,128,2,256]{1,2,3,0:T(2,128)(2,1)}, u32[]{:S(2)}) copy-start(bf16[6,128,2,256]{1,2,3,0:T(2,128)(2,1)} %get-tuple-element.15) | copy-start | bytes 2359300
  127.9 3.0 %copy-start.10 = (bf16[6,128,2,256]{1,2,3,0:T(2,128)(2,1)S(1)}, bf16[6,128,2,256]{1,2,3,0:T(2,128)(2,1)}, u32[]{:S(2)}) copy-start(bf16[6,128,2,256]{1,2,3,0:T(2,128)(2,1)} %get-tuple-element.16) | copy-start | bytes 2359300
  129.4 3.1 %copy-start.9 = (bf16[6,128,2,256]{1,2,3,0:T(2,128)(2,1)S(1)}, bf16[6,128,2,256]{1,2,3,0:T(2,128)(2,1)}, u32[]{:S(2)}) copy-start(bf16[6,128,2,256]{1,2,3,0:T(2,128)(2,1)} %get-tuple-element.17) | copy-start | bytes 2359300
  130.9 3.2 %copy-start.8 = (bf16[6,128,2,256]{1,2,3,0:T(2,128)(2,1)S(1)}, bf16[6,128,2,256]{1,2,3,0:T(2,128)(2,1)}, u32[]{:S(2)}) copy-start(bf16[6,128,2,256]{1,2,3,0:T(2,128)(2,1)} %get-tuple-element.18) | copy-start | bytes 2359300
  132.5 3.2 %copy-start.7 = (bf16[6,128,2,256]{1,2,3,0:T(2,128)(2,1)S(1)}, bf16[6,128,2,256]{1,2,3,0:T(2,128)(2,1)}, u32[]{:S(2)}) copy-start(bf16[6,128,2,256]{1,2,3,0:T(2,128)(2,1)} %get-tuple-element.19) | copy-start | bytes 2359300
  134.1 3.1 %copy-start.6 = (bf16[6,128,2,256]{1,2,3,0:T(2,128)(2,1)S(1)}, bf16[6,128,2,256]{1,2,3,0:T(2,128)(2,1)}, u32[]{:S(2)}) copy-start(bf16[6,128,2,256]{1,2,3,0:T(2,128)(2,1)} %get-tuple-element.20) | copy-start | bytes 2359300
  135.6 3.1 %copy-start.5 = (bf16[6,128,2,256]{1,2,3,0:T(2,128)(2,1)S(1)}, bf16[6,128,2,256]{1,2,3,0:T(2,128)(2,1)}, u32[]{:S(2)}) copy-start(bf16[6,128,2,256]{1,2,3,0:T(2,128)(2,1)} %get-tuple-element.14) | copy-start | bytes 2359300
  137.2 3.1 %copy-start.14 = (bf16[128,128]{1,0:T(8,128)(2,1)S(1)}, bf16[128,128]{1,0:T(8,128)(2,1)}, u32[]{:S(2)}) copy-start(bf16[128,128]{1,0:T(8,128)(2,1)} %param.26) | copy-start | bytes 98308
  137.2 3.1 %copy-start.19 = (bf16[8,128]{1,0:T(8,128)(2,1)S(1)}, bf16[8,128]{1,0:T(8,128)(2,1)}, u32[]{:S(2)}) copy-start(bf16[8,128]{1,0:T(8,128)(2,1)} %param.23) | copy-start | bytes 6148
  137.2 3.1 %copy-start.21 = (f32[128]{0:T(128)S(1)}, f32[128]{0:T(128)}, u32[]{:S(2)}) copy-start(f32[128]{0:T(128)} %param.25) | copy-start | bytes 1540
  147.9 3.1 %copy-start.3 = (bf16[6,128,2,256]{1,3,2,0:T(8,128)(2,1)S(1)}, bf16[6,128,2,256]{1,3,2,0:T(8,128)(2,1)}, u32[]{:S(2)}) copy-start(bf16[6,128,2,256]{1,3,2,0:T(8,128)(2,1)} %fusion.19) | copy-start | bytes 2359300
  147.9 13.8 %slice-start.2 = ((f32[768]{0:T(1024)}), f32[256]{0:T(256)S(1)}, s32[]{:S(2)}) async-start(f32[768]{0:T(1024)} %param.20), calls=%async_computation.6 | async-start | bytes 2048 | tf_op jit(solution)/shard_map/slice | solution.py:180
  151.3 10.4 %copy-start.23 = (bf16[1024,1024,1]{1,0,2:T(8,128)(2,1)S(1)}, bf16[1024,1024,1]{1,0,2:T(8,128)(2,1)}, u32[]{:S(2)}) copy-start(bf16[1024,1024,1]{1,0,2:T(8,128)(2,1)} %constant.108) | copy-start | bytes 6291460
  175.1 1.9 %copy-start.4 = (bf16[2,1024,768]{2,1,0:T(8,128)(2,1)S(1)}, bf16[2,1024,768]{2,1,0:T(8,128)(2,1)}, u32[]{:S(2)}) copy-start(bf16[2,1024,768]{2,1,0:T(8,128)(2,1)} %param.16) | copy-start | bytes 9437188
  177.0 6.1 %copy-start.1 = (bf16[16,64,64]{2,1,0:T(8,128)(2,1)S(1)}, bf16[16,64,64]{2,1,0:T(8,128)(2,1)}, u32[]{:S(2)}) copy-start(bf16[16,64,64]{2,1,0:T(8,128)(2,1)} %param.17) | copy-start | bytes 393220
where the time goes:
time: 184 us; the launch traced here: 183 us
  waiting for transfers between devices  57.4 us (31%)
  matrix products  44.7 us (24%)
  local copies, waits for them, and re-layouts  33.9 us (18%)
  blocking collectives  24.6 us (13%)
  starting transfers between devices  19.2 us (10%)
  other arithmetic  2.35 us (1%)
    all_to_all x2, waiting for transfers between devices, shards(): lax.all_to_all(fourier, AXES, split_axis=1, concat_axis=0, tiled=True)  44.7 us
    all_gather x1, blocking collectives, shards(): gathered = lax.all_gather(flux_local, 'band', axis=1, tiled=True)  15.8 us
    dot_general x9, matrix products, ocean_update(): jnp.einsum('io,sirw->sorw', kernel_coefficients[shift_row, shift_col], wi...  13.9 us
    all_to_all x2, waiting for transfers between devices, shards(): lax.all_to_all(damped, AXES, split_axis=0, concat_axis=1, tiled=True)  12.6 us
    all_to_all x2, starting transfers between devices, shards(): lax.all_to_all(fourier, AXES, split_axis=1, concat_axis=0, tiled=True)  11 us
    all_gather x1, blocking collectives, shards(): sea_all = lax.all_gather(sea_slots, 'band', axis=0, tiled=True)  8.83 us
    slice x1, local copies, waits for them, and re-layouts, ocean_update(): state[:, :, shift_row:shift_row + parallel_lines, shift_col:shift_col + t...  8.6 us
    all_to_all x2, starting transfers between devices, shards(): lax.all_to_all(damped, AXES, split_axis=0, concat_axis=1, tiled=True)  8.13 us
  transfers between devices with their start and end apart: 4, of which 4 were waited for; matrix products, arithmetic and copies ran while one was open for 37% of the time, Pallas kernels for 0%

commit v1 on v0

--- a/solution.py
+++ b/solution.py
@@ -5,11 +5,15 @@
 import jax.numpy as jnp
 import numpy as np
 from jax import lax
+from jax.experimental import pallas as pl
+from jax.experimental.pallas import tpu as pltpu
 from jax.sharding import PartitionSpec as P
 
 K = 512
 AXES = ("sec", "band", "ch")
-PARTS = (256, 512)
+GROUP = 16
+SLIM = 128
+MIB = 1024 * 1024
 
 
 @functools.lru_cache(maxsize=None)
@@ -19,6 +23,16 @@
     phase_angle = (cell_index * (column // 2) % meridian_number) * (2.0 * math.pi / meridian_number)
     table = np.where(column % 2 == 0, np.cos(phase_angle), -np.sin(phase_angle))
     return table.astype(np.float32).astype(jnp.bfloat16)
+
+
+@functools.lru_cache(maxsize=None)
+def folded_tables(meridian_number, groups):
+    half = meridian_number // 2
+    table = dft_table(meridian_number)[:half].astype(np.float32)
+    per_parity = table.reshape(half, groups, -1, 2, 2).transpose(3, 1, 2, 4, 0)
+    forward = per_parity.reshape(2, -1, half)
+    backward = forward.transpose(0, 2, 1) * (2.0 / meridian_number)
+    return tuple(np.ascontiguousarray(x).astype(jnp.bfloat16) for x in (forward, backward))
 
 
 def ocean_update(
@@ -64,6 +78,317 @@
         state[:, :, 1 : 1 + parallel_lines, 1 : 1 + tile_width].astype(jnp.float32) + update
     ) * mask_f[:, None]
     return fresh.astype(jnp.bfloat16)
+
+
+def compiler_params():
+    return pltpu.CompilerParams(vmem_limit_bytes=60 * MIB)
+
+
+def cost(flops, *arrays):
+    return pl.CostEstimate(
+        flops=flops, bytes_accessed=sum(x.size * x.dtype.itemsize for x in arrays), transcendentals=0
+    )
+
+
+def fold(low, high, odd):
+    low, high = low.astype(jnp.float32), high.astype(jnp.float32)
+    return jnp.where(odd == 1, low - high, low + high).astype(jnp.bfloat16)
+
+
+def lane_spans(width, size=256):
+    return [slice(at, min(at + size, width)) for at in range(0, width, size)]
+
+
+def analyse_wide(air, table, width, groups):
+    lines, cells, _ = air.shape
+    half = cells // 2
+    out = jax.ShapeDtypeStruct((groups, lines, 2 * GROUP, width), jnp.bfloat16)
+
+    def body(table_ref, air_ref, out_ref):
+        for span in lane_spans(width):
+            low = air_ref[0, :half, span].astype(jnp.float32)
+            high = air_ref[0, half:, span].astype(jnp.float32)
+            for odd, folded in enumerate((low + high, low - high)):
+                coeffs = jnp.dot(table_ref[odd], folded.astype(jnp.bfloat16), preferred_element_type=jnp.float32)
+                out_ref[:, :, odd * GROUP : (odd + 1) * GROUP, span] = coeffs.astype(jnp.bfloat16).reshape(
+                    groups, 1, GROUP, -1
+                )
+
+    return pl.pallas_call(
+        body,
+        grid=(lines,),
+        in_specs=[
+            pl.BlockSpec(table.shape, lambda a: (0, 0, 0)),
+            pl.BlockSpec((1, cells, width), lambda a: (a, 0, 0)),
+        ],
+        out_specs=pl.BlockSpec((groups, 1, 2 * GROUP, width), lambda a: (0, a, 0, 0)),
+        out_shape=out,
+        compiler_params=compiler_params(),
+        cost_estimate=cost(lines * cells * cells * width, table, air, out),
+        name="analyse_wide",
+    )(table, air)
+
+
+def analyse_slim(air, table, start, sec, sections, groups):
+    lines, cells, channels = air.shape
+    half = cells // 2
+    width = channels - start
+    plane = groups // sections
+    out = jax.ShapeDtypeStruct((lines, plane, 2 * GROUP, width), jnp.bfloat16)
+
+    def body(sec_ref, table_ref, air_ref, *refs):
+        outs, blocks = refs[:-1], refs[-1]
+        both = jnp.concatenate([air_ref[a] for a in range(lines)], axis=1)
+        folded = fold(both[:half], both[half:], pl.program_id(0))
+        coeffs = jnp.dot(table_ref[0], folded, preferred_element_type=jnp.float32)
+        blocks[...] = coeffs.astype(jnp.bfloat16).reshape(sections, plane, GROUP, lines * width)
+        for o, out_ref in enumerate(outs):
+            for a in range(lines):
+                out_ref[a] = blocks[sec_ref[0] ^ o, :, :, a * width : (a + 1) * width]
+
+    return pl.pallas_call(
+        body,
+        grid=(2,),
+        in_specs=[
+            pl.BlockSpec(memory_space=pltpu.SMEM),
+            pl.BlockSpec((1,) + table.shape[1:], lambda p: (p, 0, 0)),
+            pl.BlockSpec((lines, cells, width), lambda p: (0, 0, start // width)),
+        ],
+        out_specs=[pl.BlockSpec((lines, plane, GROUP, width), lambda p: (0, 0, p, 0))] * sections,
+        out_shape=[out] * sections,
+        scratch_shapes=[pltpu.VMEM((sections, plane, GROUP, lines * width), jnp.bfloat16)],
+        compiler_params=compiler_params(),
+        cost_estimate=cost(lines * cells * cells * width, table, *[out] * 2 * sections),
+        name="analyse_slim",
+    )(sec, table, air)
+
+
+def wavenumber_at(row):
+    return row % GROUP // 2 * 2 + row // GROUP
+
+
+def damp(transform, coeffs, damping):
+    spectrum = jnp.dot(transform, coeffs, preferred_element_type=jnp.float32)
+    scaled = (spectrum * damping).astype(jnp.bfloat16)
+    back = lax.dot_general(transform, scaled, (((0,), (0,)), ((), ())), preferred_element_type=jnp.float32)
+    return back.astype(jnp.bfloat16)
+
+
+def latitudinal_wide(coeffs, matrix, damping):
+    devices, lines, rows, width = coeffs.shape
+    modes, degrees, lats = matrix.shape
+
+    def body(x_ref, matrix_ref, damping_ref, out_ref):
+        for span in lane_spans(width):
+            by_coeff = jnp.swapaxes(x_ref[:, :, :, span].reshape(lats, rows, -1), 0, 1)
+            results = [
+                damp(matrix_ref[wavenumber_at(row)], by_coeff[row], damping_ref[:, span]) for row in range(rows)
+            ]
+            out_ref[:, :, :, span] = jnp.swapaxes(jnp.stack(results), 0, 1).reshape(devices, lines, rows, -1)
+
+    return pl.pallas_call(
+        body,
+        grid=(1,),
+        in_specs=[whole(coeffs), whole(matrix), pl.BlockSpec((degrees, width), lambda i: (0, 0))],
+        out_specs=whole(coeffs),
+        out_shape=jax.ShapeDtypeStruct(coeffs.shape, jnp.bfloat16),
+        compiler_params=compiler_params(),
+        cost_estimate=cost(4 * rows * degrees * lats * width, coeffs, coeffs, matrix),
+        name="latitudinal_wide",
+    )(coeffs, matrix, damping)
+
+
+def whole(x):
+    return pl.BlockSpec(x.shape, lambda *_: (0,) * len(x.shape))
+
+
+def to_plane(parts, place):
+    lines, plane, rows, width = parts[0].shape
+    sections = len(parts)
+    out = jax.ShapeDtypeStruct((sections, lines, rows, width), jnp.bfloat16)
+
+    def body(place_ref, *refs):
+        for p, out_ref in enumerate(refs[sections:]):
+            for o in range(sections):
+                for a in range(lines):
+                    out_ref[o, a] = refs[o][a, place_ref[0] ^ p]
+
+    return pl.pallas_call(
+        body,
+        grid=(1,),
+        in_specs=[pl.BlockSpec(memory_space=pltpu.SMEM)] + [whole(parts[0])] * sections,
+        out_specs=[whole(out)] * plane,
+        out_shape=[out] * plane,
+        compiler_params=compiler_params(),
+        cost_estimate=cost(0, *parts, *parts),
+        name="to_plane",
+    )(place, *parts)
+
+
+def from_plane(parts, place):
+    sections, lines, rows, width = parts[0].shape
+    plane = len(parts)
+    out = jax.ShapeDtypeStruct((lines, plane, rows, width), jnp.bfloat16)
+
+    def body(place_ref, *refs):
+        for o, out_ref in enumerate(refs[plane:]):
+            for p in range(plane):
+                for a in range(lines):
+                    out_ref[a, place_ref[0] ^ p] = refs[p][o, a]
+
+    return pl.pallas_call(
+        body,
+        grid=(1,),
+        in_specs=[pl.BlockSpec(memory_space=pltpu.SMEM)] + [whole(parts[0])] * plane,
+        out_specs=[whole(out)] * sections,
+        out_shape=[out] * sections,
+        compiler_params=compiler_params(),
+        cost_estimate=cost(0, *parts, *parts),
+        name="from_plane",
+    )(place, *parts)
+
+
+def latitudinal_slim(parts, matrix, damping, start):
+    sections, lines, rows, width = parts[0].shape
+    plane = len(parts)
+    degrees = damping.shape[0]
+    own = sections * lines
+    out = jax.ShapeDtypeStruct(parts[0].shape, jnp.bfloat16)
+
+    def body(matrix_ref, damping_ref, *refs):
+        latitudes = jnp.concatenate([ref[...].reshape(own, rows, width) for ref in refs[:plane]], axis=0)
+        by_coeff = jnp.swapaxes(latitudes, 0, 1)
+        results = [
+            damp(matrix_ref[wavenumber_at(row)], by_coeff[row], damping_ref[...]) for row in range(rows)
+        ]
+        by_lat = jnp.swapaxes(jnp.stack(results), 0, 1)
+        for p, out_ref in enumerate(refs[plane:]):
+            out_ref[...] = by_lat[p * own : (p + 1) * own].reshape(out_ref.shape)
+
+    return pl.pallas_call(
+        body,
+        grid=(1,),
+        in_specs=[
+            whole(matrix),
+            pl.BlockSpec((degrees, width), lambda i: (0, start // width)),
+        ]
+        + [whole(out)] * plane,
+        out_specs=[whole(out)] * plane,
+        out_shape=[out] * plane,
+        compiler_params=compiler_params(),
+        cost_estimate=cost(4 * rows * degrees * plane * own * width, matrix, *parts, *parts),
+        name="latitudinal_slim",
+    )(matrix, damping, *parts)
+
+
+def advance(air, rebuilt, sea, warmth):
+    warmed = lax.dot_general(sea, warmth, (((0,), (0,)), ((), ())), preferred_element_type=jnp.float32)
+    return (air.astype(jnp.float32) + rebuilt + warmed).astype(jnp.bfloat16)
+
+
+def three_parts(values):
+    parts, rest = [], values
+    for _ in range(3):
+        parts.append(lax.reduce_precision(rest, 8, 7))
+        rest = rest - parts[-1]
+    parts += [jnp.zeros_like(values)] * (GROUP - 3)
+    return jnp.stack(parts).astype(jnp.bfloat16)
+
+
+def synthesise_slim(parts, table, air, sea, warmth, start, sec):
+    lines, plane, rows, width = parts[0].shape
+    sections = len(parts)
+    half = air.shape[2]
+
+    def body(sec_ref, table_ref, air_ref, sea_ref, warmth_ref, *refs):
+        part_refs, out_ref, gathered = refs[:sections], refs[-2], refs[-1]
+        for o, part_ref in enumerate(part_refs):
+            for a in range(lines):
+                for odd in range(2):
+                    gathered[odd, sec_ref[0] ^ o, :, :, a * width : (a + 1) * width] = part_ref[
+                        a, :, odd * GROUP : (odd + 1) * GROUP, :
+                    ]
+        even, odd = (
+            jnp.dot(
+                table_ref[odd],
+                gathered[odd].reshape(sections * plane * GROUP, lines * width),
+                preferred_element_type=jnp.float32,
+            )
+            for odd in range(2)
+        )
+        for at, rebuilt in enumerate((even + odd, even - odd)):
+            for a in range(lines):
+                out_ref[a, at] = advance(
+                    air_ref[a, at], rebuilt[:, a * width : (a + 1) * width], sea_ref[a, at], warmth_ref[...]
+                )
+
+    return pl.pallas_call(
+        body,
+        grid=(1,),
+        in_specs=[
+            pl.BlockSpec(memory_space=pltpu.SMEM),
+            pl.BlockSpec(table.shape, lambda i: (0, 0, 0)),
+            pl.BlockSpec((lines, 2, half, width), lambda i: (0, 0, 0, start // width)),
+            whole(sea),
+            pl.BlockSpec((GROUP, width), lambda i: (0, start // width)),
+        ]
+        + [pl.BlockSpec(parts[0].shape, lambda i: (0, 0, 0, 0))] * sections,
+        out_specs=pl.BlockSpec((lines, 2, half, width), lambda i: (0, 0, 0, start // width)),
+        out_shape=jax.ShapeDtypeStruct(air.shape, jnp.bfloat16),
+        scratch_shapes=[pltpu.VMEM((2, sections, plane, GROUP, lines * width), jnp.bfloat16)],
+        compiler_params=compiler_params(),
+        cost_estimate=pl.CostEstimate(flops=10**11, bytes_accessed=3 * 10**8, transcendentals=0),
+        name="synthesise_slim",
+    )(sec, table, air, sea, warmth, *parts)
+
+
+def synthesise_wide(coeffs, table, air, sea, warmth, begun):
+    groups, lines, rows, width = coeffs.shape
+    half = air.shape[2]
+
+    def body(table_ref, coeff_ref, air_ref, sea_ref, warmth_ref, begun_ref, out_ref):
+        for span in lane_spans(width):
+            even, odd = (
+                jnp.dot(
+                    table_ref[odd],
+                    coeff_ref[:, 0, odd * GROUP : (odd + 1) * GROUP, span].reshape(groups * GROUP, -1),
+                    preferred_element_type=jnp.float32,
+                )
+                for odd in range(2)
+            )
+            for at, rebuilt in enumerate((even + odd, even - odd)):
+                out_ref[0, at, :, span] = advance(
+                    air_ref[0, at, :, span], rebuilt, sea_ref[0, at], warmth_ref[:, span]
+                )
+
+    return pl.pallas_call(
+        body,
+        grid=(lines,),
+        in_specs=[
+            pl.BlockSpec(table.shape, lambda a: (0, 0, 0)),
+            pl.BlockSpec((groups, 1, rows, width), lambda a: (0, a, 0, 0)),
+            pl.BlockSpec((1, 2, half, width), lambda a: (a, 0, 0, 0)),
+            pl.BlockSpec((1, 2, GROUP, half), lambda a: (a, 0, 0, 0)),
+            pl.BlockSpec((GROUP, width), lambda a: (0, 0)),
+            pl.BlockSpec(memory_space=pl.ANY),
+        ],
+        out_specs=pl.BlockSpec((1, 2, half, width), lambda a: (a, 0, 0, 0)),
+        out_shape=jax.ShapeDtypeStruct(air.shape, jnp.bfloat16),
+        input_output_aliases={5: 0},
+        compiler_params=compiler_params(),
+        cost_estimate=cost(4 * lines * half * half * width, table, coeffs, coeffs, coeffs),
+        name="synthesise_wide",
+    )(table, coeffs, air, sea, warmth, begun)
+
+
+def gather_flux(air, projector):
+    flux_local = jnp.einsum(
+        "anc,cf->fan",
+        air,
+        projector,
+        preferred_element_type=jnp.float32,
+    ).astype(jnp.bfloat16)
+    return lax.all_gather(flux_local, "band", axis=1, tiled=True)
 
 
 def shards(
@@ -92,38 +417,76 @@
     slot_count = water_patch_fields.shape[0]
     mode_count = associated_polynomial_matrix.shape[0]
     lat_count = associated_polynomial_matrix.shape[1]
-    table = dft_table(meridian_number)
-    forward = jnp.asarray(np.ascontiguousarray(table.T))
-    backward = jnp.asarray((table.astype(np.float32) * (2.0 / meridian_number)).astype(jnp.bfloat16))
-
-    ends = np.cumsum((0,) + PARTS)
-    spans = [slice(int(a), int(b)) for a, b in zip(ends[:-1], ends[1:])]
-    collected = []
-    for span in spans:
+    wide = channel_count - SLIM
+    in_kernels = (
+        per_device == 2 * GROUP
+        and wide > 0
+        and wide % SLIM == 0
+        and sec_count & (sec_count - 1) == 0
+        and lat_count == device_count * parallel_lines
+    )
+    if in_kernels:
+        plane = band_count * core_count
+        sec_id = lax.axis_index("sec")
+        sec = sec_id.reshape(1).astype(jnp.int32)
+        forward, backward = map(jnp.asarray, folded_tables(meridian_number, device_count))
+        hops = [[(i, i ^ o) for i in range(sec_count)] for o in range(sec_count)]
+
+        twists = [[(i, i ^ p) for i in range(plane)] for p in range(plane)]
+        place = (lax.axis_index("band") * core_count + lax.axis_index("ch")).astype(jnp.int32)
+
+        def over_sections(blocks):
+            return [lax.ppermute(x, "sec", hops[o]) if o else x for o, x in enumerate(blocks)]
+
+        def over_plane(blocks):
+            return [lax.ppermute(x, ("band", "ch"), twists[p]) if p else x for p, x in enumerate(blocks)]
+
+        at_lat = jnp.arange(lat_count, dtype=jnp.int32)
+        sections_at = at_lat // parallel_lines % sec_count ^ sec_id
+        places_at = at_lat // (parallel_lines * sec_count) ^ place
+        order = (sections_at * plane + places_at) * parallel_lines + at_lat % parallel_lines
+        shuffle = (at_lat[:, None] == order[None, :]).astype(jnp.bfloat16)
+        shuffled = jnp.einsum(
+            "mlt,tu->mlu", associated_polynomial_matrix, shuffle, preferred_element_type=jnp.float32
+        ).astype(jnp.bfloat16)
+
+        slim = analyse_slim(air_field_lattice, forward, wide, sec, sec_count, device_count)
+        air_after, *slim = lax.optimization_barrier((air_field_lattice, *slim))
+        slim = over_sections(slim)
+        wide_coeffs = analyse_wide(air_after, forward, wide, device_count)
+        wide_coeffs, *slim = lax.optimization_barrier((wide_coeffs, *slim))
+        wide_coeffs = lax.all_to_all(wide_coeffs, AXES, split_axis=0, concat_axis=0, tiled=True)
+        slim = to_plane(slim, place.reshape(1))
+        air_after, *slim = lax.optimization_barrier((air_field_lattice, *slim))
+        slim = over_plane(slim)
+        gathered = gather_flux(air_after, boundary_exchange_projector)
+        gathered, *slim = lax.optimization_barrier((gathered, *slim))
+        slim = latitudinal_slim(slim, shuffled, harmonic_damping_factor, wide)
+        slim = from_plane(over_plane(slim), place.reshape(1))
+        wide_coeffs, *slim = lax.optimization_barrier((wide_coeffs, *slim))
+        slim = over_sections(slim)
+        wide_coeffs = latitudinal_wide(wide_coeffs, associated_polynomial_matrix, harmonic_damping_factor)
+        wide_coeffs = lax.all_to_all(wide_coeffs, AXES, split_axis=0, concat_axis=0, tiled=True)
+        water_patch_fields, gathered, *slim = lax.optimization_barrier((water_patch_fields, gathered, *slim))
+    else:
+        gathered = gather_flux(air_field_lattice, boundary_exchange_projector)
+        table = dft_table(meridian_number)
+        forward = jnp.asarray(np.ascontiguousarray(table.T))
+        backward = jnp.asarray((table.astype(np.float32) * (2.0 / meridian_number)).astype(jnp.bfloat16))
         fourier = jnp.einsum(
-            "qn,anc->aqc", forward, air_field_lattice[:, :, span], preferred_element_type=jnp.float32
+            "qn,anc->aqc", forward, air_field_lattice, preferred_element_type=jnp.float32
         ).astype(jnp.bfloat16)
-        collected.append(lax.all_to_all(fourier, AXES, split_axis=1, concat_axis=0, tiled=True))
-    returned = []
-    for span, coeffs in zip(spans, collected):
-        width = coeffs.shape[-1]
-        pairs = coeffs.reshape(lat_count, mode_count, 2, width)
+        collected = lax.all_to_all(fourier, AXES, split_axis=1, concat_axis=0, tiled=True)
+        pairs = collected.reshape(lat_count, mode_count, 2, channel_count)
         spectrum = jnp.einsum(
             "mlt,tmpc->mlpc", associated_polynomial_matrix, pairs, preferred_element_type=jnp.float32
         )
-        scaled = (spectrum * harmonic_damping_factor[None, :, None, span]).astype(jnp.bfloat16)
+        scaled = (spectrum * harmonic_damping_factor[None, :, None]).astype(jnp.bfloat16)
         damped = jnp.einsum(
             "mlt,mlpc->tmpc", associated_polynomial_matrix, scaled, preferred_element_type=jnp.float32
-        ).astype(jnp.bfloat16).reshape(lat_count, per_device, width)
-        returned.append(lax.all_to_all(damped, AXES, split_axis=0, concat_axis=1, tiled=True))
-
-    flux_local = jnp.einsum(
-        "anc,cf->fan",
-        air_field_lattice,
-        boundary_exchange_projector,
-        preferred_element_type=jnp.float32,
-    ).astype(jnp.bfloat16)
-    gathered = lax.all_gather(flux_local, "band", axis=1, tiled=True)
+        ).astype(jnp.bfloat16).reshape(lat_count, per_device, channel_count)
+        returned = lax.all_to_all(damped, AXES, split_axis=0, concat_axis=1, tiled=True)
+
     sec_id = lax.axis_index("sec")
     band_id = lax.axis_index("band")
     core_id = lax.axis_index("ch")
@@ -169,18 +532,23 @@
         "jk,krw->rjw", selector, sea_all, preferred_element_type=jnp.float32
     ).astype(jnp.bfloat16)
     water_skin_warmth = water_patches.reshape(parallel_lines, meridian_number)
-    pieces_out = []
-    for span, coeffs in zip(spans, returned):
-        rebuilt = jnp.einsum("nq,aqc->anc", backward, coeffs, preferred_element_type=jnp.float32)
-        pieces_out.append(
-            (
-                air_field_lattice[:, :, span].astype(jnp.float32)
-                + rebuilt
-                + water_skin_warmth.astype(jnp.float32)[:, :, None]
-                * warmth_response_factor[None, None, span]
-            ).astype(jnp.bfloat16)
-        )
-    return (jnp.concatenate(pieces_out, axis=-1), ocean_next)
+    if in_kernels:
+        halves = (parallel_lines, 2, meridian_number // 2, -1)
+        air = air_field_lattice.reshape(halves)
+        sea = water_skin_warmth.reshape(parallel_lines, 2, 1, meridian_number // 2)
+        sea = jnp.broadcast_to(sea, (parallel_lines, 2, GROUP, meridian_number // 2))
+        warmth = three_parts(warmth_response_factor)
+        begun = synthesise_slim(slim, backward, air, sea, warmth, wide, sec)
+        advanced = synthesise_wide(wide_coeffs, backward, air, sea, warmth, begun)
+        advanced = advanced.reshape(air_field_lattice.shape)
+    else:
+        rebuilt = jnp.einsum("nq,aqc->anc", backward, returned, preferred_element_type=jnp.float32)
+        advanced = (
+            air_field_lattice.astype(jnp.float32)
+            + rebuilt
+            + water_skin_warmth.astype(jnp.float32)[:, :, None] * warmth_response_factor[None, None]
+        ).astype(jnp.bfloat16)
+    return (advanced, ocean_next)
 
 
 def solution(mesh):

time: 184 us -> 166 us (0.902)
  Pallas kernels: 0 us -> 28.4 us
  local copies, waits for them, and re-layouts: 33.9 us -> 7.78 us
  matrix products: 44.7 us -> 23 us
  starting transfers between devices: 19.2 us -> 32.5 us
  waiting for transfers between devices: 57.4 us -> 51.1 us
  blocking collectives: 24.6 us -> 21.3 us
  other arithmetic: 2.35 us -> 0.5 us
    all_to_all x4 -> x2, waiting for transfers between devices: 57.4 us -> 28.1 us  [shards(): lax.all_to_all(wide_coeffs, AXES, split_axis=0, concat_axis=0, tiled=True)]
    pallas_call x0 -> x8, Pallas kernels: none -> 28.4 us  [the longest x1 5.81 us: synthesise_wide(): pl.pallas_call(body, grid=(lines,), in_specs=[pl.BlockSpec(table.shape, l...]
    ppermute x0 -> x20, starting transfers between devices: none -> 23.3 us  [the longest x14 13.3 us: over_plane(): lax.ppermute(x, ('band', 'ch'), twists[p])]
    ppermute x0 -> x20, waiting for transfers between devices: none -> 23 us  [the longest x14 17.1 us: over_plane(): lax.ppermute(x, ('band', 'ch'), twists[p])]
    dot_general x7 -> x2, matrix products: 22.7 us -> 1.89 us  [the longest x1 0.99 us: shards(): jnp.einsum('mlt,tu->mlu', associated_polynomial_matrix, shuffle, preferre...]
    all_to_all x4 -> x2, starting transfers between devices: 19.2 us -> 9.21 us  [shards(): lax.all_to_all(wide_coeffs, AXES, split_axis=0, concat_axis=0, tiled=True)]
    reshape x5 -> x0, local copies, waits for them, and re-layouts: 8.96 us -> none  [the longest x2 5.66 us: shards(): damped = jnp.einsum('mlt,mlpc->tmpc', associated_polynomial_matrix, scale...]
    slice x8 -> x0, local copies, waits for them, and re-layouts: 8.77 us -> none  [the longest x1 8.6 us: ocean_update(): state[:, :, shift_row:shift_row + parallel_lines, shift_col:shift_col + t...]
  transfers between devices with their start and end apart: 4 -> 22, of which waited for: 4 -> 6; matrix products, arithmetic and copies ran while one was open for 37% -> 17% of each run, Pallas kernels for 0% -> 12%
where the time goes in v1:
time: 166 us
  waiting for transfers between devices  51.1 us (31%)
  starting transfers between devices  32.5 us (20%)
  Pallas kernels  28.4 us (17%)
  matrix products  23 us (14%)
  blocking collectives  21.3 us (13%)
  local copies, waits for them, and re-layouts  7.78 us (5%)
    all_to_all x2, waiting for transfers between devices, shards(): lax.all_to_all(wide_coeffs, AXES, split_axis=0, concat_axis=0, tiled=True)  28.1 us
    ppermute x14, waiting for transfers between devices, over_plane(): lax.ppermute(x, ('band', 'ch'), twists[p])  17.1 us
    dot_general x9, matrix products, ocean_update(): jnp.einsum('io,sirw->sorw', kernel_coefficients[shift_row, shift_col], wi...  13.8 us
    ppermute x14, starting transfers between devices, over_plane(): lax.ppermute(x, ('band', 'ch'), twists[p])  13.3 us
    all_gather x1, blocking collectives, gather_flux(): return lax.all_gather(flux_local, 'band', axis=1, tiled=True)  13 us
    ppermute x6, starting transfers between devices, over_sections(): lax.ppermute(x, 'sec', hops[o])  10 us
    all_to_all x2, starting transfers between devices, shards(): lax.all_to_all(wide_coeffs, AXES, split_axis=0, concat_axis=0, tiled=True)  9.21 us
    all_gather x1, blocking collectives, shards(): sea_all = lax.all_gather(sea_slots, 'band', axis=0, tiled=True)  8.32 us
  transfers between devices with their start and end apart: 22, of which 6 were waited for; matrix products, arithmetic and copies ran while one was open for 17% of the time, Pallas kernels for 12%

profile of v1, /device:TPU:0, one launch (start us, length us, event | category | flops | bytes accessed | tf_op | source)
XLA Modules:
  0.0 165.7 jit_solution(311416170397968922)
XLA Ops:
  0.7 2.8 %analyse_slim.1 = (bf16[2,8,32,128]{3,2,1,0:T(8,128)(2,1)}, bf16[2,8,32,128]{3,2,1,0:T(8,128)(2,1)}, bf16[2,8,32,128]{3,2,1,0:T(8,128)(2,1)}, bf16[2,8,32,128]{3,2,1,0:T(8,128)(2,1)}) custom-call(s32[1]{0:T(128)} %bitcast.sec_ref, bf16[2,512,512]{2,1,0:T(8,128)(2,1)} %constant.153.clone.table_ref, bf16[2,1024,768]{2,1,0:T(8,128)(2,1)} %air_ref.2), custom_call_target="tpu_custom_call" | custom-call | flops 268435456 | bytes 2097152 | tf_op jit(solution)/shard_map/analyse_slim/pallas_call | solution.py:149
  3.4 3.0 %collective-permute-start = (bf16[2,8,32,128]{3,2,1,0:T(8,128)(2,1)}, bf16[2,8,32,128]{3,2,1,0:T(8,128)(2,1)}, u32[]{:S(2)}, u32[]{:S(2)}) collective-permute-start(bf16[2,8,32,128]{3,2,1,0:T(8,128)(2,1)} %get-tuple-element.71), channel_id=1, source_target_pairs={{0,8},{8,0},{16,24},{24,16},{1,9},{9,1},{17,25},{25,17},{2,10},{10... | collective-permute-start | bytes 393224 | tf_op jit(solution)/shard_map/ppermute | solution.py:439
  6.5 2.6 %collective-permute-start.1 = (bf16[2,8,32,128]{3,2,1,0:T(8,128)(2,1)}, bf16[2,8,32,128]{3,2,1,0:T(8,128)(2,1)}, u32[]{:S(2)}, u32[]{:S(2)}) collective-permute-start(bf16[2,8,32,128]{3,2,1,0:T(8,128)(2,1)} %get-tuple-element.72), channel_id=1, source_target_pairs={{0,16},{8,24},{16,0},{24,8},{1,17},{9,25},{17,1},{25,9},{2,18},{10... | collective-permute-start | bytes 393224 | tf_op jit(solution)/shard_map/ppermute | solution.py:439
  9.1 4.7 %analyse_wide.1 = bf16[32,2,32,640]{3,2,1,0:T(8,128)(2,1)} custom-call(bf16[2,512,512]{2,1,0:T(8,128)(2,1)} %constant.153.clone.table_ref, bf16[2,1024,768]{2,1,0:T(8,128)(2,1)} %air_ref.2), custom_call_target="tpu_custom_call" | custom-call | flops 1342177280 | bytes 6815744 | tf_op jit(solution)/shard_map/analyse_wide/pallas_call | solution.py:117
  13.8 5.9 %collective-permute-done.1.refs_2_ = bf16[2,8,32,128]{3,2,1,0:T(8,128)(2,1)} collective-permute-done((bf16[2,8,32,128]{3,2,1,0:T(8,128)(2,1)}, bf16[2,8,32,128]{3,2,1,0:T(8,128)(2,1)}, u32[]{:S(2)}, u32[]{:S(2)}) %collective-permute-start.1) | collective-permute-done | bytes 131104 | tf_op jit(solution)/shard_map/ppermute | solution.py:439
  19.7 5.3 %all-to-all-start = ((bf16[32,2,32,640]{3,2,1,0:T(8,128)(2,1)}), bf16[32,2,32,640]{3,2,1,0:T(8,128)(2,1)}, u32[]{:S(2)}, u32[]{:S(2)}) async-start(bf16[32,2,32,640]{3,2,1,0:T(8,128)(2,1)} %analyse_wide.1), calls=%async_computation | async-start | bytes 5242880 | tf_op jit(solution)/shard_map/all_to_all | solution.py:458
  25.1 0.1 copy.80
  25.2 0.1 eq.64
  25.3 0.2 reduce_window_sum.11
  25.6 1.0 fusion.10.matrix_ref
  26.6 1.9 %to_plane.1 = (bf16[4,2,32,128]{3,2,1,0:T(8,128)(2,1)}, bf16[4,2,32,128]{3,2,1,0:T(8,128)(2,1)}, bf16[4,2,32,128]{3,2,1,0:T(8,128)(2,1)}, bf16[4,2,32,128]{3,2,1...) custom-call(s32[1]{0:T(128)} %bitcast.1.place_ref, ...), custom_call_target="tpu_custom_call" | custom-call | bytes 1048576 | tf_op jit(solution)/shard_map/to_plane/pallas_call | solution.py:216
  28.5 0.2 collective-permute-start.3
  28.7 1.7 %collective-permute-start.4 = (bf16[4,2,32,128]{3,2,1,0:T(8,128)(2,1)}, bf16[4,2,32,128]{3,2,1,0:T(8,128)(2,1)S(1)}, u32[]{:S(2)}, u32[]{:S(2)}) collective-permute-start(bf16[4,2,32,128]{3,2,1,0:T(8,128)(2,1)} %get-tuple-element.90), channel_id=1, source_target_pairs={{0,2},{1,3},{2,0},{3,1},{4,6},{5,7},{6,4},{7,5},{8,10},{9,11},{10,... | collective-permute-start | bytes 196616 | tf_op jit(solution)/shard_map/ppermute | solution.py:442
  30.5 1.7 %collective-permute-start.6 = (bf16[4,2,32,128]{3,2,1,0:T(8,128)(2,1)}, bf16[4,2,32,128]{3,2,1,0:T(8,128)(2,1)S(1)}, u32[]{:S(2)}, u32[]{:S(2)}) collective-permute-start(bf16[4,2,32,128]{3,2,1,0:T(8,128)(2,1)} %get-tuple-element.92), channel_id=1, source_target_pairs={{0,4},{1,5},{2,6},{3,7},{4,0},{5,1},{6,2},{7,3},{8,12},{9,13},{10,... | collective-permute-start | bytes 196616 | tf_op jit(solution)/shard_map/ppermute | solution.py:442
  32.1 0.1 collective-permute-start.7
  32.3 2.6 %collective-permute-start.8 = (bf16[4,2,32,128]{3,2,1,0:T(8,128)(2,1)}, bf16[4,2,32,128]{3,2,1,0:T(8,128)(2,1)S(1)}, u32[]{:S(2)}, u32[]{:S(2)}) collective-permute-start(bf16[4,2,32,128]{3,2,1,0:T(8,128)(2,1)} %get-tuple-element.94), channel_id=1, source_target_pairs={{0,6},{1,7},{2,4},{3,5},{4,2},{5,3},{6,0},{7,1},{8,14},{9,15},{10,... | collective-permute-start | bytes 196616 | tf_op jit(solution)/shard_map/ppermute | solution.py:442
  34.8 11.1 %collective-permute-done.4.refs_2_ = bf16[4,2,32,128]{3,2,1,0:T(8,128)(2,1)S(1)} collective-permute-done((bf16[4,2,32,128]{3,2,1,0:T(8,128)(2,1)}, bf16[4,2,32,128]{3,2,1,0:T(8,128)(2,1)S(1)}, u32[]{:S(2)}, u32[]{:S(2)}) %collective-permute-start.4) | collective-permute-done | bytes 65568 | tf_op jit(solution)/shard_map/ppermute | solution.py:442
  46.0 0.7 collective-permute-start.9
  46.7 0.9 fusion.13
  47.6 13.0 %all_gather.6 = bf16[8,8,1024]{2,0,1:T(8,128)(2,1)S(1)} all-gather(bf16[8,2,1024]{2,0,1:T(8,128)(2,1)S(1)} %fusion.13), channel_id=1, replica_groups=mesh['sec'=4,'band'=4,'ch'=2] {'band'}, dimensions={1}, use_global_device_ids=true | all-gather | bytes 163840 | tf_op jit(solution)/shard_map/all_gather | solution.py:391
  60.7 0.5 copy-done.14
  61.3 0.6 copy-done.18
  61.9 2.6 %latitudinal_slim.1 = (bf16[4,2,32,128]{3,2,1,0:T(8,128)(2,1)}, bf16[4,2,32,128]{3,2,1,0:T(8,128)(2,1)}, bf16[4,2,32,128]{3,2,1,0:T(8,128)(2,1)}, bf16[4,2,32,12...) custom-call(bf16[16,64,64]{2,1,0:T(8,128)(2,1)} %fusion.10.matrix_re, ...), custom_call_target="tpu_custom_call" | custom-call | flops 67108864 | bytes 1179648 | tf_op jit(solution)/shard_map/latitudinal_slim/pallas_call | solution.py:268
  64.5 1.1 collective-permute-start.11
  65.6 0.1 fusion.67
  65.7 0.8 collective-permute-start.12
  66.4 1.4 collective-permute-start.13
  67.9 0.3 collective-permute-start.14
  68.1 1.7 %collective-permute-start.15 = (bf16[4,2,32,128]{3,2,1,0:T(8,128)(2,1)}, bf16[4,2,32,128]{3,2,1,0:T(8,128)(2,1)S(1)}, u32[]{:S(2)}, u32[]{:S(2)}) collective-permute-start(bf16[4,2,32,128]{3,2,1,0:T(8,128)(2,1)} %get-tuple-element.110), channel_id=1, source_target_pairs={{0,6},{1,7},{2,4},{3,5},{4,2},{5,3},{6,0},{7,1},{8,14},{9,15},{10,... | collective-permute-start | bytes 196616 | tf_op jit(solution)/shard_map/ppermute | solution.py:442
  69.8 1.0 collective-permute-start.16
  70.9 1.2 stack.27.warmth_ref
  72.2 3.4 %collective-permute-done.13.refs_4_ = bf16[4,2,32,128]{3,2,1,0:T(8,128)(2,1)S(1)} collective-permute-done((bf16[4,2,32,128]{3,2,1,0:T(8,128)(2,1)}, bf16[4,2,32,128]{3,2,1,0:T(8,128)(2,1)S(1)}, u32[]{:S(2)}, u32[]{:S(2)}) %collective-permute-start.13) | collective-permute-done | bytes 65568 | tf_op jit(solution)/shard_map/ppermute | solution.py:442
  75.6 2.5 %collective-permute-done.14.refs_5_ = bf16[4,2,32,128]{3,2,1,0:T(8,128)(2,1)S(1)} collective-permute-done((bf16[4,2,32,128]{3,2,1,0:T(8,128)(2,1)}, bf16[4,2,32,128]{3,2,1,0:T(8,128)(2,1)S(1)}, u32[]{:S(2)}, u32[]{:S(2)}) %collective-permute-start.14) | collective-permute-done | bytes 65568 | tf_op jit(solution)/shard_map/ppermute | solution.py:442
  78.2 0.5 copy-done.9
  78.8 1.9 %from_plane.1 = (bf16[2,8,32,128]{3,2,1,0:T(8,128)(2,1)}, bf16[2,8,32,128]{3,2,1,0:T(8,128)(2,1)}, bf16[2,8,32,128]{3,2,1,0:T(8,128)(2,1)}, bf16[2,8,32,128]{3,2,1,0:T(8,128)(2,1)}) custom-call(s32[1]{0:T(128)} %bitcast.1.place_ref, bf16[4,2,32,128]{3,2,1,0:T(8,128)(2,1)} %get-tuple-element.104.refs_0_, bf16[4,2,32,128]{3,2,1,0:T(8,128)(2,1)} %copy-done.5, ...), custom_call_target="tpu_custom_call" | custom-call | bytes 1048576 | tf_op jit(solution)/shard_map/from_plane/pallas_call | solution.py:239
  80.7 5.0 %all-to-all-done.x_ref = bf16[32,2,32,640]{3,2,1,0:T(8,128)(2,1)} async-done(((bf16[32,2,32,640]{3,2,1,0:T(8,128)(2,1)}), bf16[32,2,32,640]{3,2,1,0:T(8,128)(2,1)}, u32[]{:S(2)}, u32[]{:S(2)}) %all-to-all-start) | async-done | bytes 2621472 | tf_op jit(solution)/shard_map/all_to_all | solution.py:458
  85.7 2.1 %collective-permute-start.18 = (bf16[2,8,32,128]{3,2,1,0:T(8,128)(2,1)}, bf16[2,8,32,128]{3,2,1,0:T(8,128)(2,1)S(1)}, u32[]{:S(2)}, u32[]{:S(2)}) collective-permute-start(bf16[2,8,32,128]{3,2,1,0:T(8,128)(2,1)} %get-tuple-element.120), channel_id=1, source_target_pairs={{0,16},{8,24},{16,0},{24,8},{1,17},{9,25},{17,1},{25,9},{2,18},{10... | collective-permute-start | bytes 393224 | tf_op jit(solution)/shard_map/ppermute | solution.py:439
  87.8 2.3 %collective-permute-start.19 = (bf16[2,8,32,128]{3,2,1,0:T(8,128)(2,1)}, bf16[2,8,32,128]{3,2,1,0:T(8,128)(2,1)}, u32[]{:S(2)}, u32[]{:S(2)}) collective-permute-start(bf16[2,8,32,128]{3,2,1,0:T(8,128)(2,1)} %get-tuple-element.121), channel_id=1, source_target_pairs={{0,24},{8,16},{16,8},{24,0},{1,25},{9,17},{17,9},{25,1},{2,26},{10... | collective-permute-start | bytes 393224 | tf_op jit(solution)/shard_map/ppermute | solution.py:439
  90.1 5.7 %latitudinal_wide.1 = bf16[32,2,32,640]{3,2,1,0:T(8,128)(2,1)} custom-call(bf16[32,2,32,640]{3,2,1,0:T(8,128)(2,1)} %all-to-all-done.x_ref, bf16[16,64,64]{2,1,0:T(8,128)(2,1)} %matrix_ref.1, f32[64,768]{1,0:T(8,128)} %damping_ref.3), custom_call_target="tpu_custom_call" | custom-call | flops 335544320 | bytes 5373952 | tf_op jit(solution)/shard_map/latitudinal_wide/pallas_call | solution.py:189
  95.9 3.9 %all-to-all-start.1 = ((bf16[32,2,32,640]{3,2,1,0:T(8,128)(2,1)}), bf16[32,2,32,640]{3,2,1,0:T(8,128)(2,1)}, u32[]{:S(2)}, u32[]{:S(2)}) async-start(bf16[32,2,32,640]{3,2,1,0:T(8,128)(2,1)} %latitudinal_wide.1), calls=%async_computation.1 | async-start | bytes 5242880 | tf_op jit(solution)/shard_map/all_to_all | solution.py:469
  99.8 0.6 copy-done.26
  100.4 0.6 copy-done.27
  101.1 0.2 copy.79
  101.3 1.5 fusion.15
  102.8 1.5 fusion.17
  104.4 1.6 fusion.19
  106.0 1.5 fusion.21
  107.5 1.5 fusion.37
  109.0 1.6 fusion.23
  110.6 1.5 fusion.25
  112.1 1.5 fusion.27
  113.6 1.5 fusion.29
  115.1 0.3 convert_reduce_fusion
  115.5 0.1 copy.92
  115.5 0.1 multiply_reduce_fusion
  115.7 6.8 %fusion.9 = bf16[6,128,2,256]{1,3,2,0:T(8,128)(2,1)S(1)} fusion(f32[6,2,256,128]{3,2,1,0:T(8,128)} %fusion.15, f32[6,2,256,128]{3,2,1,0:T(8,128)} %fusion.17, f32[6,2,256,128]{3,2,1,0:T(8,128)} %fusion.19, f32[6,2,256,128]{3,2,1,0:T(8,128)} %fusion.21, f32[6,2,256,128]{3,2,1,0:T(8,128)} %fusion.37, f32[6,2,256,128]{3,2,1,0:T(8,128)} %fusion.23, ...), kind=kOutput, calls=%fused_computation.11 | convolution fusion | flops 116391936 | bytes 15828480 | tf_op jit(solution)/shard_map/io,sirw->sorw/dot_general | solution.py:74
  122.5 1.8 %copy.98 = bf16[6,128,2,256]{3,2,1,0:T(2,128)(2,1)} copy(bf16[6,128,2,256]{1,3,2,0:T(8,128)(2,1)S(1)} %fusion.9) | data formatting | bytes 1572864
  124.3 0.3 copy.96
  124.6 8.3 %all-gather = bf16[24,1,2,256]{3,2,1,0:T(2,128)(2,1)S(1)} all-gather(bf16[6,1,2,256]{3,2,1,0:T(2,128)(2,1)S(1)} %copy.96), channel_id=2, replica_groups=mesh['sec'=4,'band'=4,'ch'=2] {'band'}, dimensions={0}, use_global_device_ids=true | all-gather | bytes 30720 | tf_op jit(solution)/shard_map/all_gather | solution.py:523
  132.9 0.2 fusion.14
  133.1 0.6 broadcast_in_dim.9.sea_ref
  133.7 3.0 %synthesise_slim.1.begun_ref = bf16[2,2,512,768]{3,2,1,0:T(8,128)(2,1)} custom-call(s32[1]{0:T(128)} %bitcast.sec_ref, bf16[2,512,512]{2,1,0:T(8,128)(2,1)} %constant.154.clone.table_ref, bf16[2,2,512,768]{3,2,1,0:T(8,128)(2,1)} %bitcast.126, bf16[2,2,16,512]{3,2,1,0:T(8,128)(2,1)} %broadcast_in_dim.9.sea_ref, bf16[16,768]{1,0:T(8,128)(2,1)} %stack.27.warmth_ref, ...), custom_call_target="tpu_custom_call" | custom-call | flops 99999997952 | bytes 300000000 | tf_op jit(solution)/shard_map/synthesise_slim/pallas_call | solution.py:325
  136.7 23.1 %all-to-all-done.1.coeff_ref = bf16[32,2,32,640]{3,2,1,0:T(8,128)(2,1)} async-done(((bf16[32,2,32,640]{3,2,1,0:T(8,128)(2,1)}), bf16[32,2,32,640]{3,2,1,0:T(8,128)(2,1)}, u32[]{:S(2)}, u32[]{:S(2)}) %all-to-all-start.1) | async-done | bytes 2621472 | tf_op jit(solution)/shard_map/all_to_all | solution.py:469
  159.9 5.8 %synthesise_wide.1 = bf16[2,2,512,768]{3,2,1,0:T(8,128)(2,1)} custom-call(bf16[2,512,512]{2,1,0:T(8,128)(2,1)} %constant.154.clone.table_ref, bf16[32,2,32,640]{3,2,1,0:T(8,128)(2,1)} %all-to-all-done.1.coeff_ref, bf16[2,2,512,768]{3,2,1,0:T(8,128)(2,1)} %bitcast.127, ...), custom_call_target="tpu_custom_call", output_to_operand_aliasing={{}: (5, {})} | custom-call | flops 1342177280 | bytes 8912896 | tf_op jit(solution)/shard_map/synthesise_wide/pallas_call | solution.py:364
  (92 shorter events, 0.6 us)
Async XLA Ops:
  0.6 115.0 %copy-start = (bf16[128,128]{1,0:T(8,128)(2,1)S(1)}, bf16[128,128]{1,0:T(8,128)(2,1)}, u32[]{:S(2)}) copy-start(bf16[128,128]{1,0:T(8,128)(2,1)} %param.26) | copy-start | bytes 98308
  3.4 10.4 %collective-permute-start = (bf16[2,8,32,128]{3,2,1,0:T(8,128)(2,1)}, bf16[2,8,32,128]{3,2,1,0:T(8,128)(2,1)}, u32[]{:S(2)}, u32[]{:S(2)}) collective-permute-start(bf16[2,8,32,128]{3,2,1,0:T(8,128)(2,1)} %get-tuple-element.71), channel_id=1, source_target_pairs={{0,8},{8,0},{16,24},{24,16},{1,9},{9,1},{17,25},{25,17},{2,10},{10... | collective-permute-start | bytes 393224 | tf_op jit(solution)/shard_map/ppermute | solution.py:439
  6.5 13.2 %collective-permute-start.1 = (bf16[2,8,32,128]{3,2,1,0:T(8,128)(2,1)}, bf16[2,8,32,128]{3,2,1,0:T(8,128)(2,1)}, u32[]{:S(2)}, u32[]{:S(2)}) collective-permute-start(bf16[2,8,32,128]{3,2,1,0:T(8,128)(2,1)} %get-tuple-element.72), channel_id=1, source_target_pairs={{0,16},{8,24},{16,0},{24,8},{1,17},{9,25},{17,1},{25,9},{2,18},{10... | collective-permute-start | bytes 393224 | tf_op jit(solution)/shard_map/ppermute | solution.py:439
  9.1 10.7 %collective-permute-start.2 = (bf16[2,8,32,128]{3,2,1,0:T(8,128)(2,1)}, bf16[2,8,32,128]{3,2,1,0:T(8,128)(2,1)}, u32[]{:S(2)}, u32[]{:S(2)}) collective-permute-start(bf16[2,8,32,128]{3,2,1,0:T(8,128)(2,1)} %get-tuple-element.73), channel_id=1, source_target_pairs={{0,24},{8,16},{16,8},{24,0},{1,25},{9,17},{17,9},{25,1},{2,26},{10... | collective-permute-start | bytes 393224 | tf_op jit(solution)/shard_map/ppermute | solution.py:439
  13.8 11.3 %copy-start.24 = (s32[32,4]{0,1:T(4,128)S(1)}, s32[32,4]{0,1:T(4,128)}, u32[]{:S(2)}) copy-start(s32[32,4]{0,1:T(4,128)} %param.27) | copy-start | bytes 1540
  13.8 11.8 %copy-start.22 = (f32[768]{0:T(1024)S(1)}, f32[768]{0:T(1024)}, u32[]{:S(2)}) copy-start(f32[768]{0:T(1024)} %param.20) | copy-start | bytes 9220
  13.8 11.8 %copy-start.20 = (s32[6,2,256]{2,1,0:T(2,128)S(1)}, s32[6,2,256]{2,1,0:T(2,128)}, u32[]{:S(2)}) copy-start(s32[6,2,256]{2,1,0:T(2,128)} %param.28) | copy-start | bytes 36868
  13.8 11.8 %copy-start.3 = (bf16[16,64,64]{2,1,0:T(8,128)(2,1)S(1)}, bf16[16,64,64]{2,1,0:T(8,128)(2,1)}, u32[]{:S(2)}) copy-start(bf16[16,64,64]{2,1,0:T(8,128)(2,1)} %matrix_ref.1) | copy-start | bytes 393220
  13.8 32.9 %copy-start.1 = (bf16[2,1024,768]{2,1,0:T(8,128)(2,1)S(1)}, bf16[2,1024,768]{2,1,0:T(8,128)(2,1)}, u32[]{:S(2)}) copy-start(bf16[2,1024,768]{2,1,0:T(8,128)(2,1)} %air_ref.2) | copy-start | bytes 9437188
  13.8 32.9 %copy-start.19 = (bf16[768,8]{0,1:T(8,128)(2,1)S(1)}, bf16[768,8]{0,1:T(8,128)(2,1)}, u32[]{:S(2)}) copy-start(bf16[768,8]{0,1:T(8,128)(2,1)} %param.19) | copy-start | bytes 36868
  19.7 66.0 %all-to-all-start = ((bf16[32,2,32,640]{3,2,1,0:T(8,128)(2,1)}), bf16[32,2,32,640]{3,2,1,0:T(8,128)(2,1)}, u32[]{:S(2)}, u32[]{:S(2)}) async-start(bf16[32,2,32,640]{3,2,1,0:T(8,128)(2,1)} %analyse_wide.1), calls=%async_computation | async-start | bytes 5242880 | tf_op jit(solution)/shard_map/all_to_all | solution.py:458
  28.5 3.8 %collective-permute-start.3 = (bf16[4,2,32,128]{3,2,1,0:T(8,128)(2,1)}, bf16[4,2,32,128]{3,2,1,0:T(8,128)(2,1)S(1)}, u32[]{:S(2)}, u32[]{:S(2)}) collective-permute-start(bf16[4,2,32,128]{3,2,1,0:T(8,128)(2,1)} %get-tuple-element.89), channel_id=1, source_target_pairs={{0,1},{1,0},{2,3},{3,2},{4,5},{5,4},{6,7},{7,6},{8,9},{9,8},{10,11... | collective-permute-start | bytes 196616 | tf_op jit(solution)/shard_map/ppermute | solution.py:442
  28.7 17.3 %collective-permute-start.4 = (bf16[4,2,32,128]{3,2,1,0:T(8,128)(2,1)}, bf16[4,2,32,128]{3,2,1,0:T(8,128)(2,1)S(1)}, u32[]{:S(2)}, u32[]{:S(2)}) collective-permute-start(bf16[4,2,32,128]{3,2,1,0:T(8,128)(2,1)} %get-tuple-element.90), channel_id=1, source_target_pairs={{0,2},{1,3},{2,0},{3,1},{4,6},{5,7},{6,4},{7,5},{8,10},{9,11},{10,... | collective-permute-start | bytes 196616 | tf_op jit(solution)/shard_map/ppermute | solution.py:442
  30.4 40.5 %copy-start.28 = (s32[6]{0:T(128)S(1)}, s32[6]{0:T(128)}, u32[]{:S(2)}) copy-start(s32[6]{0:T(128)} %param.29) | copy-start | bytes 76
  30.4 30.2 %collective-permute-start.5 = (bf16[4,2,32,128]{3,2,1,0:T(8,128)(2,1)}, bf16[4,2,32,128]{3,2,1,0:T(8,128)(2,1)S(1)}, u32[]{:S(2)}, u32[]{:S(2)}) collective-permute-start(bf16[4,2,32,128]{3,2,1,0:T(8,128)(2,1)} %get-tuple-element.91), channel_id=1, source_target_pairs={{0,3},{1,2},{2,1},{3,0},{4,7},{5,6},{6,5},{7,4},{8,11},{9,10},{10,... | collective-permute-start | bytes 196616 | tf_op jit(solution)/shard_map/ppermute | solution.py:442
  30.5 30.1 %collective-permute-start.6 = (bf16[4,2,32,128]{3,2,1,0:T(8,128)(2,1)}, bf16[4,2,32,128]{3,2,1,0:T(8,128)(2,1)S(1)}, u32[]{:S(2)}, u32[]{:S(2)}) collective-permute-start(bf16[4,2,32,128]{3,2,1,0:T(8,128)(2,1)} %get-tuple-element.92), channel_id=1, source_target_pairs={{0,4},{1,5},{2,6},{3,7},{4,0},{5,1},{6,2},{7,3},{8,12},{9,13},{10,... | collective-permute-start | bytes 196616 | tf_op jit(solution)/shard_map/ppermute | solution.py:442
  32.1 28.5 %collective-permute-start.7 = (bf16[4,2,32,128]{3,2,1,0:T(8,128)(2,1)}, bf16[4,2,32,128]{3,2,1,0:T(8,128)(2,1)S(1)}, u32[]{:S(2)}, u32[]{:S(2)}) collective-permute-start(bf16[4,2,32,128]{3,2,1,0:T(8,128)(2,1)} %get-tuple-element.93), channel_id=1, source_target_pairs={{0,5},{1,4},{2,7},{3,6},{4,1},{5,0},{6,3},{7,2},{8,13},{9,12},{10,... | collective-permute-start | bytes 196616 | tf_op jit(solution)/shard_map/ppermute | solution.py:442
  32.3 15.3 %copy-start.12 = (bf16[4,2,32,128]{3,2,1,0:T(8,128)(2,1)}, bf16[4,2,32,128]{3,2,1,0:T(8,128)(2,1)S(1)}, u32[]{:S(2)}) copy-start(bf16[4,2,32,128]{3,2,1,0:T(8,128)(2,1)S(1)} %collective-permute-done.3.refs_1_) | copy-start | bytes 196612
  32.3 28.4 %collective-permute-start.8 = (bf16[4,2,32,128]{3,2,1,0:T(8,128)(2,1)}, bf16[4,2,32,128]{3,2,1,0:T(8,128)(2,1)S(1)}, u32[]{:S(2)}, u32[]{:S(2)}) collective-permute-start(bf16[4,2,32,128]{3,2,1,0:T(8,128)(2,1)} %get-tuple-element.94), channel_id=1, source_target_pairs={{0,6},{1,7},{2,4},{3,5},{4,2},{5,3},{6,0},{7,1},{8,14},{9,15},{10,... | collective-permute-start | bytes 196616 | tf_op jit(solution)/shard_map/ppermute | solution.py:442
  46.0 1.6 copy-start.13
  46.0 14.7 %collective-permute-start.9 = (bf16[4,2,32,128]{3,2,1,0:T(8,128)(2,1)}, bf16[4,2,32,128]{3,2,1,0:T(8,128)(2,1)S(1)}, u32[]{:S(2)}, u32[]{:S(2)}) collective-permute-start(bf16[4,2,32,128]{3,2,1,0:T(8,128)(2,1)} %get-tuple-element.95), channel_id=1, source_target_pairs={{0,7},{1,6},{2,5},{3,4},{4,3},{5,2},{6,1},{7,0},{8,15},{9,14},{10,... | collective-permute-start | bytes 196616 | tf_op jit(solution)/shard_map/ppermute | solution.py:442
  60.6 0.6 copy-start.14
  60.6 0.6 copy-start.15
  60.6 0.6 copy-start.16
  60.6 0.7 copy-start.17
  61.3 0.6 copy-start.18
  64.5 3.7 %collective-permute-start.10 = (bf16[4,2,32,128]{3,2,1,0:T(8,128)(2,1)}, bf16[4,2,32,128]{3,2,1,0:T(8,128)(2,1)S(1)}, u32[]{:S(2)}, u32[]{:S(2)}) collective-permute-start(bf16[4,2,32,128]{3,2,1,0:T(8,128)(2,1)} %get-tuple-element.105), channel_id=1, source_target_pairs={{0,1},{1,0},{2,3},{3,2},{4,5},{5,4},{6,7},{7,6},{8,9},{9,8},{10,11... | collective-permute-start | bytes 196616 | tf_op jit(solution)/shard_map/ppermute | solution.py:442
  64.5 5.3 %collective-permute-start.11 = (bf16[4,2,32,128]{3,2,1,0:T(8,128)(2,1)}, bf16[4,2,32,128]{3,2,1,0:T(8,128)(2,1)S(1)}, u32[]{:S(2)}, u32[]{:S(2)}) collective-permute-start(bf16[4,2,32,128]{3,2,1,0:T(8,128)(2,1)} %get-tuple-element.106), channel_id=1, source_target_pairs={{0,2},{1,3},{2,0},{3,1},{4,6},{5,7},{6,4},{7,5},{8,10},{9,11},{10,... | collective-permute-start | bytes 196616 | tf_op jit(solution)/shard_map/ppermute | solution.py:442
  65.7 6.5 %collective-permute-start.12 = (bf16[4,2,32,128]{3,2,1,0:T(8,128)(2,1)}, bf16[4,2,32,128]{3,2,1,0:T(8,128)(2,1)S(1)}, u32[]{:S(2)}, u32[]{:S(2)}) collective-permute-start(bf16[4,2,32,128]{3,2,1,0:T(8,128)(2,1)} %get-tuple-element.107), channel_id=1, source_target_pairs={{0,3},{1,2},{2,1},{3,0},{4,7},{5,6},{6,5},{7,4},{8,11},{9,10},{10,... | collective-permute-start | bytes 196616 | tf_op jit(solution)/shard_map/ppermute | solution.py:442
  66.4 9.1 %collective-permute-start.13 = (bf16[4,2,32,128]{3,2,1,0:T(8,128)(2,1)}, bf16[4,2,32,128]{3,2,1,0:T(8,128)(2,1)S(1)}, u32[]{:S(2)}, u32[]{:S(2)}) collective-permute-start(bf16[4,2,32,128]{3,2,1,0:T(8,128)(2,1)} %get-tuple-element.108), channel_id=1, source_target_pairs={{0,4},{1,5},{2,6},{3,7},{4,0},{5,1},{6,2},{7,3},{8,12},{9,13},{10,... | collective-permute-start | bytes 196616 | tf_op jit(solution)/shard_map/ppermute | solution.py:442
  67.9 10.2 %collective-permute-start.14 = (bf16[4,2,32,128]{3,2,1,0:T(8,128)(2,1)}, bf16[4,2,32,128]{3,2,1,0:T(8,128)(2,1)S(1)}, u32[]{:S(2)}, u32[]{:S(2)}) collective-permute-start(bf16[4,2,32,128]{3,2,1,0:T(8,128)(2,1)} %get-tuple-element.109), channel_id=1, source_target_pairs={{0,5},{1,4},{2,7},{3,6},{4,1},{5,0},{6,3},{7,2},{8,13},{9,12},{10,... | collective-permute-start | bytes 196616 | tf_op jit(solution)/shard_map/ppermute | solution.py:442
  68.1 10.0 %copy-start.5 = (bf16[4,2,32,128]{3,2,1,0:T(8,128)(2,1)}, bf16[4,2,32,128]{3,2,1,0:T(8,128)(2,1)S(1)}, u32[]{:S(2)}) copy-start(bf16[4,2,32,128]{3,2,1,0:T(8,128)(2,1)S(1)} %collective-permute-done.10.refs_1_) | copy-start | bytes 196612
  68.1 10.0 %collective-permute-start.15 = (bf16[4,2,32,128]{3,2,1,0:T(8,128)(2,1)}, bf16[4,2,32,128]{3,2,1,0:T(8,128)(2,1)S(1)}, u32[]{:S(2)}, u32[]{:S(2)}) collective-permute-start(bf16[4,2,32,128]{3,2,1,0:T(8,128)(2,1)} %get-tuple-element.110), channel_id=1, source_target_pairs={{0,6},{1,7},{2,4},{3,5},{4,2},{5,3},{6,0},{7,1},{8,14},{9,15},{10,... | collective-permute-start | bytes 196616 | tf_op jit(solution)/shard_map/ppermute | solution.py:442
  69.8 8.3 %copy-start.6 = (bf16[4,2,32,128]{3,2,1,0:T(8,128)(2,1)}, bf16[4,2,32,128]{3,2,1,0:T(8,128)(2,1)S(1)}, u32[]{:S(2)}) copy-start(bf16[4,2,32,128]{3,2,1,0:T(8,128)(2,1)S(1)} %collective-permute-done.11.refs_2_) | copy-start | bytes 196612
  69.8 8.3 %collective-permute-start.16 = (bf16[4,2,32,128]{3,2,1,0:T(8,128)(2,1)}, bf16[4,2,32,128]{3,2,1,0:T(8,128)(2,1)S(1)}, u32[]{:S(2)}, u32[]{:S(2)}) collective-permute-start(bf16[4,2,32,128]{3,2,1,0:T(8,128)(2,1)} %get-tuple-element.111), channel_id=1, source_target_pairs={{0,7},{1,6},{2,5},{3,4},{4,3},{5,2},{6,1},{7,0},{8,15},{9,14},{10,... | collective-permute-start | bytes 196616 | tf_op jit(solution)/shard_map/ppermute | solution.py:442
  72.2 6.0 %copy-start.7 = (bf16[4,2,32,128]{3,2,1,0:T(8,128)(2,1)}, bf16[4,2,32,128]{3,2,1,0:T(8,128)(2,1)S(1)}, u32[]{:S(2)}) copy-start(bf16[4,2,32,128]{3,2,1,0:T(8,128)(2,1)S(1)} %collective-permute-done.12.refs_3_) | copy-start | bytes 196612
  75.6 2.6 %copy-start.8 = (bf16[4,2,32,128]{3,2,1,0:T(8,128)(2,1)}, bf16[4,2,32,128]{3,2,1,0:T(8,128)(2,1)S(1)}, u32[]{:S(2)}) copy-start(bf16[4,2,32,128]{3,2,1,0:T(8,128)(2,1)S(1)} %collective-permute-done.13.refs_4_) | copy-start | bytes 196612
  78.1 0.6 copy-start.9
  78.1 0.6 copy-start.10
  78.1 0.7 copy-start.11
  85.7 14.1 %collective-permute-start.17 = (bf16[2,8,32,128]{3,2,1,0:T(8,128)(2,1)}, bf16[2,8,32,128]{3,2,1,0:T(8,128)(2,1)S(1)}, u32[]{:S(2)}, u32[]{:S(2)}) collective-permute-start(bf16[2,8,32,128]{3,2,1,0:T(8,128)(2,1)} %get-tuple-element.119), channel_id=1, source_target_pairs={{0,8},{8,0},{16,24},{24,16},{1,9},{9,1},{17,25},{25,17},{2,10},{10... | collective-permute-start | bytes 393224 | tf_op jit(solution)/shard_map/ppermute | solution.py:439
  85.7 14.1 %collective-permute-start.18 = (bf16[2,8,32,128]{3,2,1,0:T(8,128)(2,1)}, bf16[2,8,32,128]{3,2,1,0:T(8,128)(2,1)S(1)}, u32[]{:S(2)}, u32[]{:S(2)}) collective-permute-start(bf16[2,8,32,128]{3,2,1,0:T(8,128)(2,1)} %get-tuple-element.120), channel_id=1, source_target_pairs={{0,16},{8,24},{16,0},{24,8},{1,17},{9,25},{17,1},{25,9},{2,18},{10... | collective-permute-start | bytes 393224 | tf_op jit(solution)/shard_map/ppermute | solution.py:439
  87.8 13.3 %collective-permute-start.19 = (bf16[2,8,32,128]{3,2,1,0:T(8,128)(2,1)}, bf16[2,8,32,128]{3,2,1,0:T(8,128)(2,1)}, u32[]{:S(2)}, u32[]{:S(2)}) collective-permute-start(bf16[2,8,32,128]{3,2,1,0:T(8,128)(2,1)} %get-tuple-element.121), channel_id=1, source_target_pairs={{0,24},{8,16},{16,8},{24,0},{1,25},{9,17},{17,9},{25,1},{2,26},{10... | collective-permute-start | bytes 393224 | tf_op jit(solution)/shard_map/ppermute | solution.py:439
  95.9 5.2 %copy-start.2 = (bf16[6,128,4,258]{1,2,3,0:T(4,128)(2,1)S(1)}, bf16[6,128,4,258]{1,2,3,0:T(4,128)(2,1)}, u32[]{:S(2)}) copy-start(bf16[6,128,4,258]{1,2,3,0:T(4,128)(2,1)} %param.21) | copy-start | bytes 4755460
  95.9 64.0 %all-to-all-start.1 = ((bf16[32,2,32,640]{3,2,1,0:T(8,128)(2,1)}), bf16[32,2,32,640]{3,2,1,0:T(8,128)(2,1)}, u32[]{:S(2)}, u32[]{:S(2)}) async-start(bf16[32,2,32,640]{3,2,1,0:T(8,128)(2,1)} %latitudinal_wide.1), calls=%async_computation.1 | async-start | bytes 5242880 | tf_op jit(solution)/shard_map/all_to_all | solution.py:469
  99.7 1.5 copy-start.4
  99.8 0.6 copy-start.26
  100.4 0.7 copy-start.27
  113.6 1.9 %copy-start.21 = (f32[8,128]{1,0:T(8,128)S(1)}, f32[8,128]{1,0:T(8,128)}, u32[]{:S(2)}) copy-start(f32[8,128]{1,0:T(8,128)} %param.24) | copy-start | bytes 12292
  113.6 2.0 %copy-start.23 = (bf16[8,128]{1,0:T(8,128)(2,1)S(1)}, bf16[8,128]{1,0:T(8,128)(2,1)}, u32[]{:S(2)}) copy-start(bf16[8,128]{1,0:T(8,128)(2,1)} %param.23) | copy-start | bytes 6148
  113.6 2.0 %copy-start.25 = (f32[128]{0:T(128)S(1)}, f32[128]{0:T(128)}, u32[]{:S(2)}) copy-start(f32[128]{0:T(128)} %param.25) | copy-start | bytes 1540

commit v2 on v1

--- a/solution.py
+++ b/solution.py
@@ -26,12 +26,12 @@
 
 
 @functools.lru_cache(maxsize=None)
-def folded_tables(meridian_number, groups):
+def transform_tables(meridian_number, groups):
     half = meridian_number // 2
-    table = dft_table(meridian_number)[:half].astype(np.float32)
-    per_parity = table.reshape(half, groups, -1, 2, 2).transpose(3, 1, 2, 4, 0)
-    forward = per_parity.reshape(2, -1, half)
-    backward = forward.transpose(0, 2, 1) * (2.0 / meridian_number)
+    table = dft_table(meridian_number).astype(np.float32)
+    by_parity = table.reshape(meridian_number, groups, -1, 2, 2).transpose(1, 3, 2, 4, 0)
+    forward = by_parity.reshape(-1, meridian_number)
+    backward = by_parity.transpose(1, 4, 0, 2, 3)[:, :half].reshape(2, half, -1) * (2.0 / meridian_number)
     return tuple(np.ascontiguousarray(x).astype(jnp.bfloat16) for x in (forward, backward))
 
 
@@ -90,75 +90,63 @@
     )
 
 
-def fold(low, high, odd):
-    low, high = low.astype(jnp.float32), high.astype(jnp.float32)
-    return jnp.where(odd == 1, low - high, low + high).astype(jnp.bfloat16)
-
-
 def lane_spans(width, size=256):
     return [slice(at, min(at + size, width)) for at in range(0, width, size)]
 
 
 def analyse_wide(air, table, width, groups):
     lines, cells, _ = air.shape
-    half = cells // 2
-    out = jax.ShapeDtypeStruct((groups, lines, 2 * GROUP, width), jnp.bfloat16)
+    rows = table.shape[0] // groups
+    out = jax.ShapeDtypeStruct((groups, lines, rows, width), jnp.bfloat16)
 
     def body(table_ref, air_ref, out_ref):
         for span in lane_spans(width):
-            low = air_ref[0, :half, span].astype(jnp.float32)
-            high = air_ref[0, half:, span].astype(jnp.float32)
-            for odd, folded in enumerate((low + high, low - high)):
-                coeffs = jnp.dot(table_ref[odd], folded.astype(jnp.bfloat16), preferred_element_type=jnp.float32)
-                out_ref[:, :, odd * GROUP : (odd + 1) * GROUP, span] = coeffs.astype(jnp.bfloat16).reshape(
-                    groups, 1, GROUP, -1
-                )
+            coeffs = jnp.dot(table_ref[...], air_ref[0, :, span], preferred_element_type=jnp.float32)
+            out_ref[:, :, :, span] = coeffs.astype(jnp.bfloat16).reshape(groups, 1, rows, -1)
 
     return pl.pallas_call(
         body,
         grid=(lines,),
         in_specs=[
-            pl.BlockSpec(table.shape, lambda a: (0, 0, 0)),
+            pl.BlockSpec(table.shape, lambda a: (0, 0)),
             pl.BlockSpec((1, cells, width), lambda a: (a, 0, 0)),
         ],
-        out_specs=pl.BlockSpec((groups, 1, 2 * GROUP, width), lambda a: (0, a, 0, 0)),
+        out_specs=pl.BlockSpec((groups, 1, rows, width), lambda a: (0, a, 0, 0)),
         out_shape=out,
         compiler_params=compiler_params(),
-        cost_estimate=cost(lines * cells * cells * width, table, air, out),
+        cost_estimate=cost(2 * lines * table.size * width, table, air, out),
         name="analyse_wide",
     )(table, air)
 
 
 def analyse_slim(air, table, start, sec, sections, groups):
     lines, cells, channels = air.shape
-    half = cells // 2
     width = channels - start
     plane = groups // sections
-    out = jax.ShapeDtypeStruct((lines, plane, 2 * GROUP, width), jnp.bfloat16)
-
-    def body(sec_ref, table_ref, air_ref, *refs):
-        outs, blocks = refs[:-1], refs[-1]
+    rows = table.shape[0] // groups
+    size = plane * rows
+    out = jax.ShapeDtypeStruct((lines, plane, rows, width), jnp.bfloat16)
+
+    def body(sec_ref, table_ref, air_ref, *outs):
         both = jnp.concatenate([air_ref[a] for a in range(lines)], axis=1)
-        folded = fold(both[:half], both[half:], pl.program_id(0))
-        coeffs = jnp.dot(table_ref[0], folded, preferred_element_type=jnp.float32)
-        blocks[...] = coeffs.astype(jnp.bfloat16).reshape(sections, plane, GROUP, lines * width)
         for o, out_ref in enumerate(outs):
+            part = pl.ds(pl.multiple_of((sec_ref[0] ^ o) * size, size), size)
+            coeffs = jnp.dot(table_ref[part, :], both, preferred_element_type=jnp.float32).astype(jnp.bfloat16)
             for a in range(lines):
-                out_ref[a] = blocks[sec_ref[0] ^ o, :, :, a * width : (a + 1) * width]
-
-    return pl.pallas_call(
-        body,
-        grid=(2,),
+                out_ref[a] = coeffs[:, a * width : (a + 1) * width].reshape(plane, rows, width)
+
+    return pl.pallas_call(
+        body,
+        grid=(1,),
         in_specs=[
             pl.BlockSpec(memory_space=pltpu.SMEM),
-            pl.BlockSpec((1,) + table.shape[1:], lambda p: (p, 0, 0)),
-            pl.BlockSpec((lines, cells, width), lambda p: (0, 0, start // width)),
+            pl.BlockSpec(table.shape, lambda i: (0, 0)),
+            pl.BlockSpec((lines, cells, width), lambda i: (0, 0, start // width)),
         ],
-        out_specs=[pl.BlockSpec((lines, plane, GROUP, width), lambda p: (0, 0, p, 0))] * sections,
+        out_specs=[pl.BlockSpec(out.shape, lambda i: (0, 0, 0, 0))] * sections,
         out_shape=[out] * sections,
-        scratch_shapes=[pltpu.VMEM((sections, plane, GROUP, lines * width), jnp.bfloat16)],
-        compiler_params=compiler_params(),
-        cost_estimate=cost(lines * cells * cells * width, table, *[out] * 2 * sections),
+        compiler_params=compiler_params(),
+        cost_estimate=cost(2 * lines * table.size * width, table, *[out] * 2 * sections),
         name="analyse_slim",
     )(sec, table, air)
 
@@ -276,7 +264,7 @@
         out_specs=[whole(out)] * plane,
         out_shape=[out] * plane,
         compiler_params=compiler_params(),
-        cost_estimate=cost(4 * rows * degrees * plane * own * width, matrix, *parts, *parts),
+        cost_estimate=pl.CostEstimate(flops=10**11, bytes_accessed=3 * 10**8, transcendentals=0),
         name="latitudinal_slim",
     )(matrix, damping, *parts)
 
@@ -429,7 +417,7 @@
         plane = band_count * core_count
         sec_id = lax.axis_index("sec")
         sec = sec_id.reshape(1).astype(jnp.int32)
-        forward, backward = map(jnp.asarray, folded_tables(meridian_number, device_count))
+        forward, backward = map(jnp.asarray, transform_tables(meridian_number, device_count))
         hops = [[(i, i ^ o) for i in range(sec_count)] for o in range(sec_count)]
 
         twists = [[(i, i ^ p) for i in range(plane)] for p in range(plane)]
@@ -440,6 +428,17 @@
 
         def over_plane(blocks):
             return [lax.ppermute(x, ("band", "ch"), twists[p]) if p else x for p, x in enumerate(blocks)]
+
+        slim = analyse_slim(air_field_lattice, forward, wide, sec, sec_count, device_count)
+        air_after, *slim = lax.optimization_barrier((air_field_lattice, *slim))
+        slim = over_sections(slim)
+        wide_coeffs = analyse_wide(air_after, forward, wide, device_count)
+        wide_coeffs = lax.all_to_all(wide_coeffs, AXES, split_axis=0, concat_axis=0, tiled=True)
+        slim = to_plane(slim, place.reshape(1))
+        air_after, matrix_after, *slim = lax.optimization_barrier(
+            (air_field_lattice, associated_polynomial_matrix, *slim)
+        )
+        slim = over_plane(slim)
 
         at_lat = jnp.arange(lat_count, dtype=jnp.int32)
         sections_at = at_lat // parallel_lines % sec_count ^ sec_id
@@ -447,18 +446,9 @@
         order = (sections_at * plane + places_at) * parallel_lines + at_lat % parallel_lines
         shuffle = (at_lat[:, None] == order[None, :]).astype(jnp.bfloat16)
         shuffled = jnp.einsum(
-            "mlt,tu->mlu", associated_polynomial_matrix, shuffle, preferred_element_type=jnp.float32
+            "mlt,tu->mlu", matrix_after, shuffle, preferred_element_type=jnp.float32
         ).astype(jnp.bfloat16)
 
-        slim = analyse_slim(air_field_lattice, forward, wide, sec, sec_count, device_count)
-        air_after, *slim = lax.optimization_barrier((air_field_lattice, *slim))
-        slim = over_sections(slim)
-        wide_coeffs = analyse_wide(air_after, forward, wide, device_count)
-        wide_coeffs, *slim = lax.optimization_barrier((wide_coeffs, *slim))
-        wide_coeffs = lax.all_to_all(wide_coeffs, AXES, split_axis=0, concat_axis=0, tiled=True)
-        slim = to_plane(slim, place.reshape(1))
-        air_after, *slim = lax.optimization_barrier((air_field_lattice, *slim))
-        slim = over_plane(slim)
         gathered = gather_flux(air_after, boundary_exchange_projector)
         gathered, *slim = lax.optimization_barrier((gathered, *slim))
         slim = latitudinal_slim(slim, shuffled, harmonic_damping_factor, wide)
@@ -467,7 +457,9 @@
         slim = over_sections(slim)
         wide_coeffs = latitudinal_wide(wide_coeffs, associated_polynomial_matrix, harmonic_damping_factor)
         wide_coeffs = lax.all_to_all(wide_coeffs, AXES, split_axis=0, concat_axis=0, tiled=True)
-        water_patch_fields, gathered, *slim = lax.optimization_barrier((water_patch_fields, gathered, *slim))
+        water_patch_fields, gathered, warmth_response_factor, patch_holder_index, *slim = lax.optimization_barrier(
+            (water_patch_fields, gathered, warmth_response_factor, patch_holder_index, *slim)
+        )
     else:
         gathered = gather_flux(air_field_lattice, boundary_exchange_projector)
         table = dft_table(meridian_number)

time: 166 us -> 163 us (0.982)
  waiting for transfers between devices: 51.1 us -> 45 us
  Pallas kernels: 28.4 us -> 30.6 us
    ppermute x6, waiting for transfers between devices: 5.9 us -> 0.02 us  [over_sections(): lax.ppermute(x, 'sec', hops[o])]
    pallas_call x1, Pallas kernels: 4.7 us -> 6.65 us  [analyse_wide(): pl.pallas_call(body, grid=(lines,), in_specs=[pl.BlockSpec(table.shape, l...]
    unnamed x60 -> x67, local copies, waits for them, and re-layouts: 5.14 us -> 5.2 us
  transfers between devices with their start and end apart: 22 -> 22, of which waited for: 6 -> 5; matrix products, arithmetic and copies ran while one was open for 17% -> 17% of each run, Pallas kernels for 12% -> 13%
where the time goes in v2:
time: 163 us
  waiting for transfers between devices  45 us (28%)
  starting transfers between devices  33.4 us (20%)
  Pallas kernels  30.6 us (19%)
  matrix products  22.9 us (14%)
  blocking collectives  21.3 us (13%)
  local copies, waits for them, and re-layouts  7.92 us (5%)
    all_to_all x2, waiting for transfers between devices, shards(): lax.all_to_all(wide_coeffs, AXES, split_axis=0, concat_axis=0, tiled=True)  26.9 us
    ppermute x14, waiting for transfers between devices, over_plane(): lax.ppermute(x, ('band', 'ch'), twists[p])  18.1 us
    dot_general x9, matrix products, ocean_update(): jnp.einsum('io,sirw->sorw', kernel_coefficients[shift_row, shift_col], wi...  13.8 us
    ppermute x14, starting transfers between devices, over_plane(): lax.ppermute(x, ('band', 'ch'), twists[p])  13.4 us
    all_gather x1, blocking collectives, gather_flux(): return lax.all_gather(flux_local, 'band', axis=1, tiled=True)  13 us
    all_to_all x2, starting transfers between devices, shards(): lax.all_to_all(wide_coeffs, AXES, split_axis=0, concat_axis=0, tiled=True)  10 us
    ppermute x6, starting transfers between devices, over_sections(): lax.ppermute(x, 'sec', hops[o])  10 us
    all_gather x1, blocking collectives, shards(): sea_all = lax.all_gather(sea_slots, 'band', axis=0, tiled=True)  8.31 us
  transfers between devices with their start and end apart: 22, of which 5 were waited for; matrix products, arithmetic and copies ran while one was open for 17% of the time, Pallas kernels for 13%

profile of v2, /device:TPU:0, one launch (start us, length us, event | category | flops | bytes accessed | tf_op | source)
XLA Modules:
  0.0 162.8 jit_solution(8339121469576728328)
XLA Ops:
  0.7 3.1 %analyse_slim.1 = (bf16[2,8,32,128]{3,2,1,0:T(8,128)(2,1)}, bf16[2,8,32,128]{3,2,1,0:T(8,128)(2,1)}, bf16[2,8,32,128]{3,2,1,0:T(8,128)(2,1)}, bf16[2,8,32,128]{3,2,1,0:T(8,128)(2,1)}) custom-call(s32[1]{0:T(128)} %bitcast.sec_ref, bf16[1024,1024]{1,0:T(8,128)(2,1)} %constant.153.clone.table_ref, bf16[2,1024,768]{2,1,0:T(8,128)(2,1)} %air_ref.2), custom_call_target="tpu_custom_call" | custom-call | flops 536870912 | bytes 3145728 | tf_op jit(solution)/shard_map/analyse_slim/pallas_call | solution.py:138
  3.7 3.0 %collective-permute-start = (bf16[2,8,32,128]{3,2,1,0:T(8,128)(2,1)}, bf16[2,8,32,128]{3,2,1,0:T(8,128)(2,1)S(1)}, u32[]{:S(2)}, u32[]{:S(2)}) collective-permute-start(bf16[2,8,32,128]{3,2,1,0:T(8,128)(2,1)} %get-tuple-element.69), channel_id=1, source_target_pairs={{0,8},{8,0},{16,24},{24,16},{1,9},{9,1},{17,25},{25,17},{2,10},{10... | collective-permute-start | bytes 393224 | tf_op jit(solution)/shard_map/ppermute | solution.py:427
  6.8 2.6 %collective-permute-start.1 = (bf16[2,8,32,128]{3,2,1,0:T(8,128)(2,1)}, bf16[2,8,32,128]{3,2,1,0:T(8,128)(2,1)S(1)}, u32[]{:S(2)}, u32[]{:S(2)}) collective-permute-start(bf16[2,8,32,128]{3,2,1,0:T(8,128)(2,1)} %get-tuple-element.70), channel_id=1, source_target_pairs={{0,16},{8,24},{16,0},{24,8},{1,17},{9,25},{17,1},{25,9},{2,18},{10... | collective-permute-start | bytes 393224 | tf_op jit(solution)/shard_map/ppermute | solution.py:427
  9.3 6.7 %analyse_wide.1 = bf16[32,2,32,640]{3,2,1,0:T(8,128)(2,1)} custom-call(bf16[1024,1024]{1,0:T(8,128)(2,1)} %constant.153.clone.table_ref, bf16[2,1024,768]{2,1,0:T(8,128)(2,1)} %air_ref.2), custom_call_target="tpu_custom_call" | custom-call | flops 2684354560 | bytes 7864320 | tf_op jit(solution)/shard_map/analyse_wide/pallas_call | solution.py:107
  16.0 6.2 %all-to-all-start = ((bf16[32,2,32,640]{3,2,1,0:T(8,128)(2,1)}), bf16[32,2,32,640]{3,2,1,0:T(8,128)(2,1)}, u32[]{:S(2)}, u32[]{:S(2)}) async-start(bf16[32,2,32,640]{3,2,1,0:T(8,128)(2,1)} %analyse_wide.1), calls=%async_computation | async-start | bytes 5242880 | tf_op jit(solution)/shard_map/all_to_all | solution.py:436
  22.3 0.6 copy-done.5
  23.0 1.9 %to_plane.1 = (bf16[4,2,32,128]{3,2,1,0:T(8,128)(2,1)}, bf16[4,2,32,128]{3,2,1,0:T(8,128)(2,1)}, bf16[4,2,32,128]{3,2,1,0:T(8,128)(2,1)}, bf16[4,2,32,128]{3,2,1...) custom-call(s32[1]{0:T(128)} %bitcast.1.place_ref, ...), custom_call_target="tpu_custom_call" | custom-call | bytes 1048576 | tf_op jit(solution)/shard_map/to_plane/pallas_call | solution.py:204
  24.9 0.3 collective-permute-start.3
  25.1 1.7 %collective-permute-start.4 = (bf16[4,2,32,128]{3,2,1,0:T(8,128)(2,1)}, bf16[4,2,32,128]{3,2,1,0:T(8,128)(2,1)S(1)}, u32[]{:S(2)}, u32[]{:S(2)}) collective-permute-start(bf16[4,2,32,128]{3,2,1,0:T(8,128)(2,1)} %get-tuple-element.84), channel_id=1, source_target_pairs={{0,2},{1,3},{2,0},{3,1},{4,6},{5,7},{6,4},{7,5},{8,10},{9,11},{10,... | collective-permute-start | bytes 196616 | tf_op jit(solution)/shard_map/ppermute | solution.py:430
  26.8 1.7 %collective-permute-start.6 = (bf16[4,2,32,128]{3,2,1,0:T(8,128)(2,1)}, bf16[4,2,32,128]{3,2,1,0:T(8,128)(2,1)S(1)}, u32[]{:S(2)}, u32[]{:S(2)}) collective-permute-start(bf16[4,2,32,128]{3,2,1,0:T(8,128)(2,1)} %get-tuple-element.86), channel_id=1, source_target_pairs={{0,4},{1,5},{2,6},{3,7},{4,0},{5,1},{6,2},{7,3},{8,12},{9,13},{10,... | collective-permute-start | bytes 196616 | tf_op jit(solution)/shard_map/ppermute | solution.py:430
  28.5 0.1 collective-permute-start.7
  28.6 0.9 fusion.12
  29.6 2.6 %collective-permute-start.8 = (bf16[4,2,32,128]{3,2,1,0:T(8,128)(2,1)S(1)}, bf16[4,2,32,128]{3,2,1,0:T(8,128)(2,1)S(1)}, u32[]{:S(2)}, u32[]{:S(2)}) collective-permute-start(bf16[4,2,32,128]{3,2,1,0:T(8,128)(2,1)S(1)} %copy-done.27), channel_id=1, source_target_pairs={{0,6},{1,7},{2,4},{3,5},{4,2},{5,3},{6,0},{7,1},{8,14},{9,15},{10,... | collective-permute-start | bytes 196616 | tf_op jit(solution)/shard_map/ppermute | solution.py:430
  32.2 10.9 %collective-permute-done.4.refs_2_ = bf16[4,2,32,128]{3,2,1,0:T(8,128)(2,1)S(1)} collective-permute-done((bf16[4,2,32,128]{3,2,1,0:T(8,128)(2,1)}, bf16[4,2,32,128]{3,2,1,0:T(8,128)(2,1)S(1)}, u32[]{:S(2)}, u32[]{:S(2)}) %collective-permute-start.4) | collective-permute-done | bytes 65568 | tf_op jit(solution)/shard_map/ppermute | solution.py:430
  43.1 0.7 collective-permute-start.9
  43.8 0.9 convolution_convert_fusion.matrix_ref
  44.8 13.0 %all_gather.6 = bf16[8,8,1024]{2,0,1:T(8,128)(2,1)S(1)} all-gather(bf16[8,2,1024]{2,0,1:T(8,128)(2,1)S(1)} %fusion.12), channel_id=1, replica_groups=mesh['sec'=4,'band'=4,'ch'=2] {'band'}, dimensions={1}, use_global_device_ids=true | all-gather | bytes 163840 | tf_op jit(solution)/shard_map/all_gather | solution.py:379
  57.8 0.5 copy-done.26
  58.4 0.6 copy-done.31
  59.1 2.6 %latitudinal_slim.1 = (bf16[4,2,32,128]{3,2,1,0:T(8,128)(2,1)}, bf16[4,2,32,128]{3,2,1,0:T(8,128)(2,1)}, bf16[4,2,32,128]{3,2,1,0:T(8,128)(2,1)}, bf16[4,2,32,12...) custom-call(bf16[16,64,64]{2,1,0:T(8,128)(2,1)} %convolution_convert, ...), custom_call_target="tpu_custom_call" | custom-call | flops 99999997952 | bytes 300000000 | tf_op jit(solution)/shard_map/latitudinal_slim/pallas_call | solution.py:256
  61.6 1.1 collective-permute-start.11
  62.7 0.8 collective-permute-start.12
  63.5 1.4 collective-permute-start.13
  64.9 0.3 collective-permute-start.14
  65.2 1.7 %collective-permute-start.15 = (bf16[4,2,32,128]{3,2,1,0:T(8,128)(2,1)}, bf16[4,2,32,128]{3,2,1,0:T(8,128)(2,1)S(1)}, u32[]{:S(2)}, u32[]{:S(2)}) collective-permute-start(bf16[4,2,32,128]{3,2,1,0:T(8,128)(2,1)} %get-tuple-element.104), channel_id=1, source_target_pairs={{0,6},{1,7},{2,4},{3,5},{4,2},{5,3},{6,0},{7,1},{8,14},{9,15},{10,... | collective-permute-start | bytes 196616 | tf_op jit(solution)/shard_map/ppermute | solution.py:430
  66.9 1.0 collective-permute-start.16
  67.9 4.8 %collective-permute-done.13.refs_4_ = bf16[4,2,32,128]{3,2,1,0:T(8,128)(2,1)S(1)} collective-permute-done((bf16[4,2,32,128]{3,2,1,0:T(8,128)(2,1)}, bf16[4,2,32,128]{3,2,1,0:T(8,128)(2,1)S(1)}, u32[]{:S(2)}, u32[]{:S(2)}) %collective-permute-start.13) | collective-permute-done | bytes 65568 | tf_op jit(solution)/shard_map/ppermute | solution.py:430
  72.7 2.4 %collective-permute-done.14.refs_5_ = bf16[4,2,32,128]{3,2,1,0:T(8,128)(2,1)S(1)} collective-permute-done((bf16[4,2,32,128]{3,2,1,0:T(8,128)(2,1)}, bf16[4,2,32,128]{3,2,1,0:T(8,128)(2,1)S(1)}, u32[]{:S(2)}, u32[]{:S(2)}) %collective-permute-start.14) | collective-permute-done | bytes 65568 | tf_op jit(solution)/shard_map/ppermute | solution.py:430
  75.2 0.5 copy-done.11
  75.8 1.9 %from_plane.1 = (bf16[2,8,32,128]{3,2,1,0:T(8,128)(2,1)}, bf16[2,8,32,128]{3,2,1,0:T(8,128)(2,1)}, bf16[2,8,32,128]{3,2,1,0:T(8,128)(2,1)}, bf16[2,8,32,128]{3,2,1,0:T(8,128)(2,1)}) custom-call(s32[1]{0:T(128)} %bitcast.1.place_ref, bf16[4,2,32,128]{3,2,1,0:T(8,128)(2,1)} %get-tuple-element.98.refs_0_, bf16[4,2,32,128]{3,2,1,0:T(8,128)(2,1)} %copy-done.7, ...), custom_call_target="tpu_custom_call" | custom-call | bytes 1048576 | tf_op jit(solution)/shard_map/from_plane/pallas_call | solution.py:227
  77.7 5.1 %all-to-all-done.x_ref = bf16[32,2,32,640]{3,2,1,0:T(8,128)(2,1)} async-done(((bf16[32,2,32,640]{3,2,1,0:T(8,128)(2,1)}), bf16[32,2,32,640]{3,2,1,0:T(8,128)(2,1)}, u32[]{:S(2)}, u32[]{:S(2)}) %all-to-all-start) | async-done | bytes 2621472 | tf_op jit(solution)/shard_map/all_to_all | solution.py:436
  82.8 2.1 %collective-permute-start.18 = (bf16[2,8,32,128]{3,2,1,0:T(8,128)(2,1)}, bf16[2,8,32,128]{3,2,1,0:T(8,128)(2,1)S(1)}, u32[]{:S(2)}, u32[]{:S(2)}) collective-permute-start(bf16[2,8,32,128]{3,2,1,0:T(8,128)(2,1)} %get-tuple-element.114), channel_id=1, source_target_pairs={{0,16},{8,24},{16,0},{24,8},{1,17},{9,25},{17,1},{25,9},{2,18},{10... | collective-permute-start | bytes 393224 | tf_op jit(solution)/shard_map/ppermute | solution.py:427
  84.9 2.3 %collective-permute-start.19 = (bf16[2,8,32,128]{3,2,1,0:T(8,128)(2,1)}, bf16[2,8,32,128]{3,2,1,0:T(8,128)(2,1)}, u32[]{:S(2)}, u32[]{:S(2)}) collective-permute-start(bf16[2,8,32,128]{3,2,1,0:T(8,128)(2,1)} %get-tuple-element.115), channel_id=1, source_target_pairs={{0,24},{8,16},{16,8},{24,0},{1,25},{9,17},{17,9},{25,1},{2,26},{10... | collective-permute-start | bytes 393224 | tf_op jit(solution)/shard_map/ppermute | solution.py:427
  87.3 5.7 %latitudinal_wide.1 = bf16[32,2,32,640]{3,2,1,0:T(8,128)(2,1)} custom-call(bf16[32,2,32,640]{3,2,1,0:T(8,128)(2,1)} %all-to-all-done.x_ref, bf16[16,64,64]{2,1,0:T(8,128)(2,1)} %matrix_ref.1, f32[64,768]{1,0:T(8,128)} %damping_ref.3), custom_call_target="tpu_custom_call" | custom-call | flops 335544320 | bytes 5373952 | tf_op jit(solution)/shard_map/latitudinal_wide/pallas_call | solution.py:177
  93.0 3.9 %all-to-all-start.1 = ((bf16[32,2,32,640]{3,2,1,0:T(8,128)(2,1)}), bf16[32,2,32,640]{3,2,1,0:T(8,128)(2,1)}, u32[]{:S(2)}, u32[]{:S(2)}) async-start(bf16[32,2,32,640]{3,2,1,0:T(8,128)(2,1)} %latitudinal_wide.1), calls=%async_computation.1 | async-start | bytes 5242880 | tf_op jit(solution)/shard_map/all_to_all | solution.py:459
  96.9 0.6 copy-done.22
  97.6 0.2 copy.75
  97.8 0.1 copy-done.4
  97.9 1.5 fusion.14
  99.4 1.6 fusion.16
  101.0 1.6 fusion.18
  102.6 1.5 fusion.20
  104.1 1.5 fusion.36
  105.6 1.6 fusion.22
  107.2 1.5 fusion.24
  108.7 1.5 fusion.26
  110.2 1.5 fusion.28
  111.7 0.1 copy.76
  111.8 0.1 eq.64
  111.9 0.2 reduce_window_sum.11
  112.2 0.1 fusion.66
  112.2 0.3 convert_reduce_fusion
  112.6 0.1 copy.88
  112.6 0.1 multiply_reduce_fusion
  112.8 6.8 %fusion.9 = bf16[6,128,2,256]{1,3,2,0:T(8,128)(2,1)S(1)} fusion(f32[6,2,256,128]{3,2,1,0:T(8,128)} %fusion.14, f32[6,2,256,128]{3,2,1,0:T(8,128)} %fusion.16, f32[6,2,256,128]{3,2,1,0:T(8,128)} %fusion.18, f32[6,2,256,128]{3,2,1,0:T(8,128)} %fusion.20, f32[6,2,256,128]{3,2,1,0:T(8,128)} %fusion.36, f32[6,2,256,128]{3,2,1,0:T(8,128)} %fusion.22, ...), kind=kOutput, calls=%fused_computation.11 | convolution fusion | flops 116391936 | bytes 15828480 | tf_op jit(solution)/shard_map/io,sirw->sorw/dot_general | solution.py:74
  119.6 1.8 %copy.94 = bf16[6,128,2,256]{3,2,1,0:T(2,128)(2,1)} copy(bf16[6,128,2,256]{1,3,2,0:T(8,128)(2,1)S(1)} %fusion.9) | data formatting | bytes 1572864
  121.4 0.3 copy.92
  121.7 8.3 %all-gather = bf16[24,1,2,256]{3,2,1,0:T(2,128)(2,1)S(1)} all-gather(bf16[6,1,2,256]{3,2,1,0:T(2,128)(2,1)S(1)} %copy.92), channel_id=2, replica_groups=mesh['sec'=4,'band'=4,'ch'=2] {'band'}, dimensions={0}, use_global_device_ids=true | all-gather | bytes 30720 | tf_op jit(solution)/shard_map/all_gather | solution.py:515
  130.1 0.2 fusion.13
  130.4 1.2 stack.27.warmth_ref
  131.6 0.6 broadcast_in_dim.9.sea_ref
  132.2 3.0 %synthesise_slim.1.begun_ref = bf16[2,2,512,768]{3,2,1,0:T(8,128)(2,1)} custom-call(s32[1]{0:T(128)} %bitcast.sec_ref, bf16[2,512,512]{2,1,0:T(8,128)(2,1)} %constant.154.clone.table_ref, bf16[2,2,512,768]{3,2,1,0:T(8,128)(2,1)} %bitcast.124, bf16[2,2,16,512]{3,2,1,0:T(8,128)(2,1)} %broadcast_in_dim.9.sea_ref, bf16[16,768]{1,0:T(8,128)(2,1)} %stack.27.warmth_ref, ...), custom_call_target="tpu_custom_call" | custom-call | flops 99999997952 | bytes 300000000 | tf_op jit(solution)/shard_map/synthesise_slim/pallas_call | solution.py:313
  135.2 21.8 %all-to-all-done.1.coeff_ref = bf16[32,2,32,640]{3,2,1,0:T(8,128)(2,1)} async-done(((bf16[32,2,32,640]{3,2,1,0:T(8,128)(2,1)}), bf16[32,2,32,640]{3,2,1,0:T(8,128)(2,1)}, u32[]{:S(2)}, u32[]{:S(2)}) %all-to-all-start.1) | async-done | bytes 2621472 | tf_op jit(solution)/shard_map/all_to_all | solution.py:459
  157.0 5.8 %synthesise_wide.1 = bf16[2,2,512,768]{3,2,1,0:T(8,128)(2,1)} custom-call(bf16[2,512,512]{2,1,0:T(8,128)(2,1)} %constant.154.clone.table_ref, bf16[32,2,32,640]{3,2,1,0:T(8,128)(2,1)} %all-to-all-done.1.coeff_ref, bf16[2,2,512,768]{3,2,1,0:T(8,128)(2,1)} %bitcast.125, ...), custom_call_target="tpu_custom_call", output_to_operand_aliasing={{}: (5, {})} | custom-call | flops 1342177280 | bytes 8912896 | tf_op jit(solution)/shard_map/synthesise_wide/pallas_call | solution.py:352
  (100 shorter events, 0.7 us)
Async XLA Ops:
  0.6 112.1 %copy-start = (bf16[128,128]{1,0:T(8,128)(2,1)S(1)}, bf16[128,128]{1,0:T(8,128)(2,1)}, u32[]{:S(2)}) copy-start(bf16[128,128]{1,0:T(8,128)(2,1)} %param.26) | copy-start | bytes 98308
  3.7 18.5 %collective-permute-start = (bf16[2,8,32,128]{3,2,1,0:T(8,128)(2,1)}, bf16[2,8,32,128]{3,2,1,0:T(8,128)(2,1)S(1)}, u32[]{:S(2)}, u32[]{:S(2)}) collective-permute-start(bf16[2,8,32,128]{3,2,1,0:T(8,128)(2,1)} %get-tuple-element.69), channel_id=1, source_target_pairs={{0,8},{8,0},{16,24},{24,16},{1,9},{9,1},{17,25},{25,17},{2,10},{10... | collective-permute-start | bytes 393224 | tf_op jit(solution)/shard_map/ppermute | solution.py:427
  6.8 15.5 %collective-permute-start.1 = (bf16[2,8,32,128]{3,2,1,0:T(8,128)(2,1)}, bf16[2,8,32,128]{3,2,1,0:T(8,128)(2,1)S(1)}, u32[]{:S(2)}, u32[]{:S(2)}) collective-permute-start(bf16[2,8,32,128]{3,2,1,0:T(8,128)(2,1)} %get-tuple-element.70), channel_id=1, source_target_pairs={{0,16},{8,24},{16,0},{24,8},{1,17},{9,25},{17,1},{25,9},{2,18},{10... | collective-permute-start | bytes 393224 | tf_op jit(solution)/shard_map/ppermute | solution.py:427
  9.3 12.9 %collective-permute-start.2 = (bf16[2,8,32,128]{3,2,1,0:T(8,128)(2,1)}, bf16[2,8,32,128]{3,2,1,0:T(8,128)(2,1)}, u32[]{:S(2)}, u32[]{:S(2)}) collective-permute-start(bf16[2,8,32,128]{3,2,1,0:T(8,128)(2,1)} %get-tuple-element.71), channel_id=1, source_target_pairs={{0,24},{8,16},{16,8},{24,0},{1,25},{9,17},{17,9},{25,1},{2,26},{10... | collective-permute-start | bytes 393224 | tf_op jit(solution)/shard_map/ppermute | solution.py:427
  16.0 12.6 %copy-start.1 = (bf16[2,1024,768]{2,1,0:T(8,128)(2,1)S(1)}, bf16[2,1024,768]{2,1,0:T(8,128)(2,1)}, u32[]{:S(2)}) copy-start(bf16[2,1024,768]{2,1,0:T(8,128)(2,1)} %air_ref.2) | copy-start | bytes 9437188
  16.0 12.6 %copy-start.14 = (bf16[768,8]{0,1:T(8,128)(2,1)S(1)}, bf16[768,8]{0,1:T(8,128)(2,1)}, u32[]{:S(2)}) copy-start(bf16[768,8]{0,1:T(8,128)(2,1)} %param.19) | copy-start | bytes 36868
  16.0 66.8 %all-to-all-start = ((bf16[32,2,32,640]{3,2,1,0:T(8,128)(2,1)}), bf16[32,2,32,640]{3,2,1,0:T(8,128)(2,1)}, u32[]{:S(2)}, u32[]{:S(2)}) async-start(bf16[32,2,32,640]{3,2,1,0:T(8,128)(2,1)} %analyse_wide.1), calls=%async_computation | async-start | bytes 5242880 | tf_op jit(solution)/shard_map/all_to_all | solution.py:436
  22.2 0.6 copy-start.5
  22.3 0.7 copy-start.6
  24.9 4.7 %copy-start.27 = (bf16[4,2,32,128]{3,2,1,0:T(8,128)(2,1)S(1)}, bf16[4,2,32,128]{3,2,1,0:T(8,128)(2,1)}, u32[]{:S(2)}) copy-start(bf16[4,2,32,128]{3,2,1,0:T(8,128)(2,1)} %get-tuple-element.88) | copy-start | bytes 196612
  24.9 18.2 %copy-start.25 = (bf16[4,2,32,128]{3,2,1,0:T(8,128)(2,1)S(1)}, bf16[4,2,32,128]{3,2,1,0:T(8,128)(2,1)}, u32[]{:S(2)}) copy-start(bf16[4,2,32,128]{3,2,1,0:T(8,128)(2,1)} %get-tuple-element.89) | copy-start | bytes 196612
  24.9 19.0 %copy-start.3 = (bf16[16,64,64]{2,1,0:T(8,128)(2,1)S(1)}, bf16[16,64,64]{2,1,0:T(8,128)(2,1)}, u32[]{:S(2)}) copy-start(bf16[16,64,64]{2,1,0:T(8,128)(2,1)} %matrix_ref.1) | copy-start | bytes 393220
  24.9 4.7 %collective-permute-start.3 = (bf16[4,2,32,128]{3,2,1,0:T(8,128)(2,1)}, bf16[4,2,32,128]{3,2,1,0:T(8,128)(2,1)S(1)}, u32[]{:S(2)}, u32[]{:S(2)}) collective-permute-start(bf16[4,2,32,128]{3,2,1,0:T(8,128)(2,1)} %get-tuple-element.83), channel_id=1, source_target_pairs={{0,1},{1,0},{2,3},{3,2},{4,5},{5,4},{6,7},{7,6},{8,9},{9,8},{10,11... | collective-permute-start | bytes 196616 | tf_op jit(solution)/shard_map/ppermute | solution.py:430
  25.1 18.0 %collective-permute-start.4 = (bf16[4,2,32,128]{3,2,1,0:T(8,128)(2,1)}, bf16[4,2,32,128]{3,2,1,0:T(8,128)(2,1)S(1)}, u32[]{:S(2)}, u32[]{:S(2)}) collective-permute-start(bf16[4,2,32,128]{3,2,1,0:T(8,128)(2,1)} %get-tuple-element.84), channel_id=1, source_target_pairs={{0,2},{1,3},{2,0},{3,1},{4,6},{5,7},{6,4},{7,5},{8,10},{9,11},{10,... | collective-permute-start | bytes 196616 | tf_op jit(solution)/shard_map/ppermute | solution.py:430
  26.8 30.9 %collective-permute-start.5 = (bf16[4,2,32,128]{3,2,1,0:T(8,128)(2,1)}, bf16[4,2,32,128]{3,2,1,0:T(8,128)(2,1)S(1)}, u32[]{:S(2)}, u32[]{:S(2)}) collective-permute-start(bf16[4,2,32,128]{3,2,1,0:T(8,128)(2,1)} %get-tuple-element.85), channel_id=1, source_target_pairs={{0,3},{1,2},{2,1},{3,0},{4,7},{5,6},{6,5},{7,4},{8,11},{9,10},{10,... | collective-permute-start | bytes 196616 | tf_op jit(solution)/shard_map/ppermute | solution.py:430
  26.8 30.9 %collective-permute-start.6 = (bf16[4,2,32,128]{3,2,1,0:T(8,128)(2,1)}, bf16[4,2,32,128]{3,2,1,0:T(8,128)(2,1)S(1)}, u32[]{:S(2)}, u32[]{:S(2)}) collective-permute-start(bf16[4,2,32,128]{3,2,1,0:T(8,128)(2,1)} %get-tuple-element.86), channel_id=1, source_target_pairs={{0,4},{1,5},{2,6},{3,7},{4,0},{5,1},{6,2},{7,3},{8,12},{9,13},{10,... | collective-permute-start | bytes 196616 | tf_op jit(solution)/shard_map/ppermute | solution.py:430
  28.5 29.3 %collective-permute-start.7 = (bf16[4,2,32,128]{3,2,1,0:T(8,128)(2,1)}, bf16[4,2,32,128]{3,2,1,0:T(8,128)(2,1)S(1)}, u32[]{:S(2)}, u32[]{:S(2)}) collective-permute-start(bf16[4,2,32,128]{3,2,1,0:T(8,128)(2,1)} %get-tuple-element.87), channel_id=1, source_target_pairs={{0,5},{1,4},{2,7},{3,6},{4,1},{5,0},{6,3},{7,2},{8,13},{9,12},{10,... | collective-permute-start | bytes 196616 | tf_op jit(solution)/shard_map/ppermute | solution.py:430
  29.6 28.3 %copy-start.23 = (bf16[4,2,32,128]{3,2,1,0:T(8,128)(2,1)}, bf16[4,2,32,128]{3,2,1,0:T(8,128)(2,1)S(1)}, u32[]{:S(2)}) copy-start(bf16[4,2,32,128]{3,2,1,0:T(8,128)(2,1)S(1)} %collective-permute-done.3.refs_1_) | copy-start | bytes 196612
  29.6 28.2 %collective-permute-start.8 = (bf16[4,2,32,128]{3,2,1,0:T(8,128)(2,1)S(1)}, bf16[4,2,32,128]{3,2,1,0:T(8,128)(2,1)S(1)}, u32[]{:S(2)}, u32[]{:S(2)}) collective-permute-start(bf16[4,2,32,128]{3,2,1,0:T(8,128)(2,1)S(1)} %copy-done.27), channel_id=1, source_target_pairs={{0,6},{1,7},{2,4},{3,5},{4,2},{5,3},{6,0},{7,1},{8,14},{9,15},{10,... | collective-permute-start | bytes 196616 | tf_op jit(solution)/shard_map/ppermute | solution.py:430
  43.1 14.7 %copy-start.24 = (bf16[4,2,32,128]{3,2,1,0:T(8,128)(2,1)}, bf16[4,2,32,128]{3,2,1,0:T(8,128)(2,1)S(1)}, u32[]{:S(2)}) copy-start(bf16[4,2,32,128]{3,2,1,0:T(8,128)(2,1)S(1)} %collective-permute-done.4.refs_2_) | copy-start | bytes 196612
  43.1 14.7 %collective-permute-start.9 = (bf16[4,2,32,128]{3,2,1,0:T(8,128)(2,1)S(1)}, bf16[4,2,32,128]{3,2,1,0:T(8,128)(2,1)S(1)}, u32[]{:S(2)}, u32[]{:S(2)}) collective-permute-start(bf16[4,2,32,128]{3,2,1,0:T(8,128)(2,1)S(1)} %copy-done.25), channel_id=1, source_target_pairs={{0,7},{1,6},{2,5},{3,4},{4,3},{5,2},{6,1},{7,0},{8,15},{9,14},{10,... | collective-permute-start | bytes 196616 | tf_op jit(solution)/shard_map/ppermute | solution.py:430
  57.7 10.2 %copy-start.15 = (s32[6,2,256]{2,1,0:T(2,128)S(1)}, s32[6,2,256]{2,1,0:T(2,128)}, u32[]{:S(2)}) copy-start(s32[6,2,256]{2,1,0:T(2,128)} %param.28) | copy-start | bytes 36868
  57.7 29.5 %copy-start.32 = (s32[6]{0:T(128)S(1)}, s32[6]{0:T(128)}, u32[]{:S(2)}) copy-start(s32[6]{0:T(128)} %param.29) | copy-start | bytes 76
  57.7 0.6 copy-start.26
  57.8 0.6 copy-start.28
  57.8 0.6 copy-start.29
  57.8 0.6 copy-start.30
  58.4 0.6 copy-start.31
  61.6 3.6 %collective-permute-start.10 = (bf16[4,2,32,128]{3,2,1,0:T(8,128)(2,1)}, bf16[4,2,32,128]{3,2,1,0:T(8,128)(2,1)S(1)}, u32[]{:S(2)}, u32[]{:S(2)}) collective-permute-start(bf16[4,2,32,128]{3,2,1,0:T(8,128)(2,1)} %get-tuple-element.99), channel_id=1, source_target_pairs={{0,1},{1,0},{2,3},{3,2},{4,5},{5,4},{6,7},{7,6},{8,9},{9,8},{10,11... | collective-permute-start | bytes 196616 | tf_op jit(solution)/shard_map/ppermute | solution.py:430
  61.6 5.2 %collective-permute-start.11 = (bf16[4,2,32,128]{3,2,1,0:T(8,128)(2,1)}, bf16[4,2,32,128]{3,2,1,0:T(8,128)(2,1)S(1)}, u32[]{:S(2)}, u32[]{:S(2)}) collective-permute-start(bf16[4,2,32,128]{3,2,1,0:T(8,128)(2,1)} %get-tuple-element.100), channel_id=1, source_target_pairs={{0,2},{1,3},{2,0},{3,1},{4,6},{5,7},{6,4},{7,5},{8,10},{9,11},{10,... | collective-permute-start | bytes 196616 | tf_op jit(solution)/shard_map/ppermute | solution.py:430
  62.7 5.2 %collective-permute-start.12 = (bf16[4,2,32,128]{3,2,1,0:T(8,128)(2,1)}, bf16[4,2,32,128]{3,2,1,0:T(8,128)(2,1)S(1)}, u32[]{:S(2)}, u32[]{:S(2)}) collective-permute-start(bf16[4,2,32,128]{3,2,1,0:T(8,128)(2,1)} %get-tuple-element.101), channel_id=1, source_target_pairs={{0,3},{1,2},{2,1},{3,0},{4,7},{5,6},{6,5},{7,4},{8,11},{9,10},{10,... | collective-permute-start | bytes 196616 | tf_op jit(solution)/shard_map/ppermute | solution.py:430
  63.5 9.2 %collective-permute-start.13 = (bf16[4,2,32,128]{3,2,1,0:T(8,128)(2,1)}, bf16[4,2,32,128]{3,2,1,0:T(8,128)(2,1)S(1)}, u32[]{:S(2)}, u32[]{:S(2)}) collective-permute-start(bf16[4,2,32,128]{3,2,1,0:T(8,128)(2,1)} %get-tuple-element.102), channel_id=1, source_target_pairs={{0,4},{1,5},{2,6},{3,7},{4,0},{5,1},{6,2},{7,3},{8,12},{9,13},{10,... | collective-permute-start | bytes 196616 | tf_op jit(solution)/shard_map/ppermute | solution.py:430
  64.9 10.3 %collective-permute-start.14 = (bf16[4,2,32,128]{3,2,1,0:T(8,128)(2,1)}, bf16[4,2,32,128]{3,2,1,0:T(8,128)(2,1)S(1)}, u32[]{:S(2)}, u32[]{:S(2)}) collective-permute-start(bf16[4,2,32,128]{3,2,1,0:T(8,128)(2,1)} %get-tuple-element.103), channel_id=1, source_target_pairs={{0,5},{1,4},{2,7},{3,6},{4,1},{5,0},{6,3},{7,2},{8,13},{9,12},{10,... | collective-permute-start | bytes 196616 | tf_op jit(solution)/shard_map/ppermute | solution.py:430
  65.2 10.0 %copy-start.7 = (bf16[4,2,32,128]{3,2,1,0:T(8,128)(2,1)}, bf16[4,2,32,128]{3,2,1,0:T(8,128)(2,1)S(1)}, u32[]{:S(2)}) copy-start(bf16[4,2,32,128]{3,2,1,0:T(8,128)(2,1)S(1)} %collective-permute-done.10.refs_1_) | copy-start | bytes 196612
  65.2 9.9 %collective-permute-start.15 = (bf16[4,2,32,128]{3,2,1,0:T(8,128)(2,1)}, bf16[4,2,32,128]{3,2,1,0:T(8,128)(2,1)S(1)}, u32[]{:S(2)}, u32[]{:S(2)}) collective-permute-start(bf16[4,2,32,128]{3,2,1,0:T(8,128)(2,1)} %get-tuple-element.104), channel_id=1, source_target_pairs={{0,6},{1,7},{2,4},{3,5},{4,2},{5,3},{6,0},{7,1},{8,14},{9,15},{10,... | collective-permute-start | bytes 196616 | tf_op jit(solution)/shard_map/ppermute | solution.py:430
  66.9 8.3 %copy-start.8 = (bf16[4,2,32,128]{3,2,1,0:T(8,128)(2,1)}, bf16[4,2,32,128]{3,2,1,0:T(8,128)(2,1)S(1)}, u32[]{:S(2)}) copy-start(bf16[4,2,32,128]{3,2,1,0:T(8,128)(2,1)S(1)} %collective-permute-done.11.refs_2_) | copy-start | bytes 196612
  66.9 8.3 %collective-permute-start.16 = (bf16[4,2,32,128]{3,2,1,0:T(8,128)(2,1)}, bf16[4,2,32,128]{3,2,1,0:T(8,128)(2,1)S(1)}, u32[]{:S(2)}, u32[]{:S(2)}) collective-permute-start(bf16[4,2,32,128]{3,2,1,0:T(8,128)(2,1)} %get-tuple-element.105), channel_id=1, source_target_pairs={{0,7},{1,6},{2,5},{3,4},{4,3},{5,2},{6,1},{7,0},{8,15},{9,14},{10,... | collective-permute-start | bytes 196616 | tf_op jit(solution)/shard_map/ppermute | solution.py:430
  67.9 7.3 %copy-start.9 = (bf16[4,2,32,128]{3,2,1,0:T(8,128)(2,1)}, bf16[4,2,32,128]{3,2,1,0:T(8,128)(2,1)S(1)}, u32[]{:S(2)}) copy-start(bf16[4,2,32,128]{3,2,1,0:T(8,128)(2,1)S(1)} %collective-permute-done.12.refs_3_) | copy-start | bytes 196612
  72.7 2.5 %copy-start.10 = (bf16[4,2,32,128]{3,2,1,0:T(8,128)(2,1)}, bf16[4,2,32,128]{3,2,1,0:T(8,128)(2,1)S(1)}, u32[]{:S(2)}) copy-start(bf16[4,2,32,128]{3,2,1,0:T(8,128)(2,1)S(1)} %collective-permute-done.13.refs_4_) | copy-start | bytes 196612
  75.1 0.6 copy-start.11
  75.1 0.6 copy-start.12
  75.1 0.7 copy-start.13
  82.8 14.0 %collective-permute-start.17 = (bf16[2,8,32,128]{3,2,1,0:T(8,128)(2,1)}, bf16[2,8,32,128]{3,2,1,0:T(8,128)(2,1)S(1)}, u32[]{:S(2)}, u32[]{:S(2)}) collective-permute-start(bf16[2,8,32,128]{3,2,1,0:T(8,128)(2,1)} %get-tuple-element.113), channel_id=1, source_target_pairs={{0,8},{8,0},{16,24},{24,16},{1,9},{9,1},{17,25},{25,17},{2,10},{10... | collective-permute-start | bytes 393224 | tf_op jit(solution)/shard_map/ppermute | solution.py:427
  82.8 14.1 %collective-permute-start.18 = (bf16[2,8,32,128]{3,2,1,0:T(8,128)(2,1)}, bf16[2,8,32,128]{3,2,1,0:T(8,128)(2,1)S(1)}, u32[]{:S(2)}, u32[]{:S(2)}) collective-permute-start(bf16[2,8,32,128]{3,2,1,0:T(8,128)(2,1)} %get-tuple-element.114), channel_id=1, source_target_pairs={{0,16},{8,24},{16,0},{24,8},{1,17},{9,25},{17,1},{25,9},{2,18},{10... | collective-permute-start | bytes 393224 | tf_op jit(solution)/shard_map/ppermute | solution.py:427
  84.9 12.6 %collective-permute-start.19 = (bf16[2,8,32,128]{3,2,1,0:T(8,128)(2,1)}, bf16[2,8,32,128]{3,2,1,0:T(8,128)(2,1)}, u32[]{:S(2)}, u32[]{:S(2)}) collective-permute-start(bf16[2,8,32,128]{3,2,1,0:T(8,128)(2,1)} %get-tuple-element.115), channel_id=1, source_target_pairs={{0,24},{8,16},{16,8},{24,0},{1,25},{9,17},{17,9},{25,1},{2,26},{10... | collective-permute-start | bytes 393224 | tf_op jit(solution)/shard_map/ppermute | solution.py:427
  93.0 4.6 %copy-start.2 = (bf16[6,128,4,258]{1,2,3,0:T(4,128)(2,1)S(1)}, bf16[6,128,4,258]{1,2,3,0:T(4,128)(2,1)}, u32[]{:S(2)}) copy-start(bf16[6,128,4,258]{1,2,3,0:T(4,128)(2,1)} %param.21) | copy-start | bytes 4755460
  93.0 64.0 %all-to-all-start.1 = ((bf16[32,2,32,640]{3,2,1,0:T(8,128)(2,1)}), bf16[32,2,32,640]{3,2,1,0:T(8,128)(2,1)}, u32[]{:S(2)}, u32[]{:S(2)}) async-start(bf16[32,2,32,640]{3,2,1,0:T(8,128)(2,1)} %latitudinal_wide.1), calls=%async_computation.1 | async-start | bytes 5242880 | tf_op jit(solution)/shard_map/all_to_all | solution.py:459
  96.9 1.1 copy-start.4
  96.9 0.9 copy-start.21
  96.9 0.6 copy-start.22
  110.2 1.5 copy-start.19
  110.2 2.5 %copy-start.16 = (f32[8,128]{1,0:T(8,128)S(1)}, f32[8,128]{1,0:T(8,128)}, u32[]{:S(2)}) copy-start(f32[8,128]{1,0:T(8,128)} %param.24) | copy-start | bytes 12292
  110.2 2.6 %copy-start.18 = (bf16[8,128]{1,0:T(8,128)(2,1)S(1)}, bf16[8,128]{1,0:T(8,128)(2,1)}, u32[]{:S(2)}) copy-start(bf16[8,128]{1,0:T(8,128)(2,1)} %param.23) | copy-start | bytes 6148
  110.2 2.6 %copy-start.20 = (f32[128]{0:T(128)S(1)}, f32[128]{0:T(128)}, u32[]{:S(2)}) copy-start(f32[128]{0:T(128)} %param.25) | copy-start | bytes 1540
  119.6 10.7 %copy-start.17 = (f32[768]{0:T(1024)S(1)}, f32[768]{0:T(1024)}, u32[]{:S(2)}) copy-start(f32[768]{0:T(1024)} %param.20) | copy-start | bytes 9220

commit v3 on v2

--- a/solution.py
+++ b/solution.py
@@ -80,8 +80,8 @@
     return fresh.astype(jnp.bfloat16)
 
 
-def compiler_params():
-    return pltpu.CompilerParams(vmem_limit_bytes=60 * MIB)
+def compiler_params(mib=60):
+    return pltpu.CompilerParams(vmem_limit_bytes=mib * MIB)
 
 
 def cost(flops, *arrays):
@@ -167,18 +167,21 @@
     modes, degrees, lats = matrix.shape
 
     def body(x_ref, matrix_ref, damping_ref, out_ref):
+        parity = pl.program_id(0)
         for span in lane_spans(width):
-            by_coeff = jnp.swapaxes(x_ref[:, :, :, span].reshape(lats, rows, -1), 0, 1)
+            by_coeff = jnp.swapaxes(x_ref[:, :, :, span].reshape(lats, GROUP, -1), 0, 1)
             results = [
-                damp(matrix_ref[wavenumber_at(row)], by_coeff[row], damping_ref[:, span]) for row in range(rows)
+                damp(matrix_ref[wavenumber_at(row) + parity], by_coeff[row], damping_ref[:, span])
+                for row in range(GROUP)
             ]
-            out_ref[:, :, :, span] = jnp.swapaxes(jnp.stack(results), 0, 1).reshape(devices, lines, rows, -1)
-
-    return pl.pallas_call(
-        body,
-        grid=(1,),
-        in_specs=[whole(coeffs), whole(matrix), pl.BlockSpec((degrees, width), lambda i: (0, 0))],
-        out_specs=whole(coeffs),
+            out_ref[:, :, :, span] = jnp.swapaxes(jnp.stack(results), 0, 1).reshape(devices, lines, GROUP, -1)
+
+    half_rows = pl.BlockSpec((devices, lines, GROUP, width), lambda p: (0, 0, p, 0))
+    return pl.pallas_call(
+        body,
+        grid=(rows // GROUP,),
+        in_specs=[half_rows, whole(matrix), pl.BlockSpec((degrees, width), lambda p: (0, 0))],
+        out_specs=half_rows,
         out_shape=jax.ShapeDtypeStruct(coeffs.shape, jnp.bfloat16),
         compiler_params=compiler_params(),
         cost_estimate=cost(4 * rows * degrees * lats * width, coeffs, coeffs, matrix),

time: 163 us -> 163 us (level)
  no operation moved by 1% of the time
where the time goes in v3:
time: 163 us; the launch traced here: 162 us
  waiting for transfers between devices  45 us (28%)
  starting transfers between devices  33.4 us (20%)
  Pallas kernels  30 us (18%)
  matrix products  22.9 us (14%)
  blocking collectives  21.3 us (13%)
  local copies, waits for them, and re-layouts  7.92 us (5%)
    all_to_all x2, waiting for transfers between devices, shards(): lax.all_to_all(wide_coeffs, AXES, split_axis=0, concat_axis=0, tiled=True)  26.9 us
    ppermute x14, waiting for transfers between devices, over_plane(): lax.ppermute(x, ('band', 'ch'), twists[p])  18.1 us
    dot_general x9, matrix products, ocean_update(): jnp.einsum('io,sirw->sorw', kernel_coefficients[shift_row, shift_col], wi...  13.8 us
    ppermute x14, starting transfers between devices, over_plane(): lax.ppermute(x, ('band', 'ch'), twists[p])  13.4 us
    all_gather x1, blocking collectives, gather_flux(): return lax.all_gather(flux_local, 'band', axis=1, tiled=True)  13 us
    all_to_all x2, starting transfers between devices, shards(): lax.all_to_all(wide_coeffs, AXES, split_axis=0, concat_axis=0, tiled=True)  10 us
    ppermute x6, starting transfers between devices, over_sections(): lax.ppermute(x, 'sec', hops[o])  10 us
    all_gather x1, blocking collectives, shards(): sea_all = lax.all_gather(sea_slots, 'band', axis=0, tiled=True)  8.32 us
  transfers between devices with their start and end apart: 22, of which 5 were waited for; matrix products, arithmetic and copies ran while one was open for 17% of the time, Pallas kernels for 13%

profile of v3, /device:TPU:0, one launch (start us, length us, event | category | flops | bytes accessed | tf_op | source)
XLA Modules:
  0.0 162.1 jit_solution(15425281065129639777)
XLA Ops:
  0.7 3.1 %analyse_slim.1 = (bf16[2,8,32,128]{3,2,1,0:T(8,128)(2,1)}, bf16[2,8,32,128]{3,2,1,0:T(8,128)(2,1)}, bf16[2,8,32,128]{3,2,1,0:T(8,128)(2,1)}, bf16[2,8,32,128]{3,2,1,0:T(8,128)(2,1)}) custom-call(s32[1]{0:T(128)} %bitcast.sec_ref, bf16[1024,1024]{1,0:T(8,128)(2,1)} %constant.153.clone.table_ref, bf16[2,1024,768]{2,1,0:T(8,128)(2,1)} %air_ref.2), custom_call_target="tpu_custom_call" | custom-call | flops 536870912 | bytes 3145728 | tf_op jit(solution)/shard_map/analyse_slim/pallas_call | solution.py:138
  3.7 3.0 %collective-permute-start = (bf16[2,8,32,128]{3,2,1,0:T(8,128)(2,1)}, bf16[2,8,32,128]{3,2,1,0:T(8,128)(2,1)S(1)}, u32[]{:S(2)}, u32[]{:S(2)}) collective-permute-start(bf16[2,8,32,128]{3,2,1,0:T(8,128)(2,1)} %get-tuple-element.69), channel_id=1, source_target_pairs={{0,8},{8,0},{16,24},{24,16},{1,9},{9,1},{17,25},{25,17},{2,10},{10... | collective-permute-start | bytes 393224 | tf_op jit(solution)/shard_map/ppermute | solution.py:430
  6.8 2.6 %collective-permute-start.1 = (bf16[2,8,32,128]{3,2,1,0:T(8,128)(2,1)}, bf16[2,8,32,128]{3,2,1,0:T(8,128)(2,1)S(1)}, u32[]{:S(2)}, u32[]{:S(2)}) collective-permute-start(bf16[2,8,32,128]{3,2,1,0:T(8,128)(2,1)} %get-tuple-element.70), channel_id=1, source_target_pairs={{0,16},{8,24},{16,0},{24,8},{1,17},{9,25},{17,1},{25,9},{2,18},{10... | collective-permute-start | bytes 393224 | tf_op jit(solution)/shard_map/ppermute | solution.py:430
  9.3 6.7 %analyse_wide.1 = bf16[32,2,32,640]{3,2,1,0:T(8,128)(2,1)} custom-call(bf16[1024,1024]{1,0:T(8,128)(2,1)} %constant.153.clone.table_ref, bf16[2,1024,768]{2,1,0:T(8,128)(2,1)} %air_ref.2), custom_call_target="tpu_custom_call" | custom-call | flops 2684354560 | bytes 7864320 | tf_op jit(solution)/shard_map/analyse_wide/pallas_call | solution.py:107
  16.0 6.2 %all-to-all-start = ((bf16[32,2,32,640]{3,2,1,0:T(8,128)(2,1)}), bf16[32,2,32,640]{3,2,1,0:T(8,128)(2,1)}, u32[]{:S(2)}, u32[]{:S(2)}) async-start(bf16[32,2,32,640]{3,2,1,0:T(8,128)(2,1)} %analyse_wide.1), calls=%async_computation | async-start | bytes 5242880 | tf_op jit(solution)/shard_map/all_to_all | solution.py:439
  22.3 0.6 copy-done.5
  23.0 1.9 %to_plane.1 = (bf16[4,2,32,128]{3,2,1,0:T(8,128)(2,1)}, bf16[4,2,32,128]{3,2,1,0:T(8,128)(2,1)}, bf16[4,2,32,128]{3,2,1,0:T(8,128)(2,1)}, bf16[4,2,32,128]{3,2,1...) custom-call(s32[1]{0:T(128)} %bitcast.1.place_ref, ...), custom_call_target="tpu_custom_call" | custom-call | bytes 1048576 | tf_op jit(solution)/shard_map/to_plane/pallas_call | solution.py:207
  24.9 0.3 collective-permute-start.3
  25.1 1.7 %collective-permute-start.4 = (bf16[4,2,32,128]{3,2,1,0:T(8,128)(2,1)}, bf16[4,2,32,128]{3,2,1,0:T(8,128)(2,1)S(1)}, u32[]{:S(2)}, u32[]{:S(2)}) collective-permute-start(bf16[4,2,32,128]{3,2,1,0:T(8,128)(2,1)} %get-tuple-element.84), channel_id=1, source_target_pairs={{0,2},{1,3},{2,0},{3,1},{4,6},{5,7},{6,4},{7,5},{8,10},{9,11},{10,... | collective-permute-start | bytes 196616 | tf_op jit(solution)/shard_map/ppermute | solution.py:433
  26.8 1.7 %collective-permute-start.6 = (bf16[4,2,32,128]{3,2,1,0:T(8,128)(2,1)}, bf16[4,2,32,128]{3,2,1,0:T(8,128)(2,1)S(1)}, u32[]{:S(2)}, u32[]{:S(2)}) collective-permute-start(bf16[4,2,32,128]{3,2,1,0:T(8,128)(2,1)} %get-tuple-element.86), channel_id=1, source_target_pairs={{0,4},{1,5},{2,6},{3,7},{4,0},{5,1},{6,2},{7,3},{8,12},{9,13},{10,... | collective-permute-start | bytes 196616 | tf_op jit(solution)/shard_map/ppermute | solution.py:433
  28.5 0.1 collective-permute-start.7
  28.6 0.9 fusion.12
  29.6 2.6 %collective-permute-start.8 = (bf16[4,2,32,128]{3,2,1,0:T(8,128)(2,1)S(1)}, bf16[4,2,32,128]{3,2,1,0:T(8,128)(2,1)S(1)}, u32[]{:S(2)}, u32[]{:S(2)}) collective-permute-start(bf16[4,2,32,128]{3,2,1,0:T(8,128)(2,1)S(1)} %copy-done.27), channel_id=1, source_target_pairs={{0,6},{1,7},{2,4},{3,5},{4,2},{5,3},{6,0},{7,1},{8,14},{9,15},{10,... | collective-permute-start | bytes 196616 | tf_op jit(solution)/shard_map/ppermute | solution.py:433
  32.2 10.9 %collective-permute-done.4.refs_2_ = bf16[4,2,32,128]{3,2,1,0:T(8,128)(2,1)S(1)} collective-permute-done((bf16[4,2,32,128]{3,2,1,0:T(8,128)(2,1)}, bf16[4,2,32,128]{3,2,1,0:T(8,128)(2,1)S(1)}, u32[]{:S(2)}, u32[]{:S(2)}) %collective-permute-start.4) | collective-permute-done | bytes 65568 | tf_op jit(solution)/shard_map/ppermute | solution.py:433
  43.1 0.7 collective-permute-start.9
  43.8 0.9 convolution_convert_fusion.matrix_ref
  44.8 13.0 %all_gather.6 = bf16[8,8,1024]{2,0,1:T(8,128)(2,1)S(1)} all-gather(bf16[8,2,1024]{2,0,1:T(8,128)(2,1)S(1)} %fusion.12), channel_id=1, replica_groups=mesh['sec'=4,'band'=4,'ch'=2] {'band'}, dimensions={1}, use_global_device_ids=true | all-gather | bytes 163840 | tf_op jit(solution)/shard_map/all_gather | solution.py:382
  57.8 0.5 copy-done.26
  58.4 0.6 copy-done.31
  59.1 2.6 %latitudinal_slim.1 = (bf16[4,2,32,128]{3,2,1,0:T(8,128)(2,1)}, bf16[4,2,32,128]{3,2,1,0:T(8,128)(2,1)}, bf16[4,2,32,128]{3,2,1,0:T(8,128)(2,1)}, bf16[4,2,32,12...) custom-call(bf16[16,64,64]{2,1,0:T(8,128)(2,1)} %convolution_convert, ...), custom_call_target="tpu_custom_call" | custom-call | flops 99999997952 | bytes 300000000 | tf_op jit(solution)/shard_map/latitudinal_slim/pallas_call | solution.py:259
  61.6 1.1 collective-permute-start.11
  62.7 0.8 collective-permute-start.12
  63.5 1.4 collective-permute-start.13
  64.9 0.3 collective-permute-start.14
  65.2 1.7 %collective-permute-start.15 = (bf16[4,2,32,128]{3,2,1,0:T(8,128)(2,1)}, bf16[4,2,32,128]{3,2,1,0:T(8,128)(2,1)S(1)}, u32[]{:S(2)}, u32[]{:S(2)}) collective-permute-start(bf16[4,2,32,128]{3,2,1,0:T(8,128)(2,1)} %get-tuple-element.104), channel_id=1, source_target_pairs={{0,6},{1,7},{2,4},{3,5},{4,2},{5,3},{6,0},{7,1},{8,14},{9,15},{10,... | collective-permute-start | bytes 196616 | tf_op jit(solution)/shard_map/ppermute | solution.py:433
  66.9 1.0 collective-permute-start.16
  67.9 4.8 %collective-permute-done.13.refs_4_ = bf16[4,2,32,128]{3,2,1,0:T(8,128)(2,1)S(1)} collective-permute-done((bf16[4,2,32,128]{3,2,1,0:T(8,128)(2,1)}, bf16[4,2,32,128]{3,2,1,0:T(8,128)(2,1)S(1)}, u32[]{:S(2)}, u32[]{:S(2)}) %collective-permute-start.13) | collective-permute-done | bytes 65568 | tf_op jit(solution)/shard_map/ppermute | solution.py:433
  72.7 2.4 %collective-permute-done.14.refs_5_ = bf16[4,2,32,128]{3,2,1,0:T(8,128)(2,1)S(1)} collective-permute-done((bf16[4,2,32,128]{3,2,1,0:T(8,128)(2,1)}, bf16[4,2,32,128]{3,2,1,0:T(8,128)(2,1)S(1)}, u32[]{:S(2)}, u32[]{:S(2)}) %collective-permute-start.14) | collective-permute-done | bytes 65568 | tf_op jit(solution)/shard_map/ppermute | solution.py:433
  75.2 0.5 copy-done.11
  75.8 1.9 %from_plane.1 = (bf16[2,8,32,128]{3,2,1,0:T(8,128)(2,1)}, bf16[2,8,32,128]{3,2,1,0:T(8,128)(2,1)}, bf16[2,8,32,128]{3,2,1,0:T(8,128)(2,1)}, bf16[2,8,32,128]{3,2,1,0:T(8,128)(2,1)}) custom-call(s32[1]{0:T(128)} %bitcast.1.place_ref, bf16[4,2,32,128]{3,2,1,0:T(8,128)(2,1)} %get-tuple-element.98.refs_0_, bf16[4,2,32,128]{3,2,1,0:T(8,128)(2,1)} %copy-done.7, ...), custom_call_target="tpu_custom_call" | custom-call | bytes 1048576 | tf_op jit(solution)/shard_map/from_plane/pallas_call | solution.py:230
  77.7 5.1 %all-to-all-done.x_ref = bf16[32,2,32,640]{3,2,1,0:T(8,128)(2,1)} async-done(((bf16[32,2,32,640]{3,2,1,0:T(8,128)(2,1)}), bf16[32,2,32,640]{3,2,1,0:T(8,128)(2,1)}, u32[]{:S(2)}, u32[]{:S(2)}) %all-to-all-start) | async-done | bytes 2621472 | tf_op jit(solution)/shard_map/all_to_all | solution.py:439
  82.8 2.1 %collective-permute-start.18 = (bf16[2,8,32,128]{3,2,1,0:T(8,128)(2,1)}, bf16[2,8,32,128]{3,2,1,0:T(8,128)(2,1)S(1)}, u32[]{:S(2)}, u32[]{:S(2)}) collective-permute-start(bf16[2,8,32,128]{3,2,1,0:T(8,128)(2,1)} %get-tuple-element.114), channel_id=1, source_target_pairs={{0,16},{8,24},{16,0},{24,8},{1,17},{9,25},{17,1},{25,9},{2,18},{10... | collective-permute-start | bytes 393224 | tf_op jit(solution)/shard_map/ppermute | solution.py:430
  84.9 2.3 %collective-permute-start.19 = (bf16[2,8,32,128]{3,2,1,0:T(8,128)(2,1)}, bf16[2,8,32,128]{3,2,1,0:T(8,128)(2,1)}, u32[]{:S(2)}, u32[]{:S(2)}) collective-permute-start(bf16[2,8,32,128]{3,2,1,0:T(8,128)(2,1)} %get-tuple-element.115), channel_id=1, source_target_pairs={{0,24},{8,16},{16,8},{24,0},{1,25},{9,17},{17,9},{25,1},{2,26},{10... | collective-permute-start | bytes 393224 | tf_op jit(solution)/shard_map/ppermute | solution.py:430
  87.3 5.1 %latitudinal_wide.1 = bf16[32,2,32,640]{3,2,1,0:T(8,128)(2,1)} custom-call(bf16[32,2,32,640]{3,2,1,0:T(8,128)(2,1)} %all-to-all-done.x_ref, bf16[16,64,64]{2,1,0:T(8,128)(2,1)} %matrix_ref.1, f32[64,768]{1,0:T(8,128)} %damping_ref.3), custom_call_target="tpu_custom_call" | custom-call | flops 335544320 | bytes 5373952 | tf_op jit(solution)/shard_map/latitudinal_wide/pallas_call | solution.py:180
  92.3 3.9 %all-to-all-start.1 = ((bf16[32,2,32,640]{3,2,1,0:T(8,128)(2,1)}), bf16[32,2,32,640]{3,2,1,0:T(8,128)(2,1)}, u32[]{:S(2)}, u32[]{:S(2)}) async-start(bf16[32,2,32,640]{3,2,1,0:T(8,128)(2,1)} %latitudinal_wide.1), calls=%async_computation.1 | async-start | bytes 5242880 | tf_op jit(solution)/shard_map/all_to_all | solution.py:462
  96.3 0.6 copy-done.22
  96.9 0.2 copy.75
  97.1 0.1 copy-done.4
  97.3 1.5 fusion.14
  98.8 1.6 fusion.16
  100.3 1.6 fusion.18
  101.9 1.5 fusion.20
  103.4 1.5 fusion.36
  104.9 1.6 fusion.22
  106.5 1.5 fusion.24
  108.0 1.5 fusion.26
  109.5 1.5 fusion.28
  111.0 0.1 copy.76
  111.2 0.1 eq.64
  111.3 0.2 reduce_window_sum.11
  111.5 0.1 fusion.66
  111.6 0.3 convert_reduce_fusion
  111.9 0.1 copy.88
  112.0 0.1 multiply_reduce_fusion
  112.1 6.8 %fusion.9 = bf16[6,128,2,256]{1,3,2,0:T(8,128)(2,1)S(1)} fusion(f32[6,2,256,128]{3,2,1,0:T(8,128)} %fusion.14, f32[6,2,256,128]{3,2,1,0:T(8,128)} %fusion.16, f32[6,2,256,128]{3,2,1,0:T(8,128)} %fusion.18, f32[6,2,256,128]{3,2,1,0:T(8,128)} %fusion.20, f32[6,2,256,128]{3,2,1,0:T(8,128)} %fusion.36, f32[6,2,256,128]{3,2,1,0:T(8,128)} %fusion.22, ...), kind=kOutput, calls=%fused_computation.11 | convolution fusion | flops 116391936 | bytes 15828480 | tf_op jit(solution)/shard_map/io,sirw->sorw/dot_general | solution.py:74
  118.9 1.8 %copy.94 = bf16[6,128,2,256]{3,2,1,0:T(2,128)(2,1)} copy(bf16[6,128,2,256]{1,3,2,0:T(8,128)(2,1)S(1)} %fusion.9) | data formatting | bytes 1572864
  120.7 0.3 copy.92
  121.0 8.3 %all-gather = bf16[24,1,2,256]{3,2,1,0:T(2,128)(2,1)S(1)} all-gather(bf16[6,1,2,256]{3,2,1,0:T(2,128)(2,1)S(1)} %copy.92), channel_id=2, replica_groups=mesh['sec'=4,'band'=4,'ch'=2] {'band'}, dimensions={0}, use_global_device_ids=true | all-gather | bytes 30720 | tf_op jit(solution)/shard_map/all_gather | solution.py:518
  129.4 0.2 fusion.13
  129.7 1.2 stack.27.warmth_ref
  130.9 0.6 broadcast_in_dim.9.sea_ref
  131.6 3.0 %synthesise_slim.1.begun_ref = bf16[2,2,512,768]{3,2,1,0:T(8,128)(2,1)} custom-call(s32[1]{0:T(128)} %bitcast.sec_ref, bf16[2,512,512]{2,1,0:T(8,128)(2,1)} %constant.154.clone.table_ref, bf16[2,2,512,768]{3,2,1,0:T(8,128)(2,1)} %bitcast.124, bf16[2,2,16,512]{3,2,1,0:T(8,128)(2,1)} %broadcast_in_dim.9.sea_ref, bf16[16,768]{1,0:T(8,128)(2,1)} %stack.27.warmth_ref, ...), custom_call_target="tpu_custom_call" | custom-call | flops 99999997952 | bytes 300000000 | tf_op jit(solution)/shard_map/synthesise_slim/pallas_call | solution.py:316
  134.6 21.8 %all-to-all-done.1.coeff_ref = bf16[32,2,32,640]{3,2,1,0:T(8,128)(2,1)} async-done(((bf16[32,2,32,640]{3,2,1,0:T(8,128)(2,1)}), bf16[32,2,32,640]{3,2,1,0:T(8,128)(2,1)}, u32[]{:S(2)}, u32[]{:S(2)}) %all-to-all-start.1) | async-done | bytes 2621472 | tf_op jit(solution)/shard_map/all_to_all | solution.py:462
  156.3 5.8 %synthesise_wide.1 = bf16[2,2,512,768]{3,2,1,0:T(8,128)(2,1)} custom-call(bf16[2,512,512]{2,1,0:T(8,128)(2,1)} %constant.154.clone.table_ref, bf16[32,2,32,640]{3,2,1,0:T(8,128)(2,1)} %all-to-all-done.1.coeff_ref, bf16[2,2,512,768]{3,2,1,0:T(8,128)(2,1)} %bitcast.125, ...), custom_call_target="tpu_custom_call", output_to_operand_aliasing={{}: (5, {})} | custom-call | flops 1342177280 | bytes 8912896 | tf_op jit(solution)/shard_map/synthesise_wide/pallas_call | solution.py:355
  (100 shorter events, 0.7 us)
Async XLA Ops:
  0.6 111.5 %copy-start = (bf16[128,128]{1,0:T(8,128)(2,1)S(1)}, bf16[128,128]{1,0:T(8,128)(2,1)}, u32[]{:S(2)}) copy-start(bf16[128,128]{1,0:T(8,128)(2,1)} %param.26) | copy-start | bytes 98308
  3.7 18.5 %collective-permute-start = (bf16[2,8,32,128]{3,2,1,0:T(8,128)(2,1)}, bf16[2,8,32,128]{3,2,1,0:T(8,128)(2,1)S(1)}, u32[]{:S(2)}, u32[]{:S(2)}) collective-permute-start(bf16[2,8,32,128]{3,2,1,0:T(8,128)(2,1)} %get-tuple-element.69), channel_id=1, source_target_pairs={{0,8},{8,0},{16,24},{24,16},{1,9},{9,1},{17,25},{25,17},{2,10},{10... | collective-permute-start | bytes 393224 | tf_op jit(solution)/shard_map/ppermute | solution.py:430
  6.8 15.5 %collective-permute-start.1 = (bf16[2,8,32,128]{3,2,1,0:T(8,128)(2,1)}, bf16[2,8,32,128]{3,2,1,0:T(8,128)(2,1)S(1)}, u32[]{:S(2)}, u32[]{:S(2)}) collective-permute-start(bf16[2,8,32,128]{3,2,1,0:T(8,128)(2,1)} %get-tuple-element.70), channel_id=1, source_target_pairs={{0,16},{8,24},{16,0},{24,8},{1,17},{9,25},{17,1},{25,9},{2,18},{10... | collective-permute-start | bytes 393224 | tf_op jit(solution)/shard_map/ppermute | solution.py:430
  9.3 12.9 %collective-permute-start.2 = (bf16[2,8,32,128]{3,2,1,0:T(8,128)(2,1)}, bf16[2,8,32,128]{3,2,1,0:T(8,128)(2,1)}, u32[]{:S(2)}, u32[]{:S(2)}) collective-permute-start(bf16[2,8,32,128]{3,2,1,0:T(8,128)(2,1)} %get-tuple-element.71), channel_id=1, source_target_pairs={{0,24},{8,16},{16,8},{24,0},{1,25},{9,17},{17,9},{25,1},{2,26},{10... | collective-permute-start | bytes 393224 | tf_op jit(solution)/shard_map/ppermute | solution.py:430
  16.0 12.6 %copy-start.1 = (bf16[2,1024,768]{2,1,0:T(8,128)(2,1)S(1)}, bf16[2,1024,768]{2,1,0:T(8,128)(2,1)}, u32[]{:S(2)}) copy-start(bf16[2,1024,768]{2,1,0:T(8,128)(2,1)} %air_ref.2) | copy-start | bytes 9437188
  16.0 12.6 %copy-start.14 = (bf16[768,8]{0,1:T(8,128)(2,1)S(1)}, bf16[768,8]{0,1:T(8,128)(2,1)}, u32[]{:S(2)}) copy-start(bf16[768,8]{0,1:T(8,128)(2,1)} %param.19) | copy-start | bytes 36868
  16.0 66.8 %all-to-all-start = ((bf16[32,2,32,640]{3,2,1,0:T(8,128)(2,1)}), bf16[32,2,32,640]{3,2,1,0:T(8,128)(2,1)}, u32[]{:S(2)}, u32[]{:S(2)}) async-start(bf16[32,2,32,640]{3,2,1,0:T(8,128)(2,1)} %analyse_wide.1), calls=%async_computation | async-start | bytes 5242880 | tf_op jit(solution)/shard_map/all_to_all | solution.py:439
  22.2 0.6 copy-start.5
  22.3 0.7 copy-start.6
  24.9 4.7 %copy-start.27 = (bf16[4,2,32,128]{3,2,1,0:T(8,128)(2,1)S(1)}, bf16[4,2,32,128]{3,2,1,0:T(8,128)(2,1)}, u32[]{:S(2)}) copy-start(bf16[4,2,32,128]{3,2,1,0:T(8,128)(2,1)} %get-tuple-element.88) | copy-start | bytes 196612
  24.9 18.2 %copy-start.25 = (bf16[4,2,32,128]{3,2,1,0:T(8,128)(2,1)S(1)}, bf16[4,2,32,128]{3,2,1,0:T(8,128)(2,1)}, u32[]{:S(2)}) copy-start(bf16[4,2,32,128]{3,2,1,0:T(8,128)(2,1)} %get-tuple-element.89) | copy-start | bytes 196612
  24.9 19.0 %copy-start.3 = (bf16[16,64,64]{2,1,0:T(8,128)(2,1)S(1)}, bf16[16,64,64]{2,1,0:T(8,128)(2,1)}, u32[]{:S(2)}) copy-start(bf16[16,64,64]{2,1,0:T(8,128)(2,1)} %matrix_ref.1) | copy-start | bytes 393220
  24.9 4.7 %collective-permute-start.3 = (bf16[4,2,32,128]{3,2,1,0:T(8,128)(2,1)}, bf16[4,2,32,128]{3,2,1,0:T(8,128)(2,1)S(1)}, u32[]{:S(2)}, u32[]{:S(2)}) collective-permute-start(bf16[4,2,32,128]{3,2,1,0:T(8,128)(2,1)} %get-tuple-element.83), channel_id=1, source_target_pairs={{0,1},{1,0},{2,3},{3,2},{4,5},{5,4},{6,7},{7,6},{8,9},{9,8},{10,11... | collective-permute-start | bytes 196616 | tf_op jit(solution)/shard_map/ppermute | solution.py:433
  25.1 18.0 %collective-permute-start.4 = (bf16[4,2,32,128]{3,2,1,0:T(8,128)(2,1)}, bf16[4,2,32,128]{3,2,1,0:T(8,128)(2,1)S(1)}, u32[]{:S(2)}, u32[]{:S(2)}) collective-permute-start(bf16[4,2,32,128]{3,2,1,0:T(8,128)(2,1)} %get-tuple-element.84), channel_id=1, source_target_pairs={{0,2},{1,3},{2,0},{3,1},{4,6},{5,7},{6,4},{7,5},{8,10},{9,11},{10,... | collective-permute-start | bytes 196616 | tf_op jit(solution)/shard_map/ppermute | solution.py:433
  26.8 30.9 %collective-permute-start.5 = (bf16[4,2,32,128]{3,2,1,0:T(8,128)(2,1)}, bf16[4,2,32,128]{3,2,1,0:T(8,128)(2,1)S(1)}, u32[]{:S(2)}, u32[]{:S(2)}) collective-permute-start(bf16[4,2,32,128]{3,2,1,0:T(8,128)(2,1)} %get-tuple-element.85), channel_id=1, source_target_pairs={{0,3},{1,2},{2,1},{3,0},{4,7},{5,6},{6,5},{7,4},{8,11},{9,10},{10,... | collective-permute-start | bytes 196616 | tf_op jit(solution)/shard_map/ppermute | solution.py:433
  26.8 30.9 %collective-permute-start.6 = (bf16[4,2,32,128]{3,2,1,0:T(8,128)(2,1)}, bf16[4,2,32,128]{3,2,1,0:T(8,128)(2,1)S(1)}, u32[]{:S(2)}, u32[]{:S(2)}) collective-permute-start(bf16[4,2,32,128]{3,2,1,0:T(8,128)(2,1)} %get-tuple-element.86), channel_id=1, source_target_pairs={{0,4},{1,5},{2,6},{3,7},{4,0},{5,1},{6,2},{7,3},{8,12},{9,13},{10,... | collective-permute-start | bytes 196616 | tf_op jit(solution)/shard_map/ppermute | solution.py:433
  28.5 29.3 %collective-permute-start.7 = (bf16[4,2,32,128]{3,2,1,0:T(8,128)(2,1)}, bf16[4,2,32,128]{3,2,1,0:T(8,128)(2,1)S(1)}, u32[]{:S(2)}, u32[]{:S(2)}) collective-permute-start(bf16[4,2,32,128]{3,2,1,0:T(8,128)(2,1)} %get-tuple-element.87), channel_id=1, source_target_pairs={{0,5},{1,4},{2,7},{3,6},{4,1},{5,0},{6,3},{7,2},{8,13},{9,12},{10,... | collective-permute-start | bytes 196616 | tf_op jit(solution)/shard_map/ppermute | solution.py:433
  29.6 28.3 %copy-start.23 = (bf16[4,2,32,128]{3,2,1,0:T(8,128)(2,1)}, bf16[4,2,32,128]{3,2,1,0:T(8,128)(2,1)S(1)}, u32[]{:S(2)}) copy-start(bf16[4,2,32,128]{3,2,1,0:T(8,128)(2,1)S(1)} %collective-permute-done.3.refs_1_) | copy-start | bytes 196612
  29.6 28.2 %collective-permute-start.8 = (bf16[4,2,32,128]{3,2,1,0:T(8,128)(2,1)S(1)}, bf16[4,2,32,128]{3,2,1,0:T(8,128)(2,1)S(1)}, u32[]{:S(2)}, u32[]{:S(2)}) collective-permute-start(bf16[4,2,32,128]{3,2,1,0:T(8,128)(2,1)S(1)} %copy-done.27), channel_id=1, source_target_pairs={{0,6},{1,7},{2,4},{3,5},{4,2},{5,3},{6,0},{7,1},{8,14},{9,15},{10,... | collective-permute-start | bytes 196616 | tf_op jit(solution)/shard_map/ppermute | solution.py:433
  43.1 14.7 %copy-start.24 = (bf16[4,2,32,128]{3,2,1,0:T(8,128)(2,1)}, bf16[4,2,32,128]{3,2,1,0:T(8,128)(2,1)S(1)}, u32[]{:S(2)}) copy-start(bf16[4,2,32,128]{3,2,1,0:T(8,128)(2,1)S(1)} %collective-permute-done.4.refs_2_) | copy-start | bytes 196612
  43.1 14.7 %collective-permute-start.9 = (bf16[4,2,32,128]{3,2,1,0:T(8,128)(2,1)S(1)}, bf16[4,2,32,128]{3,2,1,0:T(8,128)(2,1)S(1)}, u32[]{:S(2)}, u32[]{:S(2)}) collective-permute-start(bf16[4,2,32,128]{3,2,1,0:T(8,128)(2,1)S(1)} %copy-done.25), channel_id=1, source_target_pairs={{0,7},{1,6},{2,5},{3,4},{4,3},{5,2},{6,1},{7,0},{8,15},{9,14},{10,... | collective-permute-start | bytes 196616 | tf_op jit(solution)/shard_map/ppermute | solution.py:433
  57.7 10.2 %copy-start.15 = (s32[6,2,256]{2,1,0:T(2,128)S(1)}, s32[6,2,256]{2,1,0:T(2,128)}, u32[]{:S(2)}) copy-start(s32[6,2,256]{2,1,0:T(2,128)} %param.28) | copy-start | bytes 36868
  57.7 29.5 %copy-start.32 = (s32[6]{0:T(128)S(1)}, s32[6]{0:T(128)}, u32[]{:S(2)}) copy-start(s32[6]{0:T(128)} %param.29) | copy-start | bytes 76
  57.7 0.6 copy-start.26
  57.8 0.6 copy-start.28
  57.8 0.6 copy-start.29
  57.8 0.6 copy-start.30
  58.4 0.6 copy-start.31
  61.6 3.6 %collective-permute-start.10 = (bf16[4,2,32,128]{3,2,1,0:T(8,128)(2,1)}, bf16[4,2,32,128]{3,2,1,0:T(8,128)(2,1)S(1)}, u32[]{:S(2)}, u32[]{:S(2)}) collective-permute-start(bf16[4,2,32,128]{3,2,1,0:T(8,128)(2,1)} %get-tuple-element.99), channel_id=1, source_target_pairs={{0,1},{1,0},{2,3},{3,2},{4,5},{5,4},{6,7},{7,6},{8,9},{9,8},{10,11... | collective-permute-start | bytes 196616 | tf_op jit(solution)/shard_map/ppermute | solution.py:433
  61.6 5.2 %collective-permute-start.11 = (bf16[4,2,32,128]{3,2,1,0:T(8,128)(2,1)}, bf16[4,2,32,128]{3,2,1,0:T(8,128)(2,1)S(1)}, u32[]{:S(2)}, u32[]{:S(2)}) collective-permute-start(bf16[4,2,32,128]{3,2,1,0:T(8,128)(2,1)} %get-tuple-element.100), channel_id=1, source_target_pairs={{0,2},{1,3},{2,0},{3,1},{4,6},{5,7},{6,4},{7,5},{8,10},{9,11},{10,... | collective-permute-start | bytes 196616 | tf_op jit(solution)/shard_map/ppermute | solution.py:433
  62.7 5.2 %collective-permute-start.12 = (bf16[4,2,32,128]{3,2,1,0:T(8,128)(2,1)}, bf16[4,2,32,128]{3,2,1,0:T(8,128)(2,1)S(1)}, u32[]{:S(2)}, u32[]{:S(2)}) collective-permute-start(bf16[4,2,32,128]{3,2,1,0:T(8,128)(2,1)} %get-tuple-element.101), channel_id=1, source_target_pairs={{0,3},{1,2},{2,1},{3,0},{4,7},{5,6},{6,5},{7,4},{8,11},{9,10},{10,... | collective-permute-start | bytes 196616 | tf_op jit(solution)/shard_map/ppermute | solution.py:433
  63.5 9.2 %collective-permute-start.13 = (bf16[4,2,32,128]{3,2,1,0:T(8,128)(2,1)}, bf16[4,2,32,128]{3,2,1,0:T(8,128)(2,1)S(1)}, u32[]{:S(2)}, u32[]{:S(2)}) collective-permute-start(bf16[4,2,32,128]{3,2,1,0:T(8,128)(2,1)} %get-tuple-element.102), channel_id=1, source_target_pairs={{0,4},{1,5},{2,6},{3,7},{4,0},{5,1},{6,2},{7,3},{8,12},{9,13},{10,... | collective-permute-start | bytes 196616 | tf_op jit(solution)/shard_map/ppermute | solution.py:433
  64.9 10.3 %collective-permute-start.14 = (bf16[4,2,32,128]{3,2,1,0:T(8,128)(2,1)}, bf16[4,2,32,128]{3,2,1,0:T(8,128)(2,1)S(1)}, u32[]{:S(2)}, u32[]{:S(2)}) collective-permute-start(bf16[4,2,32,128]{3,2,1,0:T(8,128)(2,1)} %get-tuple-element.103), channel_id=1, source_target_pairs={{0,5},{1,4},{2,7},{3,6},{4,1},{5,0},{6,3},{7,2},{8,13},{9,12},{10,... | collective-permute-start | bytes 196616 | tf_op jit(solution)/shard_map/ppermute | solution.py:433
  65.2 10.0 %copy-start.7 = (bf16[4,2,32,128]{3,2,1,0:T(8,128)(2,1)}, bf16[4,2,32,128]{3,2,1,0:T(8,128)(2,1)S(1)}, u32[]{:S(2)}) copy-start(bf16[4,2,32,128]{3,2,1,0:T(8,128)(2,1)S(1)} %collective-permute-done.10.refs_1_) | copy-start | bytes 196612
  65.2 9.9 %collective-permute-start.15 = (bf16[4,2,32,128]{3,2,1,0:T(8,128)(2,1)}, bf16[4,2,32,128]{3,2,1,0:T(8,128)(2,1)S(1)}, u32[]{:S(2)}, u32[]{:S(2)}) collective-permute-start(bf16[4,2,32,128]{3,2,1,0:T(8,128)(2,1)} %get-tuple-element.104), channel_id=1, source_target_pairs={{0,6},{1,7},{2,4},{3,5},{4,2},{5,3},{6,0},{7,1},{8,14},{9,15},{10,... | collective-permute-start | bytes 196616 | tf_op jit(solution)/shard_map/ppermute | solution.py:433
  66.9 8.3 %copy-start.8 = (bf16[4,2,32,128]{3,2,1,0:T(8,128)(2,1)}, bf16[4,2,32,128]{3,2,1,0:T(8,128)(2,1)S(1)}, u32[]{:S(2)}) copy-start(bf16[4,2,32,128]{3,2,1,0:T(8,128)(2,1)S(1)} %collective-permute-done.11.refs_2_) | copy-start | bytes 196612
  66.9 8.3 %collective-permute-start.16 = (bf16[4,2,32,128]{3,2,1,0:T(8,128)(2,1)}, bf16[4,2,32,128]{3,2,1,0:T(8,128)(2,1)S(1)}, u32[]{:S(2)}, u32[]{:S(2)}) collective-permute-start(bf16[4,2,32,128]{3,2,1,0:T(8,128)(2,1)} %get-tuple-element.105), channel_id=1, source_target_pairs={{0,7},{1,6},{2,5},{3,4},{4,3},{5,2},{6,1},{7,0},{8,15},{9,14},{10,... | collective-permute-start | bytes 196616 | tf_op jit(solution)/shard_map/ppermute | solution.py:433
  67.9 7.3 %copy-start.9 = (bf16[4,2,32,128]{3,2,1,0:T(8,128)(2,1)}, bf16[4,2,32,128]{3,2,1,0:T(8,128)(2,1)S(1)}, u32[]{:S(2)}) copy-start(bf16[4,2,32,128]{3,2,1,0:T(8,128)(2,1)S(1)} %collective-permute-done.12.refs_3_) | copy-start | bytes 196612
  72.7 2.5 %copy-start.10 = (bf16[4,2,32,128]{3,2,1,0:T(8,128)(2,1)}, bf16[4,2,32,128]{3,2,1,0:T(8,128)(2,1)S(1)}, u32[]{:S(2)}) copy-start(bf16[4,2,32,128]{3,2,1,0:T(8,128)(2,1)S(1)} %collective-permute-done.13.refs_4_) | copy-start | bytes 196612
  75.1 0.6 copy-start.11
  75.1 0.6 copy-start.12
  75.1 0.7 copy-start.13
  82.8 13.4 %collective-permute-start.17 = (bf16[2,8,32,128]{3,2,1,0:T(8,128)(2,1)}, bf16[2,8,32,128]{3,2,1,0:T(8,128)(2,1)S(1)}, u32[]{:S(2)}, u32[]{:S(2)}) collective-permute-start(bf16[2,8,32,128]{3,2,1,0:T(8,128)(2,1)} %get-tuple-element.113), channel_id=1, source_target_pairs={{0,8},{8,0},{16,24},{24,16},{1,9},{9,1},{17,25},{25,17},{2,10},{10... | collective-permute-start | bytes 393224 | tf_op jit(solution)/shard_map/ppermute | solution.py:430
  82.8 13.4 %collective-permute-start.18 = (bf16[2,8,32,128]{3,2,1,0:T(8,128)(2,1)}, bf16[2,8,32,128]{3,2,1,0:T(8,128)(2,1)S(1)}, u32[]{:S(2)}, u32[]{:S(2)}) collective-permute-start(bf16[2,8,32,128]{3,2,1,0:T(8,128)(2,1)} %get-tuple-element.114), channel_id=1, source_target_pairs={{0,16},{8,24},{16,0},{24,8},{1,17},{9,25},{17,1},{25,9},{2,18},{10... | collective-permute-start | bytes 393224 | tf_op jit(solution)/shard_map/ppermute | solution.py:430
  84.9 12.0 %collective-permute-start.19 = (bf16[2,8,32,128]{3,2,1,0:T(8,128)(2,1)}, bf16[2,8,32,128]{3,2,1,0:T(8,128)(2,1)}, u32[]{:S(2)}, u32[]{:S(2)}) collective-permute-start(bf16[2,8,32,128]{3,2,1,0:T(8,128)(2,1)} %get-tuple-element.115), channel_id=1, source_target_pairs={{0,24},{8,16},{16,8},{24,0},{1,25},{9,17},{17,9},{25,1},{2,26},{10... | collective-permute-start | bytes 393224 | tf_op jit(solution)/shard_map/ppermute | solution.py:430
  92.3 4.6 %copy-start.2 = (bf16[6,128,4,258]{1,2,3,0:T(4,128)(2,1)S(1)}, bf16[6,128,4,258]{1,2,3,0:T(4,128)(2,1)}, u32[]{:S(2)}) copy-start(bf16[6,128,4,258]{1,2,3,0:T(4,128)(2,1)} %param.21) | copy-start | bytes 4755460
  92.3 64.0 %all-to-all-start.1 = ((bf16[32,2,32,640]{3,2,1,0:T(8,128)(2,1)}), bf16[32,2,32,640]{3,2,1,0:T(8,128)(2,1)}, u32[]{:S(2)}, u32[]{:S(2)}) async-start(bf16[32,2,32,640]{3,2,1,0:T(8,128)(2,1)} %latitudinal_wide.1), calls=%async_computation.1 | async-start | bytes 5242880 | tf_op jit(solution)/shard_map/all_to_all | solution.py:462
  96.2 1.1 copy-start.4
  96.2 0.9 copy-start.21
  96.3 0.6 copy-start.22
  109.5 1.5 copy-start.19
  109.5 2.5 %copy-start.16 = (f32[8,128]{1,0:T(8,128)S(1)}, f32[8,128]{1,0:T(8,128)}, u32[]{:S(2)}) copy-start(f32[8,128]{1,0:T(8,128)} %param.24) | copy-start | bytes 12292
  109.5 2.6 %copy-start.18 = (bf16[8,128]{1,0:T(8,128)(2,1)S(1)}, bf16[8,128]{1,0:T(8,128)(2,1)}, u32[]{:S(2)}) copy-start(bf16[8,128]{1,0:T(8,128)(2,1)} %param.23) | copy-start | bytes 6148
  109.5 2.6 %copy-start.20 = (f32[128]{0:T(128)S(1)}, f32[128]{0:T(128)}, u32[]{:S(2)}) copy-start(f32[128]{0:T(128)} %param.25) | copy-start | bytes 1540
  118.9 10.7 %copy-start.17 = (f32[768]{0:T(1024)S(1)}, f32[768]{0:T(1024)}, u32[]{:S(2)}) copy-start(f32[768]{0:T(1024)} %param.20) | copy-start | bytes 9220

commit v4 on v3

--- a/solution.py
+++ b/solution.py
@@ -97,21 +97,25 @@
 def analyse_wide(air, table, width, groups):
     lines, cells, _ = air.shape
     rows = table.shape[0] // groups
-    out = jax.ShapeDtypeStruct((groups, lines, rows, width), jnp.bfloat16)
+    places = [(0, 0, width - SLIM), (1, width - SLIM, width)]
+    out = jax.ShapeDtypeStruct((groups, rows, 2 * width - SLIM), jnp.bfloat16)
 
     def body(table_ref, air_ref, out_ref):
-        for span in lane_spans(width):
-            coeffs = jnp.dot(table_ref[...], air_ref[0, :, span], preferred_element_type=jnp.float32)
-            out_ref[:, :, :, span] = coeffs.astype(jnp.bfloat16).reshape(groups, 1, rows, -1)
-
-    return pl.pallas_call(
-        body,
-        grid=(lines,),
+        for line, at, size in places:
+            for span in lane_spans(size):
+                coeffs = jnp.dot(table_ref[...], air_ref[line, :, span], preferred_element_type=jnp.float32)
+                out_ref[:, :, at + span.start : at + span.stop] = coeffs.astype(jnp.bfloat16).reshape(
+                    groups, rows, -1
+                )
+
+    return pl.pallas_call(
+        body,
+        grid=(1,),
         in_specs=[
-            pl.BlockSpec(table.shape, lambda a: (0, 0)),
-            pl.BlockSpec((1, cells, width), lambda a: (a, 0, 0)),
+            pl.BlockSpec(table.shape, lambda i: (0, 0)),
+            pl.BlockSpec((lines, cells, width), lambda i: (0, 0, 0)),
         ],
-        out_specs=pl.BlockSpec((groups, 1, rows, width), lambda a: (0, a, 0, 0)),
+        out_specs=pl.BlockSpec(out.shape, lambda i: (0, 0, 0)),
         out_shape=out,
         compiler_params=compiler_params(),
         cost_estimate=cost(2 * lines * table.size * width, table, air, out),
@@ -125,14 +129,15 @@
     plane = groups // sections
     rows = table.shape[0] // groups
     size = plane * rows
-    out = jax.ShapeDtypeStruct((lines, plane, rows, width), jnp.bfloat16)
-
-    def body(sec_ref, table_ref, air_ref, *outs):
-        both = jnp.concatenate([air_ref[a] for a in range(lines)], axis=1)
+    pieces = lines + 1
+    out = jax.ShapeDtypeStruct((pieces, plane, rows, width), jnp.bfloat16)
+
+    def body(sec_ref, table_ref, air_ref, before_ref, *outs):
+        joined = jnp.concatenate([air_ref[a] for a in range(lines)] + [before_ref[0]], axis=1)
         for o, out_ref in enumerate(outs):
             part = pl.ds(pl.multiple_of((sec_ref[0] ^ o) * size, size), size)
-            coeffs = jnp.dot(table_ref[part, :], both, preferred_element_type=jnp.float32).astype(jnp.bfloat16)
-            for a in range(lines):
+            coeffs = jnp.dot(table_ref[part, :], joined, preferred_element_type=jnp.float32).astype(jnp.bfloat16)
+            for a in range(pieces):
                 out_ref[a] = coeffs[:, a * width : (a + 1) * width].reshape(plane, rows, width)
 
     return pl.pallas_call(
@@ -142,13 +147,14 @@
             pl.BlockSpec(memory_space=pltpu.SMEM),
             pl.BlockSpec(table.shape, lambda i: (0, 0)),
             pl.BlockSpec((lines, cells, width), lambda i: (0, 0, start // width)),
+            pl.BlockSpec((1, cells, width), lambda i: (0, 0, start // width - 1)),
         ],
         out_specs=[pl.BlockSpec(out.shape, lambda i: (0, 0, 0, 0))] * sections,
         out_shape=[out] * sections,
         compiler_params=compiler_params(),
-        cost_estimate=cost(2 * lines * table.size * width, table, *[out] * 2 * sections),
+        cost_estimate=cost(2 * pieces * table.size * width, table, *[out] * 2 * sections),
         name="analyse_slim",
-    )(sec, table, air)
+    )(sec, table, air, air)
 
 
 def wavenumber_at(row):
@@ -162,31 +168,40 @@
     return back.astype(jnp.bfloat16)
 
 
-def latitudinal_wide(coeffs, matrix, damping):
-    devices, lines, rows, width = coeffs.shape
+def latitudinal_wide(coeffs, joined, matrix, damping):
+    devices, rows, _ = coeffs.shape
     modes, degrees, lats = matrix.shape
-
-    def body(x_ref, matrix_ref, damping_ref, out_ref):
+    lines = lats // devices
+    width = (coeffs.shape[-1] + SLIM) // 2
+    both = width - SLIM
+
+    def body(x_ref, joined_ref, matrix_ref, damping_ref, out_ref):
         parity = pl.program_id(0)
-        for span in lane_spans(width):
-            by_coeff = jnp.swapaxes(x_ref[:, :, :, span].reshape(lats, GROUP, -1), 0, 1)
+        for span in lane_spans(both) + [slice(both, width)]:
+            first = x_ref[:, :, span] if span.start < both else joined_ref[...]
+            second = x_ref[:, :, both + span.start : both + span.stop]
+            by_coeff = jnp.swapaxes(jnp.stack([first, second], axis=1).reshape(lats, GROUP, -1), 0, 1)
             results = [
                 damp(matrix_ref[wavenumber_at(row) + parity], by_coeff[row], damping_ref[:, span])
                 for row in range(GROUP)
             ]
             out_ref[:, :, :, span] = jnp.swapaxes(jnp.stack(results), 0, 1).reshape(devices, lines, GROUP, -1)
 
-    half_rows = pl.BlockSpec((devices, lines, GROUP, width), lambda p: (0, 0, p, 0))
     return pl.pallas_call(
         body,
         grid=(rows // GROUP,),
-        in_specs=[half_rows, whole(matrix), pl.BlockSpec((degrees, width), lambda p: (0, 0))],
-        out_specs=half_rows,
-        out_shape=jax.ShapeDtypeStruct(coeffs.shape, jnp.bfloat16),
+        in_specs=[
+            pl.BlockSpec((devices, GROUP, coeffs.shape[-1]), lambda p: (0, p, 0)),
+            pl.BlockSpec((devices, GROUP, SLIM), lambda p: (0, p, 0)),
+            whole(matrix),
+            pl.BlockSpec((degrees, width), lambda p: (0, 0)),
+        ],
+        out_specs=pl.BlockSpec((devices, lines, GROUP, width), lambda p: (0, 0, p, 0)),
+        out_shape=jax.ShapeDtypeStruct((devices, lines, rows, width), jnp.bfloat16),
         compiler_params=compiler_params(),
         cost_estimate=cost(4 * rows * degrees * lats * width, coeffs, coeffs, matrix),
         name="latitudinal_wide",
-    )(coeffs, matrix, damping)
+    )(coeffs, joined, matrix, damping)
 
 
 def whole(x):
@@ -239,37 +254,44 @@
     )(place, *parts)
 
 
-def latitudinal_slim(parts, matrix, damping, start):
-    sections, lines, rows, width = parts[0].shape
+def latitudinal_slim(parts, matrix, damping, start, position):
+    sections, pieces, rows, width = parts[0].shape
+    lines = pieces - 1
     plane = len(parts)
     degrees = damping.shape[0]
     own = sections * lines
-    out = jax.ShapeDtypeStruct(parts[0].shape, jnp.bfloat16)
-
-    def body(matrix_ref, damping_ref, *refs):
-        latitudes = jnp.concatenate([ref[...].reshape(own, rows, width) for ref in refs[:plane]], axis=0)
+    out = jax.ShapeDtypeStruct((sections, lines, rows, width), jnp.bfloat16)
+    joined = jax.ShapeDtypeStruct((sections * plane, rows, width), jnp.bfloat16)
+
+    def body(position_ref, matrix_ref, damping_ref, *refs):
+        part_refs, joined_ref, out_refs = refs[:plane], refs[plane], refs[plane + 1 :]
+        latitudes = jnp.concatenate([ref[:, :lines].reshape(own, rows, width) for ref in part_refs], axis=0)
         by_coeff = jnp.swapaxes(latitudes, 0, 1)
         results = [
             damp(matrix_ref[wavenumber_at(row)], by_coeff[row], damping_ref[...]) for row in range(rows)
         ]
         by_lat = jnp.swapaxes(jnp.stack(results), 0, 1)
-        for p, out_ref in enumerate(refs[plane:]):
+        for p, out_ref in enumerate(out_refs):
             out_ref[...] = by_lat[p * own : (p + 1) * own].reshape(out_ref.shape)
+            for o in range(sections):
+                device = (position_ref[0] ^ o) * plane + (position_ref[1] ^ p)
+                joined_ref[device] = part_refs[p][o, lines]
 
     return pl.pallas_call(
         body,
         grid=(1,),
         in_specs=[
+            pl.BlockSpec(memory_space=pltpu.SMEM),
             whole(matrix),
             pl.BlockSpec((degrees, width), lambda i: (0, start // width)),
         ]
-        + [whole(out)] * plane,
-        out_specs=[whole(out)] * plane,
-        out_shape=[out] * plane,
+        + [whole(parts[0])] * plane,
+        out_specs=[whole(joined)] + [whole(out)] * plane,
+        out_shape=[joined] + [out] * plane,
         compiler_params=compiler_params(),
         cost_estimate=pl.CostEstimate(flops=10**11, bytes_accessed=3 * 10**8, transcendentals=0),
         name="latitudinal_slim",
-    )(matrix, damping, *parts)
+    )(position, matrix, damping, *parts)
 
 
 def advance(air, rebuilt, sea, warmth):
@@ -411,8 +433,9 @@
     wide = channel_count - SLIM
     in_kernels = (
         per_device == 2 * GROUP
-        and wide > 0
+        and wide > SLIM
         and wide % SLIM == 0
+        and parallel_lines == 2
         and sec_count & (sec_count - 1) == 0
         and lat_count == device_count * parallel_lines
     )
@@ -438,9 +461,7 @@
         wide_coeffs = analyse_wide(air_after, forward, wide, device_count)
         wide_coeffs = lax.all_to_all(wide_coeffs, AXES, split_axis=0, concat_axis=0, tiled=True)
         slim = to_plane(slim, place.reshape(1))
-        air_after, matrix_after, *slim = lax.optimization_barrier(
-            (air_field_lattice, associated_polynomial_matrix, *slim)
-        )
+        matrix_after, *slim = lax.optimization_barrier((associated_polynomial_matrix, *slim))
         slim = over_plane(slim)
 
         at_lat = jnp.arange(lat_count, dtype=jnp.int32)
@@ -452,17 +473,19 @@
             "mlt,tu->mlu", matrix_after, shuffle, preferred_element_type=jnp.float32
         ).astype(jnp.bfloat16)
 
-        gathered = gather_flux(air_after, boundary_exchange_projector)
-        gathered, *slim = lax.optimization_barrier((gathered, *slim))
-        slim = latitudinal_slim(slim, shuffled, harmonic_damping_factor, wide)
+        position = jnp.stack([sec_id, place]).astype(jnp.int32)
+        joined, *slim = latitudinal_slim(slim, shuffled, harmonic_damping_factor, wide, position)
         slim = from_plane(over_plane(slim), place.reshape(1))
         wide_coeffs, *slim = lax.optimization_barrier((wide_coeffs, *slim))
         slim = over_sections(slim)
-        wide_coeffs = latitudinal_wide(wide_coeffs, associated_polynomial_matrix, harmonic_damping_factor)
+        wide_coeffs = latitudinal_wide(
+            wide_coeffs, joined, associated_polynomial_matrix, harmonic_damping_factor
+        )
         wide_coeffs = lax.all_to_all(wide_coeffs, AXES, split_axis=0, concat_axis=0, tiled=True)
-        water_patch_fields, gathered, warmth_response_factor, patch_holder_index, *slim = lax.optimization_barrier(
-            (water_patch_fields, gathered, warmth_response_factor, patch_holder_index, *slim)
+        (air_after, water_patch_fields, warmth_response_factor, patch_holder_index, *slim) = lax.optimization_barrier(
+            (air_field_lattice, water_patch_fields, warmth_response_factor, patch_holder_index, *slim)
         )
+        gathered = gather_flux(air_after, boundary_exchange_projector)
     else:
         gathered = gather_flux(air_field_lattice, boundary_exchange_projector)
         table = dft_table(meridian_number)

time: 163 us -> 160 us (0.982)
  waiting for transfers between devices: 45 us -> 38.9 us
  starting transfers between devices: 33.4 us -> 35.6 us
  matrix products: 22.9 us -> 24.8 us
  blocking collectives: 21.3 us -> 19.4 us
    all_to_all x2, waiting for transfers between devices: 26.9 us -> 10.4 us  [shards(): lax.all_to_all(wide_coeffs, AXES, split_axis=0, concat_axis=0, tiled=True)]
    ppermute x14, waiting for transfers between devices: 18.1 us -> 25.6 us  [over_plane(): lax.ppermute(x, ('band', 'ch'), twists[p])]
    ppermute x6, waiting for transfers between devices: 0.02 us -> 2.99 us  [over_sections(): lax.ppermute(x, 'sec', hops[o])]
    ppermute x6, starting transfers between devices: 10 us -> 12.2 us  [over_sections(): lax.ppermute(x, 'sec', hops[o])]
    dot_general x1, matrix products: 0.91 us -> 2.81 us  [gather_flux(): jnp.einsum('anc,cf->fan', air, projector, preferred_element_type=jnp.floa...]
    all_gather x1, blocking collectives: 8.32 us -> 6.63 us  [shards(): sea_all = lax.all_gather(sea_slots, 'band', axis=0, tiled=True)]
    unnamed x67 -> x65, local copies, waits for them, and re-layouts: 5.2 us -> 4.93 us
  transfers between devices with their start and end apart: 22 -> 22, of which waited for: 5 -> 10; matrix products, arithmetic and copies ran while one was open for 17% -> 19% of each run, Pallas kernels for 13% -> 14%
where the time goes in v4:
time: 160 us
  waiting for transfers between devices  38.9 us (24%)
  starting transfers between devices  35.6 us (22%)
  Pallas kernels  31.1 us (19%)
  matrix products  24.8 us (16%)
  blocking collectives  19.4 us (12%)
  local copies, waits for them, and re-layouts  7.76 us (5%)
    ppermute x14, waiting for transfers between devices, over_plane(): lax.ppermute(x, ('band', 'ch'), twists[p])  25.6 us
    dot_general x9, matrix products, ocean_update(): jnp.einsum('io,sirw->sorw', kernel_coefficients[shift_row, shift_col], wi...  13.8 us
    ppermute x14, starting transfers between devices, over_plane(): lax.ppermute(x, ('band', 'ch'), twists[p])  13.6 us
    all_gather x1, blocking collectives, gather_flux(): return lax.all_gather(flux_local, 'band', axis=1, tiled=True)  12.8 us
    ppermute x6, starting transfers between devices, over_sections(): lax.ppermute(x, 'sec', hops[o])  12.2 us
    all_to_all x2, waiting for transfers between devices, shards(): lax.all_to_all(wide_coeffs, AXES, split_axis=0, concat_axis=0, tiled=True)  10.4 us
    all_to_all x2, starting transfers between devices, shards(): lax.all_to_all(wide_coeffs, AXES, split_axis=0, concat_axis=0, tiled=True)  9.74 us
    dot_general x1, matrix products, ocean_update(): jnp.einsum('io,sirw->sorw', water_readout_matrix, hidden, preferred_eleme...  6.79 us
  transfers between devices with their start and end apart: 22, of which 10 were waited for; matrix products, arithmetic and copies ran while one was open for 19% of the time, Pallas kernels for 14%

profile of v4, /device:TPU:0, one launch (start us, length us, event | category | flops | bytes accessed | tf_op | source)
XLA Modules:
  0.0 159.7 jit_solution(10511342150389408999)
XLA Ops:
  0.7 3.7 %analyse_slim.1 = (bf16[3,8,32,128]{3,2,1,0:T(8,128)(2,1)}, bf16[3,8,32,128]{3,2,1,0:T(8,128)(2,1)}, bf16[3,8,32,128]{3,2,1,0:T(8,128)(2,1)}, bf16[3,8,32,128]{3,2,1,0:T(8,128)(2,1)}) custom-call(s32[1]{0:T(128)} %bitcast.sec_ref, bf16[1024,1024]{1,0:T(8,128)(2,1)} %constant.153.clone.table_ref, bf16[2,1024,768]{2,1,0:T(8,128)(2,1)} %air_ref.2, ...), custom_call_target="tpu_custom_call" | custom-call | flops 805306368 | bytes 3670016 | tf_op jit(solution)/shard_map/analyse_slim/pallas_call | solution.py:143
  4.4 3.0 %collective-permute-start = (bf16[3,8,32,128]{3,2,1,0:T(8,128)(2,1)}, bf16[3,8,32,128]{3,2,1,0:T(8,128)(2,1)S(1)}, u32[]{:S(2)}, u32[]{:S(2)}) collective-permute-start(bf16[3,8,32,128]{3,2,1,0:T(8,128)(2,1)} %get-tuple-element.60), channel_id=1, source_target_pairs={{0,8},{8,0},{16,24},{24,16},{1,9},{9,1},{17,25},{25,17},{2,10},{10... | collective-permute-start | bytes 589832 | tf_op jit(solution)/shard_map/ppermute | solution.py:453
  7.4 2.6 %collective-permute-start.1 = (bf16[3,8,32,128]{3,2,1,0:T(8,128)(2,1)}, bf16[3,8,32,128]{3,2,1,0:T(8,128)(2,1)S(1)}, u32[]{:S(2)}, u32[]{:S(2)}) collective-permute-start(bf16[3,8,32,128]{3,2,1,0:T(8,128)(2,1)} %get-tuple-element.61), channel_id=1, source_target_pairs={{0,16},{8,24},{16,0},{24,8},{1,17},{9,25},{17,1},{25,9},{2,18},{10... | collective-permute-start | bytes 589832 | tf_op jit(solution)/shard_map/ppermute | solution.py:453
  10.0 6.6 %analyse_wide.1 = bf16[32,32,1152]{2,1,0:T(8,128)(2,1)} custom-call(bf16[1024,1024]{1,0:T(8,128)(2,1)} %constant.153.clone.table_ref, bf16[2,1024,768]{2,1,0:T(8,128)(2,1)} %air_ref.2), custom_call_target="tpu_custom_call" | custom-call | flops 2684354560 | bytes 7602176 | tf_op jit(solution)/shard_map/analyse_wide/pallas_call | solution.py:111
  16.7 6.1 %all-to-all-start = ((bf16[32,32,1152]{2,1,0:T(8,128)(2,1)}), bf16[32,32,1152]{2,1,0:T(8,128)(2,1)S(1)}, u32[]{:S(2)}, u32[]{:S(2)}) async-start(bf16[32,32,1152]{2,1,0:T(8,128)(2,1)} %analyse_wide.1), calls=%async_computation | async-start | bytes 4718592 | tf_op jit(solution)/shard_map/all_to_all | solution.py:462
  22.7 0.6 pad_add_fusion.position_ref
  23.3 1.5 collective-permute-done.1.refs_2_
  24.8 0.7 copy-done.6
  25.5 0.7 copy-done.7
  26.1 2.2 %to_plane.1 = (bf16[4,3,32,128]{3,2,1,0:T(8,128)(2,1)}, bf16[4,3,32,128]{3,2,1,0:T(8,128)(2,1)}, bf16[4,3,32,128]{3,2,1,0:T(8,128)(2,1)}, bf16[4,3,32,128]{3,2,1...) custom-call(s32[1]{0:T(128)} %bitcast.1.place_ref, ...), custom_call_target="tpu_custom_call" | custom-call | bytes 1572864 | tf_op jit(solution)/shard_map/to_plane/pallas_call | solution.py:222
  28.3 1.5 collective-permute-start.4
  29.9 0.3 collective-permute-start.5
  30.2 1.5 collective-permute-start.6
  31.7 0.2 collective-permute-start.7
  31.9 2.5 %collective-permute-start.8 = (bf16[4,3,32,128]{3,2,1,0:T(8,128)(2,1)}, bf16[4,3,32,128]{3,2,1,0:T(8,128)(2,1)S(1)}, u32[]{:S(2)}, u32[]{:S(2)}) collective-permute-start(bf16[4,3,32,128]{3,2,1,0:T(8,128)(2,1)} %get-tuple-element.78), channel_id=1, source_target_pairs={{0,6},{1,7},{2,4},{3,5},{4,2},{5,3},{6,0},{7,1},{8,14},{9,15},{10,... | collective-permute-start | bytes 294920 | tf_op jit(solution)/shard_map/ppermute | solution.py:456
  34.4 7.6 %collective-permute-done.4.refs_2_ = bf16[4,3,32,128]{3,2,1,0:T(8,128)(2,1)S(1)} collective-permute-done((bf16[4,3,32,128]{3,2,1,0:T(8,128)(2,1)}, bf16[4,3,32,128]{3,2,1,0:T(8,128)(2,1)S(1)}, u32[]{:S(2)}, u32[]{:S(2)}) %collective-permute-start.4) | collective-permute-done | bytes 98336 | tf_op jit(solution)/shard_map/ppermute | solution.py:456
  42.0 0.7 collective-permute-start.9
  42.6 0.9 convolution_convert_fusion.matrix_ref
  43.6 3.2 %collective-permute-done.7.refs_5_ = bf16[4,3,32,128]{3,2,1,0:T(8,128)(2,1)S(1)} collective-permute-done((bf16[4,3,32,128]{3,2,1,0:T(8,128)(2,1)}, bf16[4,3,32,128]{3,2,1,0:T(8,128)(2,1)S(1)}, u32[]{:S(2)}, u32[]{:S(2)}) %collective-permute-start.7) | collective-permute-done | bytes 98336 | tf_op jit(solution)/shard_map/ppermute | solution.py:456
  46.8 7.2 %collective-permute-done.8.refs_6_ = bf16[4,3,32,128]{3,2,1,0:T(8,128)(2,1)S(1)} collective-permute-done((bf16[4,3,32,128]{3,2,1,0:T(8,128)(2,1)}, bf16[4,3,32,128]{3,2,1,0:T(8,128)(2,1)S(1)}, u32[]{:S(2)}, u32[]{:S(2)}) %collective-permute-start.8) | collective-permute-done | bytes 98336 | tf_op jit(solution)/shard_map/ppermute | solution.py:456
  54.1 1.3 collective-permute-done.9.refs_7_
  55.4 0.6 copy-done.30
  56.1 2.8 %latitudinal_slim.1 = (bf16[32,32,128]{2,1,0:T(8,128)(2,1)}, bf16[4,2,32,128]{3,2,1,0:T(8,128)(2,1)}, bf16[4,2,32,128]{3,2,1,0:T(8,128)(2,1)}, bf16[4,2,32,128]{...) custom-call(s32[2]{0:T(128)} %pad_add_fusion.position_ref, ...), custom_call_target="tpu_custom_call" | custom-call | flops 99999997952 | bytes 300000000 | tf_op jit(solution)/shard_map/latitudinal_slim/pallas_call | solution.py:280
  58.8 0.4 collective-permute-start.10
  59.3 1.7 %collective-permute-start.11 = (bf16[4,2,32,128]{3,2,1,0:T(8,128)(2,1)}, bf16[4,2,32,128]{3,2,1,0:T(8,128)(2,1)S(1)}, u32[]{:S(2)}, u32[]{:S(2)}) collective-permute-start(bf16[4,2,32,128]{3,2,1,0:T(8,128)(2,1)} %get-tuple-element.82), channel_id=1, source_target_pairs={{0,2},{1,3},{2,0},{3,1},{4,6},{5,7},{6,4},{7,5},{8,10},{9,11},{10,... | collective-permute-start | bytes 196616 | tf_op jit(solution)/shard_map/ppermute | solution.py:456
  60.9 2.1 %collective-permute-start.13 = (bf16[4,2,32,128]{3,2,1,0:T(8,128)(2,1)}, bf16[4,2,32,128]{3,2,1,0:T(8,128)(2,1)S(1)}, u32[]{:S(2)}, u32[]{:S(2)}) collective-permute-start(bf16[4,2,32,128]{3,2,1,0:T(8,128)(2,1)} %get-tuple-element.84), channel_id=1, source_target_pairs={{0,4},{1,5},{2,6},{3,7},{4,0},{5,1},{6,2},{7,3},{8,12},{9,13},{10,... | collective-permute-start | bytes 196616 | tf_op jit(solution)/shard_map/ppermute | solution.py:456
  63.0 0.4 collective-permute-start.14
  63.4 1.2 collective-permute-start.15
  64.5 1.2 collective-permute-start.16
  65.8 1.1 collective-permute-done.13.refs_4_
  66.9 5.0 %collective-permute-done.14.refs_5_ = bf16[4,2,32,128]{3,2,1,0:T(8,128)(2,1)S(1)} collective-permute-done((bf16[4,2,32,128]{3,2,1,0:T(8,128)(2,1)}, bf16[4,2,32,128]{3,2,1,0:T(8,128)(2,1)S(1)}, u32[]{:S(2)}, u32[]{:S(2)}) %collective-permute-start.14) | collective-permute-done | bytes 65568 | tf_op jit(solution)/shard_map/ppermute | solution.py:456
  72.0 0.6 copy-done.12
  72.6 1.9 %from_plane.1 = (bf16[2,8,32,128]{3,2,1,0:T(8,128)(2,1)}, bf16[2,8,32,128]{3,2,1,0:T(8,128)(2,1)}, bf16[2,8,32,128]{3,2,1,0:T(8,128)(2,1)}, bf16[2,8,32,128]{3,2,1,0:T(8,128)(2,1)}) custom-call(s32[1]{0:T(128)} %bitcast.1.place_ref, bf16[4,2,32,128]{3,2,1,0:T(8,128)(2,1)} %get-tuple-element.80.refs_0_, bf16[4,2,32,128]{3,2,1,0:T(8,128)(2,1)} %copy-done.8, ...), custom_call_target="tpu_custom_call" | custom-call | bytes 1048576 | tf_op jit(solution)/shard_map/from_plane/pallas_call | solution.py:245
  74.5 3.8 %all-to-all-done.x_ref = bf16[32,32,1152]{2,1,0:T(8,128)(2,1)S(1)} async-done(((bf16[32,32,1152]{2,1,0:T(8,128)(2,1)}), bf16[32,32,1152]{2,1,0:T(8,128)(2,1)S(1)}, u32[]{:S(2)}, u32[]{:S(2)}) %all-to-all-start) | async-done | bytes 2359328 | tf_op jit(solution)/shard_map/all_to_all | solution.py:462
  78.3 4.2 %collective-permute-start.17 = (bf16[2,8,32,128]{3,2,1,0:T(8,128)(2,1)}, bf16[2,8,32,128]{3,2,1,0:T(8,128)(2,1)S(1)}, u32[]{:S(2)}, u32[]{:S(2)}) collective-permute-start(bf16[2,8,32,128]{3,2,1,0:T(8,128)(2,1)} %get-tuple-element.95), channel_id=1, source_target_pairs={{0,8},{8,0},{16,24},{24,16},{1,9},{9,1},{17,25},{25,17},{2,10},{10... | collective-permute-start | bytes 393224 | tf_op jit(solution)/shard_map/ppermute | solution.py:453
  82.5 2.4 %collective-permute-start.19 = (bf16[2,8,32,128]{3,2,1,0:T(8,128)(2,1)}, bf16[2,8,32,128]{3,2,1,0:T(8,128)(2,1)}, u32[]{:S(2)}, u32[]{:S(2)}) collective-permute-start(bf16[2,8,32,128]{3,2,1,0:T(8,128)(2,1)} %get-tuple-element.97), channel_id=1, source_target_pairs={{0,24},{8,16},{16,8},{24,0},{1,25},{9,17},{17,9},{25,1},{2,26},{10... | collective-permute-start | bytes 393224 | tf_op jit(solution)/shard_map/ppermute | solution.py:453
  85.0 5.1 %latitudinal_wide.1 = bf16[32,2,32,640]{3,2,1,0:T(8,128)(2,1)} custom-call(bf16[32,32,1152]{2,1,0:T(8,128)(2,1)} %copy-done.1, bf16[32,32,128]{2,1,0:T(8,128)(2,1)} %get-tuple-element.93.joined_ref, bf16[16,64,64]{2,1,0:T(8,128)(2,1)} %matrix_ref.1, f32[64,768]{1,0:T(8,128)} %damping_ref.3), custom_call_target="tpu_custom_call" | custom-call | flops 335544320 | bytes 4849664 | tf_op jit(solution)/shard_map/latitudinal_wide/pallas_call | solution.py:190
  90.1 3.7 %all-to-all-start.1 = ((bf16[32,2,32,640]{3,2,1,0:T(8,128)(2,1)}), bf16[32,2,32,640]{3,2,1,0:T(8,128)(2,1)}, u32[]{:S(2)}, u32[]{:S(2)}) async-start(bf16[32,2,32,640]{3,2,1,0:T(8,128)(2,1)} %latitudinal_wide.1), calls=%async_computation.1 | async-start | bytes 5242880 | tf_op jit(solution)/shard_map/all_to_all | solution.py:484
  93.8 1.5 collective-permute-done.18.refs_2_
  95.3 0.2 copy.95
  95.5 0.4 copy-done.23
  95.9 1.5 fusion.14
  97.4 1.5 fusion.16
  99.0 1.6 fusion.18
  100.6 1.5 fusion.20
  102.1 1.5 fusion.36
  103.6 1.6 fusion.22
  105.2 1.5 fusion.24
  106.7 1.5 fusion.26
  108.2 1.5 fusion.28
  109.9 0.2 reduce_window_sum.11
  110.2 2.8 %fusion.12 = bf16[8,2,1024]{2,0,1:T(8,128)(2,1)S(1)} fusion(bf16[2,1024,768]{2,1,0:T(8,128)(2,1)} %air_ref.2, bf16[768,8]{0,1:T(8,128)(2,1)S(1)} %copy-done.15), kind=kOutput, calls=%fused_computation.17 | convolution fusion | flops 25182208 | bytes 3190784 | tf_op jit(solution)/shard_map/anc,cf->fan/dot_general | solution.py:398
  113.0 12.8 %all_gather.6 = bf16[8,8,1024]{2,0,1:T(8,128)(2,1)S(1)} all-gather(bf16[8,2,1024]{2,0,1:T(8,128)(2,1)S(1)} %fusion.12), channel_id=1, replica_groups=mesh['sec'=4,'band'=4,'ch'=2] {'band'}, dimensions={1}, use_global_device_ids=true | all-gather | bytes 163840 | tf_op jit(solution)/shard_map/all_gather | solution.py:404
  126.0 0.3 convert_reduce_fusion
  126.5 6.8 %fusion.9 = bf16[6,128,2,256]{1,3,2,0:T(8,128)(2,1)S(1)} fusion(f32[6,2,256,128]{3,2,1,0:T(8,128)} %fusion.14, f32[6,2,256,128]{3,2,1,0:T(8,128)} %fusion.16, f32[6,2,256,128]{3,2,1,0:T(8,128)} %fusion.18, f32[6,2,256,128]{3,2,1,0:T(8,128)} %fusion.20, f32[6,2,256,128]{3,2,1,0:T(8,128)} %fusion.36, f32[6,2,256,128]{3,2,1,0:T(8,128)} %fusion.22, ...), kind=kOutput, calls=%fused_computation.11 | convolution fusion | flops 116391936 | bytes 15828480 | tf_op jit(solution)/shard_map/io,sirw->sorw/dot_general | solution.py:74
  133.3 1.8 %copy.115 = bf16[6,128,2,256]{3,2,1,0:T(2,128)(2,1)} copy(bf16[6,128,2,256]{1,3,2,0:T(8,128)(2,1)S(1)} %fusion.9) | data formatting | bytes 1572864
  135.1 0.3 copy.113
  135.4 6.6 %all-gather = bf16[24,1,2,256]{3,2,1,0:T(2,128)(2,1)S(1)} all-gather(bf16[6,1,2,256]{3,2,1,0:T(2,128)(2,1)S(1)} %copy.113), channel_id=2, replica_groups=mesh['sec'=4,'band'=4,'ch'=2] {'band'}, dimensions={0}, use_global_device_ids=true | all-gather | bytes 30720 | tf_op jit(solution)/shard_map/all_gather | solution.py:541
  142.1 0.2 fusion.13
  142.4 1.2 stack.33.warmth_ref
  143.6 0.7 broadcast_in_dim.9.sea_ref
  144.3 3.0 %synthesise_slim.1.begun_ref = bf16[2,2,512,768]{3,2,1,0:T(8,128)(2,1)} custom-call(s32[1]{0:T(128)} %bitcast.sec_ref, bf16[2,512,512]{2,1,0:T(8,128)(2,1)} %constant.154.clone.table_ref, bf16[2,2,512,768]{3,2,1,0:T(8,128)(2,1)} %bitcast.125, bf16[2,2,16,512]{3,2,1,0:T(8,128)(2,1)} %broadcast_in_dim.9.sea_ref, bf16[16,768]{1,0:T(8,128)(2,1)} %stack.33.warmth_ref, ...), custom_call_target="tpu_custom_call" | custom-call | flops 99999997952 | bytes 300000000 | tf_op jit(solution)/shard_map/synthesise_slim/pallas_call | solution.py:338
  147.3 6.6 %all-to-all-done.1.coeff_ref = bf16[32,2,32,640]{3,2,1,0:T(8,128)(2,1)} async-done(((bf16[32,2,32,640]{3,2,1,0:T(8,128)(2,1)}), bf16[32,2,32,640]{3,2,1,0:T(8,128)(2,1)}, u32[]{:S(2)}, u32[]{:S(2)}) %all-to-all-start.1) | async-done | bytes 2621472 | tf_op jit(solution)/shard_map/all_to_all | solution.py:484
  153.9 5.8 %synthesise_wide.1 = bf16[2,2,512,768]{3,2,1,0:T(8,128)(2,1)} custom-call(bf16[2,512,512]{2,1,0:T(8,128)(2,1)} %constant.154.clone.table_ref, bf16[32,2,32,640]{3,2,1,0:T(8,128)(2,1)} %all-to-all-done.1.coeff_ref, bf16[2,2,512,768]{3,2,1,0:T(8,128)(2,1)} %bitcast.126, ...), custom_call_target="tpu_custom_call", output_to_operand_aliasing={{}: (5, {})} | custom-call | flops 1342177280 | bytes 8912896 | tf_op jit(solution)/shard_map/synthesise_wide/pallas_call | solution.py:377
  (100 shorter events, 1.0 us)
Async XLA Ops:
  0.6 125.8 %copy-start = (bf16[128,128]{1,0:T(8,128)(2,1)S(1)}, bf16[128,128]{1,0:T(8,128)(2,1)}, u32[]{:S(2)}) copy-start(bf16[128,128]{1,0:T(8,128)(2,1)} %param.26) | copy-start | bytes 98308
  4.4 18.9 %collective-permute-start = (bf16[3,8,32,128]{3,2,1,0:T(8,128)(2,1)}, bf16[3,8,32,128]{3,2,1,0:T(8,128)(2,1)S(1)}, u32[]{:S(2)}, u32[]{:S(2)}) collective-permute-start(bf16[3,8,32,128]{3,2,1,0:T(8,128)(2,1)} %get-tuple-element.60), channel_id=1, source_target_pairs={{0,8},{8,0},{16,24},{24,16},{1,9},{9,1},{17,25},{25,17},{2,10},{10... | collective-permute-start | bytes 589832 | tf_op jit(solution)/shard_map/ppermute | solution.py:453
  7.4 17.4 %collective-permute-start.1 = (bf16[3,8,32,128]{3,2,1,0:T(8,128)(2,1)}, bf16[3,8,32,128]{3,2,1,0:T(8,128)(2,1)S(1)}, u32[]{:S(2)}, u32[]{:S(2)}) collective-permute-start(bf16[3,8,32,128]{3,2,1,0:T(8,128)(2,1)} %get-tuple-element.61), channel_id=1, source_target_pairs={{0,16},{8,24},{16,0},{24,8},{1,17},{9,25},{17,1},{25,9},{2,18},{10... | collective-permute-start | bytes 589832 | tf_op jit(solution)/shard_map/ppermute | solution.py:453
  10.0 14.8 %collective-permute-start.2 = (bf16[3,8,32,128]{3,2,1,0:T(8,128)(2,1)}, bf16[3,8,32,128]{3,2,1,0:T(8,128)(2,1)S(1)}, u32[]{:S(2)}, u32[]{:S(2)}) collective-permute-start(bf16[3,8,32,128]{3,2,1,0:T(8,128)(2,1)} %get-tuple-element.62), channel_id=1, source_target_pairs={{0,24},{8,16},{16,8},{24,0},{1,25},{9,17},{17,9},{25,1},{2,26},{10... | collective-permute-start | bytes 589832 | tf_op jit(solution)/shard_map/ppermute | solution.py:453
  16.7 26.0 %copy-start.3 = (bf16[16,64,64]{2,1,0:T(8,128)(2,1)S(1)}, bf16[16,64,64]{2,1,0:T(8,128)(2,1)}, u32[]{:S(2)}) copy-start(bf16[16,64,64]{2,1,0:T(8,128)(2,1)} %matrix_ref.1) | copy-start | bytes 393220
  16.7 61.6 %all-to-all-start = ((bf16[32,32,1152]{2,1,0:T(8,128)(2,1)}), bf16[32,32,1152]{2,1,0:T(8,128)(2,1)S(1)}, u32[]{:S(2)}, u32[]{:S(2)}) async-start(bf16[32,32,1152]{2,1,0:T(8,128)(2,1)} %analyse_wide.1), calls=%async_computation | async-start | bytes 4718592 | tf_op jit(solution)/shard_map/all_to_all | solution.py:462
  23.3 1.5 copy-start.5
  24.8 0.7 copy-start.6
  25.5 0.7 copy-start.7
  28.3 3.6 %collective-permute-start.3 = (bf16[4,3,32,128]{3,2,1,0:T(8,128)(2,1)}, bf16[4,3,32,128]{3,2,1,0:T(8,128)(2,1)S(1)}, u32[]{:S(2)}, u32[]{:S(2)}) collective-permute-start(bf16[4,3,32,128]{3,2,1,0:T(8,128)(2,1)} %get-tuple-element.73), channel_id=1, source_target_pairs={{0,1},{1,0},{2,3},{3,2},{4,5},{5,4},{6,7},{7,6},{8,9},{9,8},{10,11... | collective-permute-start | bytes 294920 | tf_op jit(solution)/shard_map/ppermute | solution.py:456
  28.3 13.6 %collective-permute-start.4 = (bf16[4,3,32,128]{3,2,1,0:T(8,128)(2,1)}, bf16[4,3,32,128]{3,2,1,0:T(8,128)(2,1)S(1)}, u32[]{:S(2)}, u32[]{:S(2)}) collective-permute-start(bf16[4,3,32,128]{3,2,1,0:T(8,128)(2,1)} %get-tuple-element.74), channel_id=1, source_target_pairs={{0,2},{1,3},{2,0},{3,1},{4,6},{5,7},{6,4},{7,5},{8,10},{9,11},{10,... | collective-permute-start | bytes 294920 | tf_op jit(solution)/shard_map/ppermute | solution.py:456
  29.9 13.7 %collective-permute-start.5 = (bf16[4,3,32,128]{3,2,1,0:T(8,128)(2,1)}, bf16[4,3,32,128]{3,2,1,0:T(8,128)(2,1)S(1)}, u32[]{:S(2)}, u32[]{:S(2)}) collective-permute-start(bf16[4,3,32,128]{3,2,1,0:T(8,128)(2,1)} %get-tuple-element.75), channel_id=1, source_target_pairs={{0,3},{1,2},{2,1},{3,0},{4,7},{5,6},{6,5},{7,4},{8,11},{9,10},{10,... | collective-permute-start | bytes 294920 | tf_op jit(solution)/shard_map/ppermute | solution.py:456
  30.2 13.4 %collective-permute-start.6 = (bf16[4,3,32,128]{3,2,1,0:T(8,128)(2,1)}, bf16[4,3,32,128]{3,2,1,0:T(8,128)(2,1)S(1)}, u32[]{:S(2)}, u32[]{:S(2)}) collective-permute-start(bf16[4,3,32,128]{3,2,1,0:T(8,128)(2,1)} %get-tuple-element.76), channel_id=1, source_target_pairs={{0,4},{1,5},{2,6},{3,7},{4,0},{5,1},{6,2},{7,3},{8,12},{9,13},{10,... | collective-permute-start | bytes 294920 | tf_op jit(solution)/shard_map/ppermute | solution.py:456
  31.7 15.1 %collective-permute-start.7 = (bf16[4,3,32,128]{3,2,1,0:T(8,128)(2,1)}, bf16[4,3,32,128]{3,2,1,0:T(8,128)(2,1)S(1)}, u32[]{:S(2)}, u32[]{:S(2)}) collective-permute-start(bf16[4,3,32,128]{3,2,1,0:T(8,128)(2,1)} %get-tuple-element.77), channel_id=1, source_target_pairs={{0,5},{1,4},{2,7},{3,6},{4,1},{5,0},{6,3},{7,2},{8,13},{9,12},{10,... | collective-permute-start | bytes 294920 | tf_op jit(solution)/shard_map/ppermute | solution.py:456
  31.9 23.5 %copy-start.24 = (bf16[4,3,32,128]{3,2,1,0:T(8,128)(2,1)}, bf16[4,3,32,128]{3,2,1,0:T(8,128)(2,1)S(1)}, u32[]{:S(2)}) copy-start(bf16[4,3,32,128]{3,2,1,0:T(8,128)(2,1)S(1)} %collective-permute-done.3.refs_1_) | copy-start | bytes 294916
  31.9 22.2 %collective-permute-start.8 = (bf16[4,3,32,128]{3,2,1,0:T(8,128)(2,1)}, bf16[4,3,32,128]{3,2,1,0:T(8,128)(2,1)S(1)}, u32[]{:S(2)}, u32[]{:S(2)}) collective-permute-start(bf16[4,3,32,128]{3,2,1,0:T(8,128)(2,1)} %get-tuple-element.78), channel_id=1, source_target_pairs={{0,6},{1,7},{2,4},{3,5},{4,2},{5,3},{6,0},{7,1},{8,14},{9,15},{10,... | collective-permute-start | bytes 294920 | tf_op jit(solution)/shard_map/ppermute | solution.py:456
  41.9 13.4 %copy-start.25 = (bf16[4,3,32,128]{3,2,1,0:T(8,128)(2,1)}, bf16[4,3,32,128]{3,2,1,0:T(8,128)(2,1)S(1)}, u32[]{:S(2)}) copy-start(bf16[4,3,32,128]{3,2,1,0:T(8,128)(2,1)S(1)} %collective-permute-done.4.refs_2_) | copy-start | bytes 294916
  42.0 13.4 %collective-permute-start.9 = (bf16[4,3,32,128]{3,2,1,0:T(8,128)(2,1)}, bf16[4,3,32,128]{3,2,1,0:T(8,128)(2,1)S(1)}, u32[]{:S(2)}, u32[]{:S(2)}) collective-permute-start(bf16[4,3,32,128]{3,2,1,0:T(8,128)(2,1)} %get-tuple-element.79), channel_id=1, source_target_pairs={{0,7},{1,6},{2,5},{3,4},{4,3},{5,2},{6,1},{7,0},{8,15},{9,14},{10,... | collective-permute-start | bytes 294920 | tf_op jit(solution)/shard_map/ppermute | solution.py:456
  43.6 22.2 %copy-start.16 = (s32[6,2,256]{2,1,0:T(2,128)S(1)}, s32[6,2,256]{2,1,0:T(2,128)}, u32[]{:S(2)}) copy-start(s32[6,2,256]{2,1,0:T(2,128)} %param.28) | copy-start | bytes 36868
  43.6 41.4 %copy-start.31 = (s32[6]{0:T(128)S(1)}, s32[6]{0:T(128)}, u32[]{:S(2)}) copy-start(s32[6]{0:T(128)} %param.29) | copy-start | bytes 76
  43.6 11.8 %copy-start.26 = (bf16[4,3,32,128]{3,2,1,0:T(8,128)(2,1)}, bf16[4,3,32,128]{3,2,1,0:T(8,128)(2,1)S(1)}, u32[]{:S(2)}) copy-start(bf16[4,3,32,128]{3,2,1,0:T(8,128)(2,1)S(1)} %collective-permute-done.5.refs_3_) | copy-start | bytes 294916
  43.6 11.8 %copy-start.27 = (bf16[4,3,32,128]{3,2,1,0:T(8,128)(2,1)}, bf16[4,3,32,128]{3,2,1,0:T(8,128)(2,1)S(1)}, u32[]{:S(2)}) copy-start(bf16[4,3,32,128]{3,2,1,0:T(8,128)(2,1)S(1)} %collective-permute-done.6.refs_4_) | copy-start | bytes 294916
  46.8 8.6 %copy-start.28 = (bf16[4,3,32,128]{3,2,1,0:T(8,128)(2,1)}, bf16[4,3,32,128]{3,2,1,0:T(8,128)(2,1)S(1)}, u32[]{:S(2)}) copy-start(bf16[4,3,32,128]{3,2,1,0:T(8,128)(2,1)S(1)} %collective-permute-done.7.refs_5_) | copy-start | bytes 294916
  54.1 1.3 copy-start.29
  55.4 0.6 copy-start.30
  58.8 4.5 %collective-permute-start.10 = (bf16[4,2,32,128]{3,2,1,0:T(8,128)(2,1)}, bf16[4,2,32,128]{3,2,1,0:T(8,128)(2,1)S(1)}, u32[]{:S(2)}, u32[]{:S(2)}) collective-permute-start(bf16[4,2,32,128]{3,2,1,0:T(8,128)(2,1)} %get-tuple-element.81), channel_id=1, source_target_pairs={{0,1},{1,0},{2,3},{3,2},{4,5},{5,4},{6,7},{7,6},{8,9},{9,8},{10,11... | collective-permute-start | bytes 196616 | tf_op jit(solution)/shard_map/ppermute | solution.py:456
  59.3 5.3 %collective-permute-start.11 = (bf16[4,2,32,128]{3,2,1,0:T(8,128)(2,1)}, bf16[4,2,32,128]{3,2,1,0:T(8,128)(2,1)S(1)}, u32[]{:S(2)}, u32[]{:S(2)}) collective-permute-start(bf16[4,2,32,128]{3,2,1,0:T(8,128)(2,1)} %get-tuple-element.82), channel_id=1, source_target_pairs={{0,2},{1,3},{2,0},{3,1},{4,6},{5,7},{6,4},{7,5},{8,10},{9,11},{10,... | collective-permute-start | bytes 196616 | tf_op jit(solution)/shard_map/ppermute | solution.py:456
  60.9 4.9 %collective-permute-start.12 = (bf16[4,2,32,128]{3,2,1,0:T(8,128)(2,1)}, bf16[4,2,32,128]{3,2,1,0:T(8,128)(2,1)S(1)}, u32[]{:S(2)}, u32[]{:S(2)}) collective-permute-start(bf16[4,2,32,128]{3,2,1,0:T(8,128)(2,1)} %get-tuple-element.83), channel_id=1, source_target_pairs={{0,3},{1,2},{2,1},{3,0},{4,7},{5,6},{6,5},{7,4},{8,11},{9,10},{10,... | collective-permute-start | bytes 196616 | tf_op jit(solution)/shard_map/ppermute | solution.py:456
  60.9 6.0 %collective-permute-start.13 = (bf16[4,2,32,128]{3,2,1,0:T(8,128)(2,1)}, bf16[4,2,32,128]{3,2,1,0:T(8,128)(2,1)S(1)}, u32[]{:S(2)}, u32[]{:S(2)}) collective-permute-start(bf16[4,2,32,128]{3,2,1,0:T(8,128)(2,1)} %get-tuple-element.84), channel_id=1, source_target_pairs={{0,4},{1,5},{2,6},{3,7},{4,0},{5,1},{6,2},{7,3},{8,12},{9,13},{10,... | collective-permute-start | bytes 196616 | tf_op jit(solution)/shard_map/ppermute | solution.py:456
  63.0 8.9 %collective-permute-start.14 = (bf16[4,2,32,128]{3,2,1,0:T(8,128)(2,1)}, bf16[4,2,32,128]{3,2,1,0:T(8,128)(2,1)S(1)}, u32[]{:S(2)}, u32[]{:S(2)}) collective-permute-start(bf16[4,2,32,128]{3,2,1,0:T(8,128)(2,1)} %get-tuple-element.85), channel_id=1, source_target_pairs={{0,5},{1,4},{2,7},{3,6},{4,1},{5,0},{6,3},{7,2},{8,13},{9,12},{10,... | collective-permute-start | bytes 196616 | tf_op jit(solution)/shard_map/ppermute | solution.py:456
  63.4 8.6 %copy-start.8 = (bf16[4,2,32,128]{3,2,1,0:T(8,128)(2,1)}, bf16[4,2,32,128]{3,2,1,0:T(8,128)(2,1)S(1)}, u32[]{:S(2)}) copy-start(bf16[4,2,32,128]{3,2,1,0:T(8,128)(2,1)S(1)} %collective-permute-done.10.refs_1_) | copy-start | bytes 196612
  63.4 8.6 %collective-permute-start.15 = (bf16[4,2,32,128]{3,2,1,0:T(8,128)(2,1)}, bf16[4,2,32,128]{3,2,1,0:T(8,128)(2,1)S(1)}, u32[]{:S(2)}, u32[]{:S(2)}) collective-permute-start(bf16[4,2,32,128]{3,2,1,0:T(8,128)(2,1)} %get-tuple-element.86), channel_id=1, source_target_pairs={{0,6},{1,7},{2,4},{3,5},{4,2},{5,3},{6,0},{7,1},{8,14},{9,15},{10,... | collective-permute-start | bytes 196616 | tf_op jit(solution)/shard_map/ppermute | solution.py:456
  64.5 7.4 %copy-start.9 = (bf16[4,2,32,128]{3,2,1,0:T(8,128)(2,1)}, bf16[4,2,32,128]{3,2,1,0:T(8,128)(2,1)S(1)}, u32[]{:S(2)}) copy-start(bf16[4,2,32,128]{3,2,1,0:T(8,128)(2,1)S(1)} %collective-permute-done.11.refs_2_) | copy-start | bytes 196612
  64.5 7.4 %collective-permute-start.16 = (bf16[4,2,32,128]{3,2,1,0:T(8,128)(2,1)}, bf16[4,2,32,128]{3,2,1,0:T(8,128)(2,1)S(1)}, u32[]{:S(2)}, u32[]{:S(2)}) collective-permute-start(bf16[4,2,32,128]{3,2,1,0:T(8,128)(2,1)} %get-tuple-element.87), channel_id=1, source_target_pairs={{0,7},{1,6},{2,5},{3,4},{4,3},{5,2},{6,1},{7,0},{8,15},{9,14},{10,... | collective-permute-start | bytes 196616 | tf_op jit(solution)/shard_map/ppermute | solution.py:456
  65.8 6.2 %copy-start.10 = (bf16[4,2,32,128]{3,2,1,0:T(8,128)(2,1)}, bf16[4,2,32,128]{3,2,1,0:T(8,128)(2,1)S(1)}, u32[]{:S(2)}) copy-start(bf16[4,2,32,128]{3,2,1,0:T(8,128)(2,1)S(1)} %collective-permute-done.12.refs_3_) | copy-start | bytes 196612
  66.9 5.1 %copy-start.11 = (bf16[4,2,32,128]{3,2,1,0:T(8,128)(2,1)}, bf16[4,2,32,128]{3,2,1,0:T(8,128)(2,1)S(1)}, u32[]{:S(2)}) copy-start(bf16[4,2,32,128]{3,2,1,0:T(8,128)(2,1)S(1)} %collective-permute-done.13.refs_4_) | copy-start | bytes 196612
  72.0 0.6 copy-start.12
  72.0 0.6 copy-start.13
  72.0 0.7 copy-start.14
  78.3 6.7 %copy-start.1 = (bf16[32,32,1152]{2,1,0:T(8,128)(2,1)}, bf16[32,32,1152]{2,1,0:T(8,128)(2,1)S(1)}, u32[]{:S(2)}) copy-start(bf16[32,32,1152]{2,1,0:T(8,128)(2,1)S(1)} %all-to-all-done.x_ref) | copy-start | bytes 7077892
  78.3 15.4 %collective-permute-start.17 = (bf16[2,8,32,128]{3,2,1,0:T(8,128)(2,1)}, bf16[2,8,32,128]{3,2,1,0:T(8,128)(2,1)S(1)}, u32[]{:S(2)}, u32[]{:S(2)}) collective-permute-start(bf16[2,8,32,128]{3,2,1,0:T(8,128)(2,1)} %get-tuple-element.95), channel_id=1, source_target_pairs={{0,8},{8,0},{16,24},{24,16},{1,9},{9,1},{17,25},{25,17},{2,10},{10... | collective-permute-start | bytes 393224 | tf_op jit(solution)/shard_map/ppermute | solution.py:453
  82.5 12.8 %collective-permute-start.18 = (bf16[2,8,32,128]{3,2,1,0:T(8,128)(2,1)}, bf16[2,8,32,128]{3,2,1,0:T(8,128)(2,1)S(1)}, u32[]{:S(2)}, u32[]{:S(2)}) collective-permute-start(bf16[2,8,32,128]{3,2,1,0:T(8,128)(2,1)} %get-tuple-element.96), channel_id=1, source_target_pairs={{0,16},{8,24},{16,0},{24,8},{1,17},{9,25},{17,1},{25,9},{2,18},{10... | collective-permute-start | bytes 393224 | tf_op jit(solution)/shard_map/ppermute | solution.py:453
  82.5 12.8 %collective-permute-start.19 = (bf16[2,8,32,128]{3,2,1,0:T(8,128)(2,1)}, bf16[2,8,32,128]{3,2,1,0:T(8,128)(2,1)}, u32[]{:S(2)}, u32[]{:S(2)}) collective-permute-start(bf16[2,8,32,128]{3,2,1,0:T(8,128)(2,1)} %get-tuple-element.97), channel_id=1, source_target_pairs={{0,24},{8,16},{16,8},{24,0},{1,25},{9,17},{17,9},{25,1},{2,26},{10... | collective-permute-start | bytes 393224 | tf_op jit(solution)/shard_map/ppermute | solution.py:453
  90.1 5.2 %copy-start.2 = (bf16[6,128,4,258]{1,2,3,0:T(4,128)(2,1)S(1)}, bf16[6,128,4,258]{1,2,3,0:T(4,128)(2,1)}, u32[]{:S(2)}) copy-start(bf16[6,128,4,258]{1,2,3,0:T(4,128)(2,1)} %param.21) | copy-start | bytes 4755460
  90.1 63.9 %all-to-all-start.1 = ((bf16[32,2,32,640]{3,2,1,0:T(8,128)(2,1)}), bf16[32,2,32,640]{3,2,1,0:T(8,128)(2,1)}, u32[]{:S(2)}, u32[]{:S(2)}) async-start(bf16[32,2,32,640]{3,2,1,0:T(8,128)(2,1)} %latitudinal_wide.1), calls=%async_computation.1 | async-start | bytes 5242880 | tf_op jit(solution)/shard_map/all_to_all | solution.py:484
  93.7 2.2 %copy-start.4 = (bf16[3,3,128,128]{3,2,1,0:T(8,128)(2,1)S(1)}, bf16[3,3,128,128]{3,2,1,0:T(8,128)(2,1)}, u32[]{:S(2)}) copy-start(bf16[3,3,128,128]{3,2,1,0:T(8,128)(2,1)} %param.22) | copy-start | bytes 884740
  93.8 1.8 %copy-start.22 = (bf16[2,8,32,128]{3,2,1,0:T(8,128)(2,1)}, bf16[2,8,32,128]{3,2,1,0:T(8,128)(2,1)S(1)}, u32[]{:S(2)}) copy-start(bf16[2,8,32,128]{3,2,1,0:T(8,128)(2,1)S(1)} %collective-permute-done.17.refs_1_) | copy-start | bytes 393220
  95.3 0.7 copy-start.23
  108.2 1.5 copy-start.20
  108.2 2.0 %copy-start.15 = (bf16[768,8]{0,1:T(8,128)(2,1)S(1)}, bf16[768,8]{0,1:T(8,128)(2,1)}, u32[]{:S(2)}) copy-start(bf16[768,8]{0,1:T(8,128)(2,1)} %param.19) | copy-start | bytes 36868
  110.2 16.2 %copy-start.17 = (f32[8,128]{1,0:T(8,128)S(1)}, f32[8,128]{1,0:T(8,128)}, u32[]{:S(2)}) copy-start(f32[8,128]{1,0:T(8,128)} %param.24) | copy-start | bytes 12292
  110.2 16.3 %copy-start.19 = (bf16[8,128]{1,0:T(8,128)(2,1)S(1)}, bf16[8,128]{1,0:T(8,128)(2,1)}, u32[]{:S(2)}) copy-start(bf16[8,128]{1,0:T(8,128)(2,1)} %param.23) | copy-start | bytes 6148
  110.2 16.3 %copy-start.21 = (f32[128]{0:T(128)S(1)}, f32[128]{0:T(128)}, u32[]{:S(2)}) copy-start(f32[128]{0:T(128)} %param.25) | copy-start | bytes 1540
  133.3 9.0 %copy-start.18 = (f32[768]{0:T(1024)S(1)}, f32[768]{0:T(1024)}, u32[]{:S(2)}) copy-start(f32[768]{0:T(1024)} %param.20) | copy-start | bytes 9220

commit v5 on v4

--- a/solution.py
+++ b/solution.py
@@ -225,7 +225,7 @@
         in_specs=[pl.BlockSpec(memory_space=pltpu.SMEM)] + [whole(parts[0])] * sections,
         out_specs=[whole(out)] * plane,
         out_shape=[out] * plane,
-        compiler_params=compiler_params(),
+        compiler_params=compiler_params(63),
         cost_estimate=cost(0, *parts, *parts),
         name="to_plane",
     )(place, *parts)
@@ -248,7 +248,7 @@
         in_specs=[pl.BlockSpec(memory_space=pltpu.SMEM)] + [whole(parts[0])] * plane,
         out_specs=[whole(out)] * sections,
         out_shape=[out] * sections,
-        compiler_params=compiler_params(),
+        compiler_params=compiler_params(63),
         cost_estimate=cost(0, *parts, *parts),
         name="from_plane",
     )(place, *parts)
@@ -288,7 +288,7 @@
         + [whole(parts[0])] * plane,
         out_specs=[whole(joined)] + [whole(out)] * plane,
         out_shape=[joined] + [out] * plane,
-        compiler_params=compiler_params(),
+        compiler_params=compiler_params(63),
         cost_estimate=pl.CostEstimate(flops=10**11, bytes_accessed=3 * 10**8, transcendentals=0),
         name="latitudinal_slim",
     )(position, matrix, damping, *parts)
@@ -453,7 +453,8 @@
             return [lax.ppermute(x, "sec", hops[o]) if o else x for o, x in enumerate(blocks)]
 
         def over_plane(blocks):
-            return [lax.ppermute(x, ("band", "ch"), twists[p]) if p else x for p, x in enumerate(blocks)]
+            moved = {p: lax.ppermute(blocks[p], ("band", "ch"), twists[p]) for p in range(plane - 1, 0, -1)}
+            return [moved.get(p, x) for p, x in enumerate(blocks)]
 
         slim = analyse_slim(air_field_lattice, forward, wide, sec, sec_count, device_count)
         air_after, *slim = lax.optimization_barrier((air_field_lattice, *slim))

time: 160 us -> 160 us (level)
    unnamed x65 -> x61, local copies, waits for them, and re-layouts: 4.93 us -> 4.29 us
where the time goes in v5:
time: 160 us; the launch traced here: 159 us
  waiting for transfers between devices  39.2 us (25%)
  starting transfers between devices  35.1 us (22%)
  Pallas kernels  31.1 us (19%)
  matrix products  24.8 us (16%)
  blocking collectives  19.6 us (12%)
  local copies, waits for them, and re-layouts  7.1 us (4%)
    ppermute x14, waiting for transfers between devices, over_plane(): lax.ppermute(blocks[p], ('band', 'ch'), twists[p])  25.8 us
    dot_general x9, matrix products, ocean_update(): jnp.einsum('io,sirw->sorw', kernel_coefficients[shift_row, shift_col], wi...  13.8 us
    ppermute x14, starting transfers between devices, over_plane(): lax.ppermute(blocks[p], ('band', 'ch'), twists[p])  13.7 us
    all_gather x1, blocking collectives, gather_flux(): return lax.all_gather(flux_local, 'band', axis=1, tiled=True)  12.9 us
    ppermute x6, starting transfers between devices, over_sections(): lax.ppermute(x, 'sec', hops[o])  11.5 us
    all_to_all x2, waiting for transfers between devices, shards(): lax.all_to_all(wide_coeffs, AXES, split_axis=0, concat_axis=0, tiled=True)  10.6 us
    all_to_all x2, starting transfers between devices, shards(): lax.all_to_all(wide_coeffs, AXES, split_axis=0, concat_axis=0, tiled=True)  9.84 us
    dot_general x1, matrix products, ocean_update(): jnp.einsum('io,sirw->sorw', water_readout_matrix, hidden, preferred_eleme...  6.79 us
  transfers between devices with their start and end apart: 22, of which 10 were waited for; matrix products, arithmetic and copies ran while one was open for 19% of the time, Pallas kernels for 14%

profile of v5, /device:TPU:0, one launch (start us, length us, event | category | flops | bytes accessed | tf_op | source)
XLA Modules:
  0.0 159.0 jit_solution(4340492302612926061)
XLA Ops:
  0.7 3.7 %analyse_slim.1 = (bf16[3,8,32,128]{3,2,1,0:T(8,128)(2,1)}, bf16[3,8,32,128]{3,2,1,0:T(8,128)(2,1)}, bf16[3,8,32,128]{3,2,1,0:T(8,128)(2,1)}, bf16[3,8,32,128]{3,2,1,0:T(8,128)(2,1)}) custom-call(s32[1]{0:T(128)} %bitcast.sec_ref, bf16[1024,1024]{1,0:T(8,128)(2,1)} %constant.153.clone.table_ref, bf16[2,1024,768]{2,1,0:T(8,128)(2,1)} %air_ref.2, ...), custom_call_target="tpu_custom_call" | custom-call | flops 805306368 | bytes 3670016 | tf_op jit(solution)/shard_map/analyse_slim/pallas_call | solution.py:143
  4.4 3.0 %collective-permute-start = (bf16[3,8,32,128]{3,2,1,0:T(8,128)(2,1)}, bf16[3,8,32,128]{3,2,1,0:T(8,128)(2,1)S(1)}, u32[]{:S(2)}, u32[]{:S(2)}) collective-permute-start(bf16[3,8,32,128]{3,2,1,0:T(8,128)(2,1)} %get-tuple-element.60), channel_id=1, source_target_pairs={{0,8},{8,0},{16,24},{24,16},{1,9},{9,1},{17,25},{25,17},{2,10},{10... | collective-permute-start | bytes 589832 | tf_op jit(solution)/shard_map/ppermute | solution.py:453
  7.4 2.6 %collective-permute-start.1 = (bf16[3,8,32,128]{3,2,1,0:T(8,128)(2,1)}, bf16[3,8,32,128]{3,2,1,0:T(8,128)(2,1)S(1)}, u32[]{:S(2)}, u32[]{:S(2)}) collective-permute-start(bf16[3,8,32,128]{3,2,1,0:T(8,128)(2,1)} %get-tuple-element.61), channel_id=1, source_target_pairs={{0,16},{8,24},{16,0},{24,8},{1,17},{9,25},{17,1},{25,9},{2,18},{10... | collective-permute-start | bytes 589832 | tf_op jit(solution)/shard_map/ppermute | solution.py:453
  10.0 6.6 %analyse_wide.1 = bf16[32,32,1152]{2,1,0:T(8,128)(2,1)} custom-call(bf16[1024,1024]{1,0:T(8,128)(2,1)} %constant.153.clone.table_ref, bf16[2,1024,768]{2,1,0:T(8,128)(2,1)} %air_ref.2), custom_call_target="tpu_custom_call" | custom-call | flops 2684354560 | bytes 7602176 | tf_op jit(solution)/shard_map/analyse_wide/pallas_call | solution.py:111
  16.6 6.2 %all-to-all-start = ((bf16[32,32,1152]{2,1,0:T(8,128)(2,1)}), bf16[32,32,1152]{2,1,0:T(8,128)(2,1)}, u32[]{:S(2)}, u32[]{:S(2)}) async-start(bf16[32,32,1152]{2,1,0:T(8,128)(2,1)} %analyse_wide.1), calls=%async_computation | async-start | bytes 4718592 | tf_op jit(solution)/shard_map/all_to_all | solution.py:463
  22.8 0.7 pad_add_fusion.position_ref
  23.5 1.3 collective-permute-done.1.refs_2_
  24.8 0.7 copy-done.5
  25.4 0.7 copy-done.6
  26.1 2.2 %to_plane.1 = (bf16[4,3,32,128]{3,2,1,0:T(8,128)(2,1)}, bf16[4,3,32,128]{3,2,1,0:T(8,128)(2,1)}, bf16[4,3,32,128]{3,2,1,0:T(8,128)(2,1)}, bf16[4,3,32,128]{3,2,1...) custom-call(s32[1]{0:T(128)} %bitcast.1.place_ref, ...), custom_call_target="tpu_custom_call" | custom-call | bytes 1572864 | tf_op jit(solution)/shard_map/to_plane/pallas_call | solution.py:222
  28.3 1.5 collective-permute-start.4
  29.9 0.3 collective-permute-start.5
  30.2 1.5 collective-permute-start.6
  31.7 0.2 collective-permute-start.7
  31.9 2.5 %collective-permute-start.8 = (bf16[4,3,32,128]{3,2,1,0:T(8,128)(2,1)}, bf16[4,3,32,128]{3,2,1,0:T(8,128)(2,1)S(1)}, u32[]{:S(2)}, u32[]{:S(2)}) collective-permute-start(bf16[4,3,32,128]{3,2,1,0:T(8,128)(2,1)} %get-tuple-element.78), channel_id=1, source_target_pairs={{0,6},{1,7},{2,4},{3,5},{4,2},{5,3},{6,0},{7,1},{8,14},{9,15},{10,... | collective-permute-start | bytes 294920 | tf_op jit(solution)/shard_map/ppermute | solution.py:456
  34.3 7.6 %collective-permute-done.4.refs_2_ = bf16[4,3,32,128]{3,2,1,0:T(8,128)(2,1)S(1)} collective-permute-done((bf16[4,3,32,128]{3,2,1,0:T(8,128)(2,1)}, bf16[4,3,32,128]{3,2,1,0:T(8,128)(2,1)S(1)}, u32[]{:S(2)}, u32[]{:S(2)}) %collective-permute-start.4) | collective-permute-done | bytes 98336 | tf_op jit(solution)/shard_map/ppermute | solution.py:456
  41.9 0.8 collective-permute-start.9
  42.7 0.9 convolution_convert_fusion.matrix_ref
  43.7 3.1 %collective-permute-done.7.refs_5_ = bf16[4,3,32,128]{3,2,1,0:T(8,128)(2,1)S(1)} collective-permute-done((bf16[4,3,32,128]{3,2,1,0:T(8,128)(2,1)}, bf16[4,3,32,128]{3,2,1,0:T(8,128)(2,1)S(1)}, u32[]{:S(2)}, u32[]{:S(2)}) %collective-permute-start.7) | collective-permute-done | bytes 98336 | tf_op jit(solution)/shard_map/ppermute | solution.py:456
  46.8 7.3 %collective-permute-done.8.refs_6_ = bf16[4,3,32,128]{3,2,1,0:T(8,128)(2,1)S(1)} collective-permute-done((bf16[4,3,32,128]{3,2,1,0:T(8,128)(2,1)}, bf16[4,3,32,128]{3,2,1,0:T(8,128)(2,1)S(1)}, u32[]{:S(2)}, u32[]{:S(2)}) %collective-permute-start.8) | collective-permute-done | bytes 98336 | tf_op jit(solution)/shard_map/ppermute | solution.py:456
  54.1 1.4 collective-permute-done.9.refs_7_
  55.5 2.8 %latitudinal_slim.1 = (bf16[32,32,128]{2,1,0:T(8,128)(2,1)}, bf16[4,2,32,128]{3,2,1,0:T(8,128)(2,1)}, bf16[4,2,32,128]{3,2,1,0:T(8,128)(2,1)}, bf16[4,2,32,128]{...) custom-call(s32[2]{0:T(128)} %pad_add_fusion.position_ref, ...), custom_call_target="tpu_custom_call" | custom-call | flops 99999997952 | bytes 300000000 | tf_op jit(solution)/shard_map/latitudinal_slim/pallas_call | solution.py:280
  58.3 0.5 collective-permute-start.10
  58.8 1.7 %collective-permute-start.11 = (bf16[4,2,32,128]{3,2,1,0:T(8,128)(2,1)}, bf16[4,2,32,128]{3,2,1,0:T(8,128)(2,1)S(1)}, u32[]{:S(2)}, u32[]{:S(2)}) collective-permute-start(bf16[4,2,32,128]{3,2,1,0:T(8,128)(2,1)} %get-tuple-element.82), channel_id=1, source_target_pairs={{0,2},{1,3},{2,0},{3,1},{4,6},{5,7},{6,4},{7,5},{8,10},{9,11},{10,... | collective-permute-start | bytes 196616 | tf_op jit(solution)/shard_map/ppermute | solution.py:456
  60.4 2.1 %collective-permute-start.13 = (bf16[4,2,32,128]{3,2,1,0:T(8,128)(2,1)}, bf16[4,2,32,128]{3,2,1,0:T(8,128)(2,1)S(1)}, u32[]{:S(2)}, u32[]{:S(2)}) collective-permute-start(bf16[4,2,32,128]{3,2,1,0:T(8,128)(2,1)} %get-tuple-element.84), channel_id=1, source_target_pairs={{0,4},{1,5},{2,6},{3,7},{4,0},{5,1},{6,2},{7,3},{8,12},{9,13},{10,... | collective-permute-start | bytes 196616 | tf_op jit(solution)/shard_map/ppermute | solution.py:456
  62.5 0.4 collective-permute-start.14
  62.9 1.2 collective-permute-start.15
  64.1 1.2 collective-permute-start.16
  65.3 1.3 collective-permute-done.13.refs_4_
  66.6 5.0 %collective-permute-done.14.refs_5_ = bf16[4,2,32,128]{3,2,1,0:T(8,128)(2,1)S(1)} collective-permute-done((bf16[4,2,32,128]{3,2,1,0:T(8,128)(2,1)}, bf16[4,2,32,128]{3,2,1,0:T(8,128)(2,1)S(1)}, u32[]{:S(2)}, u32[]{:S(2)}) %collective-permute-start.14) | collective-permute-done | bytes 65568 | tf_op jit(solution)/shard_map/ppermute | solution.py:456
  71.7 0.6 copy-done.11
  72.3 1.9 %from_plane.1 = (bf16[2,8,32,128]{3,2,1,0:T(8,128)(2,1)}, bf16[2,8,32,128]{3,2,1,0:T(8,128)(2,1)}, bf16[2,8,32,128]{3,2,1,0:T(8,128)(2,1)}, bf16[2,8,32,128]{3,2,1,0:T(8,128)(2,1)}) custom-call(s32[1]{0:T(128)} %bitcast.1.place_ref, bf16[4,2,32,128]{3,2,1,0:T(8,128)(2,1)} %get-tuple-element.80.refs_0_, bf16[4,2,32,128]{3,2,1,0:T(8,128)(2,1)} %copy-done.7, ...), custom_call_target="tpu_custom_call" | custom-call | bytes 1048576 | tf_op jit(solution)/shard_map/from_plane/pallas_call | solution.py:245
  74.2 4.2 %all-to-all-done.x_ref = bf16[32,32,1152]{2,1,0:T(8,128)(2,1)} async-done(((bf16[32,32,1152]{2,1,0:T(8,128)(2,1)}), bf16[32,32,1152]{2,1,0:T(8,128)(2,1)}, u32[]{:S(2)}, u32[]{:S(2)}) %all-to-all-start) | async-done | bytes 2359328 | tf_op jit(solution)/shard_map/all_to_all | solution.py:463
  78.4 3.4 %collective-permute-start.17 = (bf16[2,8,32,128]{3,2,1,0:T(8,128)(2,1)}, bf16[2,8,32,128]{3,2,1,0:T(8,128)(2,1)S(1)}, u32[]{:S(2)}, u32[]{:S(2)}) collective-permute-start(bf16[2,8,32,128]{3,2,1,0:T(8,128)(2,1)} %get-tuple-element.95), channel_id=1, source_target_pairs={{0,8},{8,0},{16,24},{24,16},{1,9},{9,1},{17,25},{25,17},{2,10},{10... | collective-permute-start | bytes 393224 | tf_op jit(solution)/shard_map/ppermute | solution.py:453
  81.8 2.4 %collective-permute-start.19 = (bf16[2,8,32,128]{3,2,1,0:T(8,128)(2,1)}, bf16[2,8,32,128]{3,2,1,0:T(8,128)(2,1)}, u32[]{:S(2)}, u32[]{:S(2)}) collective-permute-start(bf16[2,8,32,128]{3,2,1,0:T(8,128)(2,1)} %get-tuple-element.97), channel_id=1, source_target_pairs={{0,24},{8,16},{16,8},{24,0},{1,25},{9,17},{17,9},{25,1},{2,26},{10... | collective-permute-start | bytes 393224 | tf_op jit(solution)/shard_map/ppermute | solution.py:453
  84.3 5.0 %latitudinal_wide.1 = bf16[32,2,32,640]{3,2,1,0:T(8,128)(2,1)} custom-call(bf16[32,32,1152]{2,1,0:T(8,128)(2,1)} %all-to-all-done.x_ref, bf16[32,32,128]{2,1,0:T(8,128)(2,1)} %get-tuple-element.93.joined_ref, bf16[16,64,64]{2,1,0:T(8,128)(2,1)} %matrix_ref.1, f32[64,768]{1,0:T(8,128)} %damping_ref.3), custom_call_target="tpu_custom_call" | custom-call | flops 335544320 | bytes 4849664 | tf_op jit(solution)/shard_map/latitudinal_wide/pallas_call | solution.py:190
  89.4 3.7 %all-to-all-start.1 = ((bf16[32,2,32,640]{3,2,1,0:T(8,128)(2,1)}), bf16[32,2,32,640]{3,2,1,0:T(8,128)(2,1)}, u32[]{:S(2)}, u32[]{:S(2)}) async-start(bf16[32,2,32,640]{3,2,1,0:T(8,128)(2,1)} %latitudinal_wide.1), calls=%async_computation.1 | async-start | bytes 5242880 | tf_op jit(solution)/shard_map/all_to_all | solution.py:485
  93.0 1.5 collective-permute-done.18.refs_2_
  94.6 0.2 copy.95
  94.8 0.4 copy-done.22
  95.3 1.5 fusion.14
  96.8 1.5 fusion.16
  98.3 1.6 fusion.18
  99.9 1.5 fusion.20
  101.4 1.5 fusion.36
  102.9 1.6 fusion.22
  104.5 1.5 fusion.24
  106.0 1.5 fusion.26
  107.5 1.5 fusion.28
  109.1 0.1 copy.96
  109.3 0.2 reduce_window_sum.11
  109.6 2.8 %fusion.12 = bf16[8,2,1024]{2,0,1:T(8,128)(2,1)S(1)} fusion(bf16[2,1024,768]{2,1,0:T(8,128)(2,1)} %air_ref.2, bf16[768,8]{0,1:T(8,128)(2,1)S(1)} %copy-done.14), kind=kOutput, calls=%fused_computation.17 | convolution fusion | flops 25182208 | bytes 3190784 | tf_op jit(solution)/shard_map/anc,cf->fan/dot_general | solution.py:398
  112.4 12.9 %all_gather.6 = bf16[8,8,1024]{2,0,1:T(8,128)(2,1)S(1)} all-gather(bf16[8,2,1024]{2,0,1:T(8,128)(2,1)S(1)} %fusion.12), channel_id=1, replica_groups=mesh['sec'=4,'band'=4,'ch'=2] {'band'}, dimensions={1}, use_global_device_ids=true | all-gather | bytes 163840 | tf_op jit(solution)/shard_map/all_gather | solution.py:404
  125.5 0.3 convert_reduce_fusion
  126.0 6.8 %fusion.9 = bf16[6,128,2,256]{1,3,2,0:T(8,128)(2,1)S(1)} fusion(f32[6,2,256,128]{3,2,1,0:T(8,128)} %fusion.14, f32[6,2,256,128]{3,2,1,0:T(8,128)} %fusion.16, f32[6,2,256,128]{3,2,1,0:T(8,128)} %fusion.18, f32[6,2,256,128]{3,2,1,0:T(8,128)} %fusion.20, f32[6,2,256,128]{3,2,1,0:T(8,128)} %fusion.36, f32[6,2,256,128]{3,2,1,0:T(8,128)} %fusion.22, ...), kind=kOutput, calls=%fused_computation.11 | convolution fusion | flops 116391936 | bytes 15828480 | tf_op jit(solution)/shard_map/io,sirw->sorw/dot_general | solution.py:74
  132.8 1.8 %copy.115 = bf16[6,128,2,256]{3,2,1,0:T(2,128)(2,1)} copy(bf16[6,128,2,256]{1,3,2,0:T(8,128)(2,1)S(1)} %fusion.9) | data formatting | bytes 1572864
  134.6 0.3 copy.113
  134.9 6.6 %all-gather = bf16[24,1,2,256]{3,2,1,0:T(2,128)(2,1)S(1)} all-gather(bf16[6,1,2,256]{3,2,1,0:T(2,128)(2,1)S(1)} %copy.113), channel_id=2, replica_groups=mesh['sec'=4,'band'=4,'ch'=2] {'band'}, dimensions={0}, use_global_device_ids=true | all-gather | bytes 30720 | tf_op jit(solution)/shard_map/all_gather | solution.py:542
  141.6 0.2 fusion.13
  141.9 1.2 stack.33.warmth_ref
  143.2 0.6 broadcast_in_dim.9.sea_ref
  143.8 3.0 %synthesise_slim.1.begun_ref = bf16[2,2,512,768]{3,2,1,0:T(8,128)(2,1)} custom-call(s32[1]{0:T(128)} %bitcast.sec_ref, bf16[2,512,512]{2,1,0:T(8,128)(2,1)} %constant.154.clone.table_ref, bf16[2,2,512,768]{3,2,1,0:T(8,128)(2,1)} %bitcast.125, bf16[2,2,16,512]{3,2,1,0:T(8,128)(2,1)} %broadcast_in_dim.9.sea_ref, bf16[16,768]{1,0:T(8,128)(2,1)} %stack.33.warmth_ref, ...), custom_call_target="tpu_custom_call" | custom-call | flops 99999997952 | bytes 300000000 | tf_op jit(solution)/shard_map/synthesise_slim/pallas_call | solution.py:338
  146.8 6.4 %all-to-all-done.1.coeff_ref = bf16[32,2,32,640]{3,2,1,0:T(8,128)(2,1)} async-done(((bf16[32,2,32,640]{3,2,1,0:T(8,128)(2,1)}), bf16[32,2,32,640]{3,2,1,0:T(8,128)(2,1)}, u32[]{:S(2)}, u32[]{:S(2)}) %all-to-all-start.1) | async-done | bytes 2621472 | tf_op jit(solution)/shard_map/all_to_all | solution.py:485
  153.2 5.8 %synthesise_wide.1 = bf16[2,2,512,768]{3,2,1,0:T(8,128)(2,1)} custom-call(bf16[2,512,512]{2,1,0:T(8,128)(2,1)} %constant.154.clone.table_ref, bf16[32,2,32,640]{3,2,1,0:T(8,128)(2,1)} %all-to-all-done.1.coeff_ref, bf16[2,2,512,768]{3,2,1,0:T(8,128)(2,1)} %bitcast.126, ...), custom_call_target="tpu_custom_call", output_to_operand_aliasing={{}: (5, {})} | custom-call | flops 1342177280 | bytes 8912896 | tf_op jit(solution)/shard_map/synthesise_wide/pallas_call | solution.py:377
  (96 shorter events, 0.9 us)
Async XLA Ops:
  0.6 125.4 %copy-start = (bf16[128,128]{1,0:T(8,128)(2,1)S(1)}, bf16[128,128]{1,0:T(8,128)(2,1)}, u32[]{:S(2)}) copy-start(bf16[128,128]{1,0:T(8,128)(2,1)} %param.26) | copy-start | bytes 98308
  4.4 19.1 %collective-permute-start = (bf16[3,8,32,128]{3,2,1,0:T(8,128)(2,1)}, bf16[3,8,32,128]{3,2,1,0:T(8,128)(2,1)S(1)}, u32[]{:S(2)}, u32[]{:S(2)}) collective-permute-start(bf16[3,8,32,128]{3,2,1,0:T(8,128)(2,1)} %get-tuple-element.60), channel_id=1, source_target_pairs={{0,8},{8,0},{16,24},{24,16},{1,9},{9,1},{17,25},{25,17},{2,10},{10... | collective-permute-start | bytes 589832 | tf_op jit(solution)/shard_map/ppermute | solution.py:453
  7.4 17.4 %collective-permute-start.1 = (bf16[3,8,32,128]{3,2,1,0:T(8,128)(2,1)}, bf16[3,8,32,128]{3,2,1,0:T(8,128)(2,1)S(1)}, u32[]{:S(2)}, u32[]{:S(2)}) collective-permute-start(bf16[3,8,32,128]{3,2,1,0:T(8,128)(2,1)} %get-tuple-element.61), channel_id=1, source_target_pairs={{0,16},{8,24},{16,0},{24,8},{1,17},{9,25},{17,1},{25,9},{2,18},{10... | collective-permute-start | bytes 589832 | tf_op jit(solution)/shard_map/ppermute | solution.py:453
  10.0 14.8 %collective-permute-start.2 = (bf16[3,8,32,128]{3,2,1,0:T(8,128)(2,1)}, bf16[3,8,32,128]{3,2,1,0:T(8,128)(2,1)S(1)}, u32[]{:S(2)}, u32[]{:S(2)}) collective-permute-start(bf16[3,8,32,128]{3,2,1,0:T(8,128)(2,1)} %get-tuple-element.62), channel_id=1, source_target_pairs={{0,24},{8,16},{16,8},{24,0},{1,25},{9,17},{17,9},{25,1},{2,26},{10... | collective-permute-start | bytes 589832 | tf_op jit(solution)/shard_map/ppermute | solution.py:453
  16.6 26.1 %copy-start.2 = (bf16[16,64,64]{2,1,0:T(8,128)(2,1)S(1)}, bf16[16,64,64]{2,1,0:T(8,128)(2,1)}, u32[]{:S(2)}) copy-start(bf16[16,64,64]{2,1,0:T(8,128)(2,1)} %matrix_ref.1) | copy-start | bytes 393220
  16.6 61.8 %all-to-all-start = ((bf16[32,32,1152]{2,1,0:T(8,128)(2,1)}), bf16[32,32,1152]{2,1,0:T(8,128)(2,1)}, u32[]{:S(2)}, u32[]{:S(2)}) async-start(bf16[32,32,1152]{2,1,0:T(8,128)(2,1)} %analyse_wide.1), calls=%async_computation | async-start | bytes 4718592 | tf_op jit(solution)/shard_map/all_to_all | solution.py:463
  23.5 1.3 copy-start.4
  24.8 0.7 copy-start.5
  25.4 0.7 copy-start.6
  28.3 3.6 %collective-permute-start.3 = (bf16[4,3,32,128]{3,2,1,0:T(8,128)(2,1)}, bf16[4,3,32,128]{3,2,1,0:T(8,128)(2,1)S(1)}, u32[]{:S(2)}, u32[]{:S(2)}) collective-permute-start(bf16[4,3,32,128]{3,2,1,0:T(8,128)(2,1)} %get-tuple-element.73), channel_id=1, source_target_pairs={{0,1},{1,0},{2,3},{3,2},{4,5},{5,4},{6,7},{7,6},{8,9},{9,8},{10,11... | collective-permute-start | bytes 294920 | tf_op jit(solution)/shard_map/ppermute | solution.py:456
  28.3 13.6 %collective-permute-start.4 = (bf16[4,3,32,128]{3,2,1,0:T(8,128)(2,1)}, bf16[4,3,32,128]{3,2,1,0:T(8,128)(2,1)S(1)}, u32[]{:S(2)}, u32[]{:S(2)}) collective-permute-start(bf16[4,3,32,128]{3,2,1,0:T(8,128)(2,1)} %get-tuple-element.74), channel_id=1, source_target_pairs={{0,2},{1,3},{2,0},{3,1},{4,6},{5,7},{6,4},{7,5},{8,10},{9,11},{10,... | collective-permute-start | bytes 294920 | tf_op jit(solution)/shard_map/ppermute | solution.py:456
  29.9 13.8 %collective-permute-start.5 = (bf16[4,3,32,128]{3,2,1,0:T(8,128)(2,1)}, bf16[4,3,32,128]{3,2,1,0:T(8,128)(2,1)S(1)}, u32[]{:S(2)}, u32[]{:S(2)}) collective-permute-start(bf16[4,3,32,128]{3,2,1,0:T(8,128)(2,1)} %get-tuple-element.75), channel_id=1, source_target_pairs={{0,3},{1,2},{2,1},{3,0},{4,7},{5,6},{6,5},{7,4},{8,11},{9,10},{10,... | collective-permute-start | bytes 294920 | tf_op jit(solution)/shard_map/ppermute | solution.py:456
  30.2 13.5 %collective-permute-start.6 = (bf16[4,3,32,128]{3,2,1,0:T(8,128)(2,1)}, bf16[4,3,32,128]{3,2,1,0:T(8,128)(2,1)S(1)}, u32[]{:S(2)}, u32[]{:S(2)}) collective-permute-start(bf16[4,3,32,128]{3,2,1,0:T(8,128)(2,1)} %get-tuple-element.76), channel_id=1, source_target_pairs={{0,4},{1,5},{2,6},{3,7},{4,0},{5,1},{6,2},{7,3},{8,12},{9,13},{10,... | collective-permute-start | bytes 294920 | tf_op jit(solution)/shard_map/ppermute | solution.py:456
  31.7 15.1 %collective-permute-start.7 = (bf16[4,3,32,128]{3,2,1,0:T(8,128)(2,1)}, bf16[4,3,32,128]{3,2,1,0:T(8,128)(2,1)S(1)}, u32[]{:S(2)}, u32[]{:S(2)}) collective-permute-start(bf16[4,3,32,128]{3,2,1,0:T(8,128)(2,1)} %get-tuple-element.77), channel_id=1, source_target_pairs={{0,5},{1,4},{2,7},{3,6},{4,1},{5,0},{6,3},{7,2},{8,13},{9,12},{10,... | collective-permute-start | bytes 294920 | tf_op jit(solution)/shard_map/ppermute | solution.py:456
  31.9 23.6 %copy-start.23 = (bf16[4,3,32,128]{3,2,1,0:T(8,128)(2,1)}, bf16[4,3,32,128]{3,2,1,0:T(8,128)(2,1)S(1)}, u32[]{:S(2)}) copy-start(bf16[4,3,32,128]{3,2,1,0:T(8,128)(2,1)S(1)} %collective-permute-done.3.refs_1_) | copy-start | bytes 294916
  31.9 22.2 %collective-permute-start.8 = (bf16[4,3,32,128]{3,2,1,0:T(8,128)(2,1)}, bf16[4,3,32,128]{3,2,1,0:T(8,128)(2,1)S(1)}, u32[]{:S(2)}, u32[]{:S(2)}) collective-permute-start(bf16[4,3,32,128]{3,2,1,0:T(8,128)(2,1)} %get-tuple-element.78), channel_id=1, source_target_pairs={{0,6},{1,7},{2,4},{3,5},{4,2},{5,3},{6,0},{7,1},{8,14},{9,15},{10,... | collective-permute-start | bytes 294920 | tf_op jit(solution)/shard_map/ppermute | solution.py:456
  41.9 13.6 %copy-start.24 = (bf16[4,3,32,128]{3,2,1,0:T(8,128)(2,1)}, bf16[4,3,32,128]{3,2,1,0:T(8,128)(2,1)S(1)}, u32[]{:S(2)}) copy-start(bf16[4,3,32,128]{3,2,1,0:T(8,128)(2,1)S(1)} %collective-permute-done.4.refs_2_) | copy-start | bytes 294916
  41.9 13.5 %collective-permute-start.9 = (bf16[4,3,32,128]{3,2,1,0:T(8,128)(2,1)}, bf16[4,3,32,128]{3,2,1,0:T(8,128)(2,1)}, u32[]{:S(2)}, u32[]{:S(2)}) collective-permute-start(bf16[4,3,32,128]{3,2,1,0:T(8,128)(2,1)} %get-tuple-element.79), channel_id=1, source_target_pairs={{0,7},{1,6},{2,5},{3,4},{4,3},{5,2},{6,1},{7,0},{8,15},{9,14},{10,... | collective-permute-start | bytes 294920 | tf_op jit(solution)/shard_map/ppermute | solution.py:456
  43.7 21.6 %copy-start.15 = (s32[6,2,256]{2,1,0:T(2,128)S(1)}, s32[6,2,256]{2,1,0:T(2,128)}, u32[]{:S(2)}) copy-start(s32[6,2,256]{2,1,0:T(2,128)} %param.28) | copy-start | bytes 36868
  43.7 40.6 %copy-start.29 = (s32[6]{0:T(128)S(1)}, s32[6]{0:T(128)}, u32[]{:S(2)}) copy-start(s32[6]{0:T(128)} %param.29) | copy-start | bytes 76
  43.7 11.8 %copy-start.25 = (bf16[4,3,32,128]{3,2,1,0:T(8,128)(2,1)}, bf16[4,3,32,128]{3,2,1,0:T(8,128)(2,1)S(1)}, u32[]{:S(2)}) copy-start(bf16[4,3,32,128]{3,2,1,0:T(8,128)(2,1)S(1)} %collective-permute-done.5.refs_3_) | copy-start | bytes 294916
  43.7 11.8 %copy-start.26 = (bf16[4,3,32,128]{3,2,1,0:T(8,128)(2,1)}, bf16[4,3,32,128]{3,2,1,0:T(8,128)(2,1)S(1)}, u32[]{:S(2)}) copy-start(bf16[4,3,32,128]{3,2,1,0:T(8,128)(2,1)S(1)} %collective-permute-done.6.refs_4_) | copy-start | bytes 294916
  46.8 8.7 %copy-start.27 = (bf16[4,3,32,128]{3,2,1,0:T(8,128)(2,1)}, bf16[4,3,32,128]{3,2,1,0:T(8,128)(2,1)S(1)}, u32[]{:S(2)}) copy-start(bf16[4,3,32,128]{3,2,1,0:T(8,128)(2,1)S(1)} %collective-permute-done.7.refs_5_) | copy-start | bytes 294916
  54.1 1.4 copy-start.28
  58.3 4.6 %collective-permute-start.10 = (bf16[4,2,32,128]{3,2,1,0:T(8,128)(2,1)}, bf16[4,2,32,128]{3,2,1,0:T(8,128)(2,1)S(1)}, u32[]{:S(2)}, u32[]{:S(2)}) collective-permute-start(bf16[4,2,32,128]{3,2,1,0:T(8,128)(2,1)} %get-tuple-element.81), channel_id=1, source_target_pairs={{0,1},{1,0},{2,3},{3,2},{4,5},{5,4},{6,7},{7,6},{8,9},{9,8},{10,11... | collective-permute-start | bytes 196616 | tf_op jit(solution)/shard_map/ppermute | solution.py:456
  58.8 5.3 %collective-permute-start.11 = (bf16[4,2,32,128]{3,2,1,0:T(8,128)(2,1)}, bf16[4,2,32,128]{3,2,1,0:T(8,128)(2,1)S(1)}, u32[]{:S(2)}, u32[]{:S(2)}) collective-permute-start(bf16[4,2,32,128]{3,2,1,0:T(8,128)(2,1)} %get-tuple-element.82), channel_id=1, source_target_pairs={{0,2},{1,3},{2,0},{3,1},{4,6},{5,7},{6,4},{7,5},{8,10},{9,11},{10,... | collective-permute-start | bytes 196616 | tf_op jit(solution)/shard_map/ppermute | solution.py:456
  60.4 4.9 %collective-permute-start.12 = (bf16[4,2,32,128]{3,2,1,0:T(8,128)(2,1)}, bf16[4,2,32,128]{3,2,1,0:T(8,128)(2,1)S(1)}, u32[]{:S(2)}, u32[]{:S(2)}) collective-permute-start(bf16[4,2,32,128]{3,2,1,0:T(8,128)(2,1)} %get-tuple-element.83), channel_id=1, source_target_pairs={{0,3},{1,2},{2,1},{3,0},{4,7},{5,6},{6,5},{7,4},{8,11},{9,10},{10,... | collective-permute-start | bytes 196616 | tf_op jit(solution)/shard_map/ppermute | solution.py:456
  60.4 6.2 %collective-permute-start.13 = (bf16[4,2,32,128]{3,2,1,0:T(8,128)(2,1)}, bf16[4,2,32,128]{3,2,1,0:T(8,128)(2,1)S(1)}, u32[]{:S(2)}, u32[]{:S(2)}) collective-permute-start(bf16[4,2,32,128]{3,2,1,0:T(8,128)(2,1)} %get-tuple-element.84), channel_id=1, source_target_pairs={{0,4},{1,5},{2,6},{3,7},{4,0},{5,1},{6,2},{7,3},{8,12},{9,13},{10,... | collective-permute-start | bytes 196616 | tf_op jit(solution)/shard_map/ppermute | solution.py:456
  62.5 9.1 %collective-permute-start.14 = (bf16[4,2,32,128]{3,2,1,0:T(8,128)(2,1)}, bf16[4,2,32,128]{3,2,1,0:T(8,128)(2,1)S(1)}, u32[]{:S(2)}, u32[]{:S(2)}) collective-permute-start(bf16[4,2,32,128]{3,2,1,0:T(8,128)(2,1)} %get-tuple-element.85), channel_id=1, source_target_pairs={{0,5},{1,4},{2,7},{3,6},{4,1},{5,0},{6,3},{7,2},{8,13},{9,12},{10,... | collective-permute-start | bytes 196616 | tf_op jit(solution)/shard_map/ppermute | solution.py:456
  62.9 8.8 %copy-start.7 = (bf16[4,2,32,128]{3,2,1,0:T(8,128)(2,1)}, bf16[4,2,32,128]{3,2,1,0:T(8,128)(2,1)S(1)}, u32[]{:S(2)}) copy-start(bf16[4,2,32,128]{3,2,1,0:T(8,128)(2,1)S(1)} %collective-permute-done.10.refs_1_) | copy-start | bytes 196612
  62.9 8.8 %collective-permute-start.15 = (bf16[4,2,32,128]{3,2,1,0:T(8,128)(2,1)}, bf16[4,2,32,128]{3,2,1,0:T(8,128)(2,1)S(1)}, u32[]{:S(2)}, u32[]{:S(2)}) collective-permute-start(bf16[4,2,32,128]{3,2,1,0:T(8,128)(2,1)} %get-tuple-element.86), channel_id=1, source_target_pairs={{0,6},{1,7},{2,4},{3,5},{4,2},{5,3},{6,0},{7,1},{8,14},{9,15},{10,... | collective-permute-start | bytes 196616 | tf_op jit(solution)/shard_map/ppermute | solution.py:456
  64.1 7.6 %copy-start.8 = (bf16[4,2,32,128]{3,2,1,0:T(8,128)(2,1)}, bf16[4,2,32,128]{3,2,1,0:T(8,128)(2,1)S(1)}, u32[]{:S(2)}) copy-start(bf16[4,2,32,128]{3,2,1,0:T(8,128)(2,1)S(1)} %collective-permute-done.11.refs_2_) | copy-start | bytes 196612
  64.1 7.6 %collective-permute-start.16 = (bf16[4,2,32,128]{3,2,1,0:T(8,128)(2,1)}, bf16[4,2,32,128]{3,2,1,0:T(8,128)(2,1)S(1)}, u32[]{:S(2)}, u32[]{:S(2)}) collective-permute-start(bf16[4,2,32,128]{3,2,1,0:T(8,128)(2,1)} %get-tuple-element.87), channel_id=1, source_target_pairs={{0,7},{1,6},{2,5},{3,4},{4,3},{5,2},{6,1},{7,0},{8,15},{9,14},{10,... | collective-permute-start | bytes 196616 | tf_op jit(solution)/shard_map/ppermute | solution.py:456
  65.3 6.4 %copy-start.9 = (bf16[4,2,32,128]{3,2,1,0:T(8,128)(2,1)}, bf16[4,2,32,128]{3,2,1,0:T(8,128)(2,1)S(1)}, u32[]{:S(2)}) copy-start(bf16[4,2,32,128]{3,2,1,0:T(8,128)(2,1)S(1)} %collective-permute-done.12.refs_3_) | copy-start | bytes 196612
  66.6 5.1 %copy-start.10 = (bf16[4,2,32,128]{3,2,1,0:T(8,128)(2,1)}, bf16[4,2,32,128]{3,2,1,0:T(8,128)(2,1)S(1)}, u32[]{:S(2)}) copy-start(bf16[4,2,32,128]{3,2,1,0:T(8,128)(2,1)S(1)} %collective-permute-done.13.refs_4_) | copy-start | bytes 196612
  71.7 0.6 copy-start.11
  71.7 0.6 copy-start.12
  71.7 0.7 copy-start.13
  78.4 14.6 %collective-permute-start.17 = (bf16[2,8,32,128]{3,2,1,0:T(8,128)(2,1)}, bf16[2,8,32,128]{3,2,1,0:T(8,128)(2,1)S(1)}, u32[]{:S(2)}, u32[]{:S(2)}) collective-permute-start(bf16[2,8,32,128]{3,2,1,0:T(8,128)(2,1)} %get-tuple-element.95), channel_id=1, source_target_pairs={{0,8},{8,0},{16,24},{24,16},{1,9},{9,1},{17,25},{25,17},{2,10},{10... | collective-permute-start | bytes 393224 | tf_op jit(solution)/shard_map/ppermute | solution.py:453
  81.8 12.8 %collective-permute-start.18 = (bf16[2,8,32,128]{3,2,1,0:T(8,128)(2,1)}, bf16[2,8,32,128]{3,2,1,0:T(8,128)(2,1)S(1)}, u32[]{:S(2)}, u32[]{:S(2)}) collective-permute-start(bf16[2,8,32,128]{3,2,1,0:T(8,128)(2,1)} %get-tuple-element.96), channel_id=1, source_target_pairs={{0,16},{8,24},{16,0},{24,8},{1,17},{9,25},{17,1},{25,9},{2,18},{10... | collective-permute-start | bytes 393224 | tf_op jit(solution)/shard_map/ppermute | solution.py:453
  81.8 12.8 %collective-permute-start.19 = (bf16[2,8,32,128]{3,2,1,0:T(8,128)(2,1)}, bf16[2,8,32,128]{3,2,1,0:T(8,128)(2,1)}, u32[]{:S(2)}, u32[]{:S(2)}) collective-permute-start(bf16[2,8,32,128]{3,2,1,0:T(8,128)(2,1)} %get-tuple-element.97), channel_id=1, source_target_pairs={{0,24},{8,16},{16,8},{24,0},{1,25},{9,17},{17,9},{25,1},{2,26},{10... | collective-permute-start | bytes 393224 | tf_op jit(solution)/shard_map/ppermute | solution.py:453
  89.3 5.3 %copy-start.1 = (bf16[6,128,4,258]{1,2,3,0:T(4,128)(2,1)S(1)}, bf16[6,128,4,258]{1,2,3,0:T(4,128)(2,1)}, u32[]{:S(2)}) copy-start(bf16[6,128,4,258]{1,2,3,0:T(4,128)(2,1)} %param.21) | copy-start | bytes 4755460
  89.4 63.9 %all-to-all-start.1 = ((bf16[32,2,32,640]{3,2,1,0:T(8,128)(2,1)}), bf16[32,2,32,640]{3,2,1,0:T(8,128)(2,1)}, u32[]{:S(2)}, u32[]{:S(2)}) async-start(bf16[32,2,32,640]{3,2,1,0:T(8,128)(2,1)} %latitudinal_wide.1), calls=%async_computation.1 | async-start | bytes 5242880 | tf_op jit(solution)/shard_map/all_to_all | solution.py:485
  93.0 2.2 %copy-start.3 = (bf16[3,3,128,128]{3,2,1,0:T(8,128)(2,1)S(1)}, bf16[3,3,128,128]{3,2,1,0:T(8,128)(2,1)}, u32[]{:S(2)}) copy-start(bf16[3,3,128,128]{3,2,1,0:T(8,128)(2,1)} %param.22) | copy-start | bytes 884740
  93.0 1.8 %copy-start.21 = (bf16[2,8,32,128]{3,2,1,0:T(8,128)(2,1)}, bf16[2,8,32,128]{3,2,1,0:T(8,128)(2,1)S(1)}, u32[]{:S(2)}) copy-start(bf16[2,8,32,128]{3,2,1,0:T(8,128)(2,1)S(1)} %collective-permute-done.17.refs_1_) | copy-start | bytes 393220
  94.6 0.7 copy-start.22
  107.5 1.5 copy-start.19
  107.5 2.0 %copy-start.14 = (bf16[768,8]{0,1:T(8,128)(2,1)S(1)}, bf16[768,8]{0,1:T(8,128)(2,1)}, u32[]{:S(2)}) copy-start(bf16[768,8]{0,1:T(8,128)(2,1)} %param.19) | copy-start | bytes 36868
  109.5 16.4 %copy-start.16 = (f32[8,128]{1,0:T(8,128)S(1)}, f32[8,128]{1,0:T(8,128)}, u32[]{:S(2)}) copy-start(f32[8,128]{1,0:T(8,128)} %param.24) | copy-start | bytes 12292
  109.5 16.5 %copy-start.18 = (bf16[8,128]{1,0:T(8,128)(2,1)S(1)}, bf16[8,128]{1,0:T(8,128)(2,1)}, u32[]{:S(2)}) copy-start(bf16[8,128]{1,0:T(8,128)(2,1)} %param.23) | copy-start | bytes 6148
  109.6 16.5 %copy-start.20 = (f32[128]{0:T(128)S(1)}, f32[128]{0:T(128)}, u32[]{:S(2)}) copy-start(f32[128]{0:T(128)} %param.25) | copy-start | bytes 1540
  132.8 9.0 %copy-start.17 = (f32[768]{0:T(1024)S(1)}, f32[768]{0:T(1024)}, u32[]{:S(2)}) copy-start(f32[768]{0:T(1024)} %param.20) | copy-start | bytes 9220

commit v6 on v5

--- a/solution.py
+++ b/solution.py
@@ -217,7 +217,7 @@
         for p, out_ref in enumerate(refs[sections:]):
             for o in range(sections):
                 for a in range(lines):
-                    out_ref[o, a] = refs[o][a, place_ref[0] ^ p]
+                    out_ref[o, a] = refs[sections - 1 - o][a, place_ref[0] ^ p]
 
     return pl.pallas_call(
         body,
@@ -228,7 +228,7 @@
         compiler_params=compiler_params(63),
         cost_estimate=cost(0, *parts, *parts),
         name="to_plane",
-    )(place, *parts)
+    )(place, *parts[::-1])
 
 
 def from_plane(parts, place):

time: 160 us -> 158 us (0.988)
  starting transfers between devices: 35.1 us -> 33.5 us
    all_to_all x2, waiting for transfers between devices: 10.6 us -> 8.97 us  [shards(): lax.all_to_all(wide_coeffs, AXES, split_axis=0, concat_axis=0, tiled=True)]
  transfers between devices with their start and end apart: 22 -> 22, of which waited for: 10 -> 11; matrix products, arithmetic and copies ran while one was open for 19% -> 19% of each run, Pallas kernels for 14% -> 14%
where the time goes in v6:
time: 158 us
  waiting for transfers between devices  37.9 us (24%)
  starting transfers between devices  33.5 us (21%)
  Pallas kernels  31.1 us (20%)
  matrix products  24.8 us (16%)
  blocking collectives  20.7 us (13%)
  local copies, waits for them, and re-layouts  7.45 us (5%)
    ppermute x14, waiting for transfers between devices, over_plane(): lax.ppermute(blocks[p], ('band', 'ch'), twists[p])  26 us
    all_gather x1, blocking collectives, gather_flux(): return lax.all_gather(flux_local, 'band', axis=1, tiled=True)  14.1 us
    dot_general x9, matrix products, ocean_update(): jnp.einsum('io,sirw->sorw', kernel_coefficients[shift_row, shift_col], wi...  13.8 us
    ppermute x14, starting transfers between devices, over_plane(): lax.ppermute(blocks[p], ('band', 'ch'), twists[p])  12.9 us
    all_to_all x2, starting transfers between devices, shards(): lax.all_to_all(wide_coeffs, AXES, split_axis=0, concat_axis=0, tiled=True)  10.6 us
    ppermute x6, starting transfers between devices, over_sections(): lax.ppermute(x, 'sec', hops[o])  10 us
    all_to_all x2, waiting for transfers between devices, shards(): lax.all_to_all(wide_coeffs, AXES, split_axis=0, concat_axis=0, tiled=True)  8.97 us
    dot_general x1, matrix products, ocean_update(): jnp.einsum('io,sirw->sorw', water_readout_matrix, hidden, preferred_eleme...  6.79 us
  transfers between devices with their start and end apart: 22, of which 11 were waited for; matrix products, arithmetic and copies ran while one was open for 19% of the time, Pallas kernels for 14%

profile of v6, /device:TPU:0, one launch (start us, length us, event | category | flops | bytes accessed | tf_op | source)
XLA Modules:
  0.0 157.6 jit_solution(3476811784320628124)
XLA Ops:
  0.7 3.7 %analyse_slim.1 = (bf16[3,8,32,128]{3,2,1,0:T(8,128)(2,1)}, bf16[3,8,32,128]{3,2,1,0:T(8,128)(2,1)}, bf16[3,8,32,128]{3,2,1,0:T(8,128)(2,1)}, bf16[3,8,32,128]{3,2,1,0:T(8,128)(2,1)}) custom-call(s32[1]{0:T(128)} %bitcast.sec_ref, bf16[1024,1024]{1,0:T(8,128)(2,1)} %constant.153.clone.table_ref, bf16[2,1024,768]{2,1,0:T(8,128)(2,1)} %air_ref.2, ...), custom_call_target="tpu_custom_call" | custom-call | flops 805306368 | bytes 3670016 | tf_op jit(solution)/shard_map/analyse_slim/pallas_call | solution.py:143
  4.4 5.0 %collective-permute-start = (bf16[3,8,32,128]{3,2,1,0:T(8,128)(2,1)}, bf16[3,8,32,128]{3,2,1,0:T(8,128)(2,1)S(1)}, u32[]{:S(2)}, u32[]{:S(2)}) collective-permute-start(bf16[3,8,32,128]{3,2,1,0:T(8,128)(2,1)} %get-tuple-element.59), channel_id=1, source_target_pairs={{0,24},{8,16},{16,8},{24,0},{1,25},{9,17},{17,9},{25,1},{2,26},{10... | collective-permute-start | bytes 589832 | tf_op jit(solution)/shard_map/ppermute | solution.py:453
  9.4 0.6 collective-permute-start.2
  10.0 6.6 %analyse_wide.1 = bf16[32,32,1152]{2,1,0:T(8,128)(2,1)} custom-call(bf16[1024,1024]{1,0:T(8,128)(2,1)} %constant.153.clone.table_ref, bf16[2,1024,768]{2,1,0:T(8,128)(2,1)} %air_ref.2), custom_call_target="tpu_custom_call" | custom-call | flops 2684354560 | bytes 7602176 | tf_op jit(solution)/shard_map/analyse_wide/pallas_call | solution.py:111
  16.6 6.2 %all-to-all-start = ((bf16[32,32,1152]{2,1,0:T(8,128)(2,1)}), bf16[32,32,1152]{2,1,0:T(8,128)(2,1)}, u32[]{:S(2)}, u32[]{:S(2)}) async-start(bf16[32,32,1152]{2,1,0:T(8,128)(2,1)} %analyse_wide.1), calls=%async_computation | async-start | bytes 4718592 | tf_op jit(solution)/shard_map/all_to_all | solution.py:463
  22.8 0.7 pad_add_fusion.position_ref
  23.5 2.9 %collective-permute-done.1.refs_1_ = bf16[3,8,32,128]{3,2,1,0:T(8,128)(2,1)S(1)} collective-permute-done((bf16[3,8,32,128]{3,2,1,0:T(8,128)(2,1)}, bf16[3,8,32,128]{3,2,1,0:T(8,128)(2,1)S(1)}, u32[]{:S(2)}, u32[]{:S(2)}) %collective-permute-start.1) | collective-permute-done | bytes 196640 | tf_op jit(solution)/shard_map/ppermute | solution.py:453
  26.4 0.7 copy-done.5
  27.1 0.7 copy-done.6
  27.8 2.2 %to_plane.1 = (bf16[4,3,32,128]{3,2,1,0:T(8,128)(2,1)}, bf16[4,3,32,128]{3,2,1,0:T(8,128)(2,1)}, bf16[4,3,32,128]{3,2,1,0:T(8,128)(2,1)}, bf16[4,3,32,128]{3,2,1...) custom-call(s32[1]{0:T(128)} %bitcast.1.place_ref, ...), custom_call_target="tpu_custom_call" | custom-call | bytes 1572864 | tf_op jit(solution)/shard_map/to_plane/pallas_call | solution.py:222
  30.0 1.5 collective-permute-start.4
  31.5 0.3 collective-permute-start.5
  31.8 1.5 collective-permute-start.6
  33.4 0.2 collective-permute-start.7
  33.5 2.5 %collective-permute-start.8 = (bf16[4,3,32,128]{3,2,1,0:T(8,128)(2,1)}, bf16[4,3,32,128]{3,2,1,0:T(8,128)(2,1)S(1)}, u32[]{:S(2)}, u32[]{:S(2)}) collective-permute-start(bf16[4,3,32,128]{3,2,1,0:T(8,128)(2,1)} %get-tuple-element.78), channel_id=1, source_target_pairs={{0,6},{1,7},{2,4},{3,5},{4,2},{5,3},{6,0},{7,1},{8,14},{9,15},{10,... | collective-permute-start | bytes 294920 | tf_op jit(solution)/shard_map/ppermute | solution.py:456
  36.0 6.9 %collective-permute-done.4.refs_2_ = bf16[4,3,32,128]{3,2,1,0:T(8,128)(2,1)S(1)} collective-permute-done((bf16[4,3,32,128]{3,2,1,0:T(8,128)(2,1)}, bf16[4,3,32,128]{3,2,1,0:T(8,128)(2,1)S(1)}, u32[]{:S(2)}, u32[]{:S(2)}) %collective-permute-start.4) | collective-permute-done | bytes 98336 | tf_op jit(solution)/shard_map/ppermute | solution.py:456
  42.9 0.5 collective-permute-start.9
  43.4 0.9 convolution_convert_fusion.matrix_ref
  44.4 3.1 %collective-permute-done.7.refs_5_ = bf16[4,3,32,128]{3,2,1,0:T(8,128)(2,1)S(1)} collective-permute-done((bf16[4,3,32,128]{3,2,1,0:T(8,128)(2,1)}, bf16[4,3,32,128]{3,2,1,0:T(8,128)(2,1)S(1)}, u32[]{:S(2)}, u32[]{:S(2)}) %collective-permute-start.7) | collective-permute-done | bytes 98336 | tf_op jit(solution)/shard_map/ppermute | solution.py:456
  47.5 6.9 %collective-permute-done.8.refs_6_ = bf16[4,3,32,128]{3,2,1,0:T(8,128)(2,1)S(1)} collective-permute-done((bf16[4,3,32,128]{3,2,1,0:T(8,128)(2,1)}, bf16[4,3,32,128]{3,2,1,0:T(8,128)(2,1)S(1)}, u32[]{:S(2)}, u32[]{:S(2)}) %collective-permute-start.8) | collective-permute-done | bytes 98336 | tf_op jit(solution)/shard_map/ppermute | solution.py:456
  54.4 1.7 %collective-permute-done.9.refs_7_ = bf16[4,3,32,128]{3,2,1,0:T(8,128)(2,1)} collective-permute-done((bf16[4,3,32,128]{3,2,1,0:T(8,128)(2,1)}, bf16[4,3,32,128]{3,2,1,0:T(8,128)(2,1)}, u32[]{:S(2)}, u32[]{:S(2)}) %collective-permute-start.9) | collective-permute-done | bytes 98336 | tf_op jit(solution)/shard_map/ppermute | solution.py:456
  56.2 2.8 %latitudinal_slim.1 = (bf16[32,32,128]{2,1,0:T(8,128)(2,1)}, bf16[4,2,32,128]{3,2,1,0:T(8,128)(2,1)}, bf16[4,2,32,128]{3,2,1,0:T(8,128)(2,1)}, bf16[4,2,32,128]{...) custom-call(s32[2]{0:T(128)} %pad_add_fusion.position_ref, ...), custom_call_target="tpu_custom_call" | custom-call | flops 99999997952 | bytes 300000000 | tf_op jit(solution)/shard_map/latitudinal_slim/pallas_call | solution.py:280
  58.9 0.6 collective-permute-start.10
  59.5 1.4 collective-permute-start.11
  61.0 1.5 collective-permute-start.13
  62.4 0.6 collective-permute-start.14
  63.0 1.1 collective-permute-start.15
  64.2 1.2 collective-permute-start.16
  65.4 0.1 collective-permute-done.12.refs_3_
  65.5 1.5 collective-permute-done.13.refs_4_
  67.0 5.6 %collective-permute-done.14.refs_5_ = bf16[4,2,32,128]{3,2,1,0:T(8,128)(2,1)S(1)} collective-permute-done((bf16[4,2,32,128]{3,2,1,0:T(8,128)(2,1)}, bf16[4,2,32,128]{3,2,1,0:T(8,128)(2,1)S(1)}, u32[]{:S(2)}, u32[]{:S(2)}) %collective-permute-start.14) | collective-permute-done | bytes 65568 | tf_op jit(solution)/shard_map/ppermute | solution.py:456
  72.7 0.6 copy-done.11
  73.3 1.9 %from_plane.1 = (bf16[2,8,32,128]{3,2,1,0:T(8,128)(2,1)}, bf16[2,8,32,128]{3,2,1,0:T(8,128)(2,1)}, bf16[2,8,32,128]{3,2,1,0:T(8,128)(2,1)}, bf16[2,8,32,128]{3,2,1,0:T(8,128)(2,1)}) custom-call(s32[1]{0:T(128)} %bitcast.1.place_ref, bf16[4,2,32,128]{3,2,1,0:T(8,128)(2,1)} %get-tuple-element.80.refs_0_, bf16[4,2,32,128]{3,2,1,0:T(8,128)(2,1)} %copy-done.7, ...), custom_call_target="tpu_custom_call" | custom-call | bytes 1048576 | tf_op jit(solution)/shard_map/from_plane/pallas_call | solution.py:245
  75.2 2.6 %all-to-all-done.x_ref = bf16[32,32,1152]{2,1,0:T(8,128)(2,1)} async-done(((bf16[32,32,1152]{2,1,0:T(8,128)(2,1)}), bf16[32,32,1152]{2,1,0:T(8,128)(2,1)}, u32[]{:S(2)}, u32[]{:S(2)}) %all-to-all-start) | async-done | bytes 2359328 | tf_op jit(solution)/shard_map/all_to_all | solution.py:463
  77.8 2.4 %collective-permute-start.18 = (bf16[2,8,32,128]{3,2,1,0:T(8,128)(2,1)}, bf16[2,8,32,128]{3,2,1,0:T(8,128)(2,1)S(1)}, u32[]{:S(2)}, u32[]{:S(2)}) collective-permute-start(bf16[2,8,32,128]{3,2,1,0:T(8,128)(2,1)} %get-tuple-element.96), channel_id=1, source_target_pairs={{0,16},{8,24},{16,0},{24,8},{1,17},{9,25},{17,1},{25,9},{2,18},{10... | collective-permute-start | bytes 393224 | tf_op jit(solution)/shard_map/ppermute | solution.py:453
  80.2 1.9 %collective-permute-start.19 = (bf16[2,8,32,128]{3,2,1,0:T(8,128)(2,1)}, bf16[2,8,32,128]{3,2,1,0:T(8,128)(2,1)}, u32[]{:S(2)}, u32[]{:S(2)}) collective-permute-start(bf16[2,8,32,128]{3,2,1,0:T(8,128)(2,1)} %get-tuple-element.97), channel_id=1, source_target_pairs={{0,24},{8,16},{16,8},{24,0},{1,25},{9,17},{17,9},{25,1},{2,26},{10... | collective-permute-start | bytes 393224 | tf_op jit(solution)/shard_map/ppermute | solution.py:453
  82.2 5.0 %latitudinal_wide.1 = bf16[32,2,32,640]{3,2,1,0:T(8,128)(2,1)} custom-call(bf16[32,32,1152]{2,1,0:T(8,128)(2,1)} %all-to-all-done.x_ref, bf16[32,32,128]{2,1,0:T(8,128)(2,1)} %get-tuple-element.93.joined_ref, bf16[16,64,64]{2,1,0:T(8,128)(2,1)} %matrix_ref.1, f32[64,768]{1,0:T(8,128)} %damping_ref.3), custom_call_target="tpu_custom_call" | custom-call | flops 335544320 | bytes 4849664 | tf_op jit(solution)/shard_map/latitudinal_wide/pallas_call | solution.py:190
  87.2 4.4 %all-to-all-start.1 = ((bf16[32,2,32,640]{3,2,1,0:T(8,128)(2,1)}), bf16[32,2,32,640]{3,2,1,0:T(8,128)(2,1)}, u32[]{:S(2)}, u32[]{:S(2)}) async-start(bf16[32,2,32,640]{3,2,1,0:T(8,128)(2,1)} %latitudinal_wide.1), calls=%async_computation.1 | async-start | bytes 5242880 | tf_op jit(solution)/shard_map/all_to_all | solution.py:485
  91.7 0.2 copy.95
  92.0 0.4 copy-done.21
  92.4 0.3 copy-done.3
  92.7 1.5 fusion.14
  94.2 1.5 fusion.16
  95.8 1.6 %fusion.18 = f32[6,2,256,128]{3,2,1,0:T(8,128)} fusion(bf16[6,128,4,258]{1,3,2,0:T(8,128)(2,1)S(1)} %copy.95, bf16[3,3,128,128]{3,2,1,0:T(8,128)(2,1)S(1)} %copy-done.3), kind=kOutput, calls=%fused_computation.24 | convolution fusion | flops 100663296 | bytes 2392064 | tf_op jit(solution)/shard_map/io,sirw->sorw/dot_general | solution.py:65
  97.4 1.5 fusion.20
  98.9 1.5 fusion.36
  100.4 1.6 %fusion.22 = f32[6,2,256,128]{3,2,1,0:T(8,128)} fusion(bf16[6,128,4,258]{1,3,2,0:T(8,128)(2,1)S(1)} %copy.95, bf16[3,3,128,128]{3,2,1,0:T(8,128)(2,1)S(1)} %copy-done.3), kind=kOutput, calls=%fused_computation.28 | convolution fusion | flops 100663296 | bytes 2392064 | tf_op jit(solution)/shard_map/io,sirw->sorw/dot_general | solution.py:65
  102.0 1.5 fusion.24
  103.5 1.5 fusion.26
  105.0 1.5 fusion.28
  106.8 0.2 reduce_window_sum.11
  107.0 2.8 %fusion.12 = bf16[8,2,1024]{2,0,1:T(8,128)(2,1)S(1)} fusion(bf16[2,1024,768]{2,1,0:T(8,128)(2,1)} %air_ref.2, bf16[768,8]{0,1:T(8,128)(2,1)S(1)} %copy-done.14), kind=kOutput, calls=%fused_computation.17 | convolution fusion | flops 25182208 | bytes 3190784 | tf_op jit(solution)/shard_map/anc,cf->fan/dot_general | solution.py:398
  109.9 14.1 %all_gather.6 = bf16[8,8,1024]{2,0,1:T(8,128)(2,1)S(1)} all-gather(bf16[8,2,1024]{2,0,1:T(8,128)(2,1)S(1)} %fusion.12), channel_id=1, replica_groups=mesh['sec'=4,'band'=4,'ch'=2] {'band'}, dimensions={1}, use_global_device_ids=true | all-gather | bytes 163840 | tf_op jit(solution)/shard_map/all_gather | solution.py:404
  124.1 0.3 convert_reduce_fusion
  124.6 6.8 %fusion.9 = bf16[6,128,2,256]{1,3,2,0:T(8,128)(2,1)S(1)} fusion(f32[6,2,256,128]{3,2,1,0:T(8,128)} %fusion.14, f32[6,2,256,128]{3,2,1,0:T(8,128)} %fusion.16, f32[6,2,256,128]{3,2,1,0:T(8,128)} %fusion.18, f32[6,2,256,128]{3,2,1,0:T(8,128)} %fusion.20, f32[6,2,256,128]{3,2,1,0:T(8,128)} %fusion.36, f32[6,2,256,128]{3,2,1,0:T(8,128)} %fusion.22, ...), kind=kOutput, calls=%fused_computation.11 | convolution fusion | flops 116391936 | bytes 15828480 | tf_op jit(solution)/shard_map/io,sirw->sorw/dot_general | solution.py:74
  131.4 1.8 %copy.115 = bf16[6,128,2,256]{3,2,1,0:T(2,128)(2,1)} copy(bf16[6,128,2,256]{1,3,2,0:T(8,128)(2,1)S(1)} %fusion.9) | data formatting | bytes 1572864
  133.2 0.3 copy.113
  133.6 6.6 %all-gather = bf16[24,1,2,256]{3,2,1,0:T(2,128)(2,1)S(1)} all-gather(bf16[6,1,2,256]{3,2,1,0:T(2,128)(2,1)S(1)} %copy.113), channel_id=2, replica_groups=mesh['sec'=4,'band'=4,'ch'=2] {'band'}, dimensions={0}, use_global_device_ids=true | all-gather | bytes 30720 | tf_op jit(solution)/shard_map/all_gather | solution.py:542
  140.3 0.2 fusion.13
  140.6 1.2 stack.33.warmth_ref
  141.8 0.6 broadcast_in_dim.9.sea_ref
  142.4 3.0 %synthesise_slim.1.begun_ref = bf16[2,2,512,768]{3,2,1,0:T(8,128)(2,1)} custom-call(s32[1]{0:T(128)} %bitcast.sec_ref, bf16[2,512,512]{2,1,0:T(8,128)(2,1)} %constant.154.clone.table_ref, bf16[2,2,512,768]{3,2,1,0:T(8,128)(2,1)} %bitcast.125, bf16[2,2,16,512]{3,2,1,0:T(8,128)(2,1)} %broadcast_in_dim.9.sea_ref, bf16[16,768]{1,0:T(8,128)(2,1)} %stack.33.warmth_ref, ...), custom_call_target="tpu_custom_call" | custom-call | flops 99999997952 | bytes 300000000 | tf_op jit(solution)/shard_map/synthesise_slim/pallas_call | solution.py:338
  145.4 6.4 %all-to-all-done.1.coeff_ref = bf16[32,2,32,640]{3,2,1,0:T(8,128)(2,1)} async-done(((bf16[32,2,32,640]{3,2,1,0:T(8,128)(2,1)}), bf16[32,2,32,640]{3,2,1,0:T(8,128)(2,1)}, u32[]{:S(2)}, u32[]{:S(2)}) %all-to-all-start.1) | async-done | bytes 2621472 | tf_op jit(solution)/shard_map/all_to_all | solution.py:485
  151.8 5.8 %synthesise_wide.1 = bf16[2,2,512,768]{3,2,1,0:T(8,128)(2,1)} custom-call(bf16[2,512,512]{2,1,0:T(8,128)(2,1)} %constant.154.clone.table_ref, bf16[32,2,32,640]{3,2,1,0:T(8,128)(2,1)} %all-to-all-done.1.coeff_ref, bf16[2,2,512,768]{3,2,1,0:T(8,128)(2,1)} %bitcast.126, ...), custom_call_target="tpu_custom_call", output_to_operand_aliasing={{}: (5, {})} | custom-call | flops 1342177280 | bytes 8912896 | tf_op jit(solution)/shard_map/synthesise_wide/pallas_call | solution.py:377
  (96 shorter events, 1.1 us)
Async XLA Ops:
  0.6 124.0 %copy-start = (bf16[128,128]{1,0:T(8,128)(2,1)S(1)}, bf16[128,128]{1,0:T(8,128)(2,1)}, u32[]{:S(2)}) copy-start(bf16[128,128]{1,0:T(8,128)(2,1)} %param.26) | copy-start | bytes 98308
  4.4 19.1 %collective-permute-start = (bf16[3,8,32,128]{3,2,1,0:T(8,128)(2,1)}, bf16[3,8,32,128]{3,2,1,0:T(8,128)(2,1)S(1)}, u32[]{:S(2)}, u32[]{:S(2)}) collective-permute-start(bf16[3,8,32,128]{3,2,1,0:T(8,128)(2,1)} %get-tuple-element.59), channel_id=1, source_target_pairs={{0,24},{8,16},{16,8},{24,0},{1,25},{9,17},{17,9},{25,1},{2,26},{10... | collective-permute-start | bytes 589832 | tf_op jit(solution)/shard_map/ppermute | solution.py:453
  9.4 17.0 %collective-permute-start.1 = (bf16[3,8,32,128]{3,2,1,0:T(8,128)(2,1)}, bf16[3,8,32,128]{3,2,1,0:T(8,128)(2,1)S(1)}, u32[]{:S(2)}, u32[]{:S(2)}) collective-permute-start(bf16[3,8,32,128]{3,2,1,0:T(8,128)(2,1)} %get-tuple-element.60), channel_id=1, source_target_pairs={{0,16},{8,24},{16,0},{24,8},{1,17},{9,25},{17,1},{25,9},{2,18},{10... | collective-permute-start | bytes 589832 | tf_op jit(solution)/shard_map/ppermute | solution.py:453
  9.4 17.0 %collective-permute-start.2 = (bf16[3,8,32,128]{3,2,1,0:T(8,128)(2,1)}, bf16[3,8,32,128]{3,2,1,0:T(8,128)(2,1)S(1)}, u32[]{:S(2)}, u32[]{:S(2)}) collective-permute-start(bf16[3,8,32,128]{3,2,1,0:T(8,128)(2,1)} %get-tuple-element.61), channel_id=1, source_target_pairs={{0,8},{8,0},{16,24},{24,16},{1,9},{9,1},{17,25},{25,17},{2,10},{10... | collective-permute-start | bytes 589832 | tf_op jit(solution)/shard_map/ppermute | solution.py:453
  16.6 26.8 %copy-start.2 = (bf16[16,64,64]{2,1,0:T(8,128)(2,1)S(1)}, bf16[16,64,64]{2,1,0:T(8,128)(2,1)}, u32[]{:S(2)}) copy-start(bf16[16,64,64]{2,1,0:T(8,128)(2,1)} %matrix_ref.1) | copy-start | bytes 393220
  16.6 61.1 %all-to-all-start = ((bf16[32,32,1152]{2,1,0:T(8,128)(2,1)}), bf16[32,32,1152]{2,1,0:T(8,128)(2,1)}, u32[]{:S(2)}, u32[]{:S(2)}) async-start(bf16[32,32,1152]{2,1,0:T(8,128)(2,1)} %analyse_wide.1), calls=%async_computation | async-start | bytes 4718592 | tf_op jit(solution)/shard_map/all_to_all | solution.py:463
  23.5 2.9 %copy-start.4 = (bf16[3,8,32,128]{3,2,1,0:T(8,128)(2,1)}, bf16[3,8,32,128]{3,2,1,0:T(8,128)(2,1)S(1)}, u32[]{:S(2)}) copy-start(bf16[3,8,32,128]{3,2,1,0:T(8,128)(2,1)S(1)} %collective-permute-done.refs_0_) | copy-start | bytes 589828
  26.4 0.7 copy-start.5
  27.1 0.7 copy-start.6
  30.0 3.6 %collective-permute-start.3 = (bf16[4,3,32,128]{3,2,1,0:T(8,128)(2,1)}, bf16[4,3,32,128]{3,2,1,0:T(8,128)(2,1)S(1)}, u32[]{:S(2)}, u32[]{:S(2)}) collective-permute-start(bf16[4,3,32,128]{3,2,1,0:T(8,128)(2,1)} %get-tuple-element.73), channel_id=1, source_target_pairs={{0,1},{1,0},{2,3},{3,2},{4,5},{5,4},{6,7},{7,6},{8,9},{9,8},{10,11... | collective-permute-start | bytes 294920 | tf_op jit(solution)/shard_map/ppermute | solution.py:456
  30.0 12.9 %collective-permute-start.4 = (bf16[4,3,32,128]{3,2,1,0:T(8,128)(2,1)}, bf16[4,3,32,128]{3,2,1,0:T(8,128)(2,1)S(1)}, u32[]{:S(2)}, u32[]{:S(2)}) collective-permute-start(bf16[4,3,32,128]{3,2,1,0:T(8,128)(2,1)} %get-tuple-element.74), channel_id=1, source_target_pairs={{0,2},{1,3},{2,0},{3,1},{4,6},{5,7},{6,4},{7,5},{8,10},{9,11},{10,... | collective-permute-start | bytes 294920 | tf_op jit(solution)/shard_map/ppermute | solution.py:456
  31.5 12.9 %collective-permute-start.5 = (bf16[4,3,32,128]{3,2,1,0:T(8,128)(2,1)}, bf16[4,3,32,128]{3,2,1,0:T(8,128)(2,1)S(1)}, u32[]{:S(2)}, u32[]{:S(2)}) collective-permute-start(bf16[4,3,32,128]{3,2,1,0:T(8,128)(2,1)} %get-tuple-element.75), channel_id=1, source_target_pairs={{0,3},{1,2},{2,1},{3,0},{4,7},{5,6},{6,5},{7,4},{8,11},{9,10},{10,... | collective-permute-start | bytes 294920 | tf_op jit(solution)/shard_map/ppermute | solution.py:456
  31.8 12.6 %collective-permute-start.6 = (bf16[4,3,32,128]{3,2,1,0:T(8,128)(2,1)}, bf16[4,3,32,128]{3,2,1,0:T(8,128)(2,1)S(1)}, u32[]{:S(2)}, u32[]{:S(2)}) collective-permute-start(bf16[4,3,32,128]{3,2,1,0:T(8,128)(2,1)} %get-tuple-element.76), channel_id=1, source_target_pairs={{0,4},{1,5},{2,6},{3,7},{4,0},{5,1},{6,2},{7,3},{8,12},{9,13},{10,... | collective-permute-start | bytes 294920 | tf_op jit(solution)/shard_map/ppermute | solution.py:456
  33.4 14.1 %collective-permute-start.7 = (bf16[4,3,32,128]{3,2,1,0:T(8,128)(2,1)}, bf16[4,3,32,128]{3,2,1,0:T(8,128)(2,1)S(1)}, u32[]{:S(2)}, u32[]{:S(2)}) collective-permute-start(bf16[4,3,32,128]{3,2,1,0:T(8,128)(2,1)} %get-tuple-element.77), channel_id=1, source_target_pairs={{0,5},{1,4},{2,7},{3,6},{4,1},{5,0},{6,3},{7,2},{8,13},{9,12},{10,... | collective-permute-start | bytes 294920 | tf_op jit(solution)/shard_map/ppermute | solution.py:456
  33.5 22.6 %copy-start.23 = (bf16[4,3,32,128]{3,2,1,0:T(8,128)(2,1)}, bf16[4,3,32,128]{3,2,1,0:T(8,128)(2,1)S(1)}, u32[]{:S(2)}) copy-start(bf16[4,3,32,128]{3,2,1,0:T(8,128)(2,1)S(1)} %collective-permute-done.3.refs_1_) | copy-start | bytes 294916
  33.5 20.9 %collective-permute-start.8 = (bf16[4,3,32,128]{3,2,1,0:T(8,128)(2,1)}, bf16[4,3,32,128]{3,2,1,0:T(8,128)(2,1)S(1)}, u32[]{:S(2)}, u32[]{:S(2)}) collective-permute-start(bf16[4,3,32,128]{3,2,1,0:T(8,128)(2,1)} %get-tuple-element.78), channel_id=1, source_target_pairs={{0,6},{1,7},{2,4},{3,5},{4,2},{5,3},{6,0},{7,1},{8,14},{9,15},{10,... | collective-permute-start | bytes 294920 | tf_op jit(solution)/shard_map/ppermute | solution.py:456
  42.9 13.2 %copy-start.24 = (bf16[4,3,32,128]{3,2,1,0:T(8,128)(2,1)}, bf16[4,3,32,128]{3,2,1,0:T(8,128)(2,1)S(1)}, u32[]{:S(2)}) copy-start(bf16[4,3,32,128]{3,2,1,0:T(8,128)(2,1)S(1)} %collective-permute-done.4.refs_2_) | copy-start | bytes 294916
  42.9 13.2 %collective-permute-start.9 = (bf16[4,3,32,128]{3,2,1,0:T(8,128)(2,1)}, bf16[4,3,32,128]{3,2,1,0:T(8,128)(2,1)}, u32[]{:S(2)}, u32[]{:S(2)}) collective-permute-start(bf16[4,3,32,128]{3,2,1,0:T(8,128)(2,1)} %get-tuple-element.79), channel_id=1, source_target_pairs={{0,7},{1,6},{2,5},{3,4},{4,3},{5,2},{6,1},{7,0},{8,15},{9,14},{10,... | collective-permute-start | bytes 294920 | tf_op jit(solution)/shard_map/ppermute | solution.py:456
  44.3 21.1 %copy-start.15 = (s32[6,2,256]{2,1,0:T(2,128)S(1)}, s32[6,2,256]{2,1,0:T(2,128)}, u32[]{:S(2)}) copy-start(s32[6,2,256]{2,1,0:T(2,128)} %param.28) | copy-start | bytes 36868
  44.3 37.9 %copy-start.29 = (s32[6]{0:T(128)S(1)}, s32[6]{0:T(128)}, u32[]{:S(2)}) copy-start(s32[6]{0:T(128)} %param.29) | copy-start | bytes 76
  44.4 11.7 %copy-start.25 = (bf16[4,3,32,128]{3,2,1,0:T(8,128)(2,1)}, bf16[4,3,32,128]{3,2,1,0:T(8,128)(2,1)S(1)}, u32[]{:S(2)}) copy-start(bf16[4,3,32,128]{3,2,1,0:T(8,128)(2,1)S(1)} %collective-permute-done.5.refs_3_) | copy-start | bytes 294916
  44.4 11.7 %copy-start.26 = (bf16[4,3,32,128]{3,2,1,0:T(8,128)(2,1)}, bf16[4,3,32,128]{3,2,1,0:T(8,128)(2,1)S(1)}, u32[]{:S(2)}) copy-start(bf16[4,3,32,128]{3,2,1,0:T(8,128)(2,1)S(1)} %collective-permute-done.6.refs_4_) | copy-start | bytes 294916
  47.5 8.7 %copy-start.27 = (bf16[4,3,32,128]{3,2,1,0:T(8,128)(2,1)}, bf16[4,3,32,128]{3,2,1,0:T(8,128)(2,1)S(1)}, u32[]{:S(2)}) copy-start(bf16[4,3,32,128]{3,2,1,0:T(8,128)(2,1)S(1)} %collective-permute-done.7.refs_5_) | copy-start | bytes 294916
  54.4 1.8 %copy-start.28 = (bf16[4,3,32,128]{3,2,1,0:T(8,128)(2,1)}, bf16[4,3,32,128]{3,2,1,0:T(8,128)(2,1)S(1)}, u32[]{:S(2)}) copy-start(bf16[4,3,32,128]{3,2,1,0:T(8,128)(2,1)S(1)} %collective-permute-done.8.refs_6_) | copy-start | bytes 294916
  58.9 4.1 %collective-permute-start.10 = (bf16[4,2,32,128]{3,2,1,0:T(8,128)(2,1)}, bf16[4,2,32,128]{3,2,1,0:T(8,128)(2,1)S(1)}, u32[]{:S(2)}, u32[]{:S(2)}) collective-permute-start(bf16[4,2,32,128]{3,2,1,0:T(8,128)(2,1)} %get-tuple-element.81), channel_id=1, source_target_pairs={{0,1},{1,0},{2,3},{3,2},{4,5},{5,4},{6,7},{7,6},{8,9},{9,8},{10,11... | collective-permute-start | bytes 196616 | tf_op jit(solution)/shard_map/ppermute | solution.py:456
  59.5 4.6 %collective-permute-start.11 = (bf16[4,2,32,128]{3,2,1,0:T(8,128)(2,1)}, bf16[4,2,32,128]{3,2,1,0:T(8,128)(2,1)S(1)}, u32[]{:S(2)}, u32[]{:S(2)}) collective-permute-start(bf16[4,2,32,128]{3,2,1,0:T(8,128)(2,1)} %get-tuple-element.82), channel_id=1, source_target_pairs={{0,2},{1,3},{2,0},{3,1},{4,6},{5,7},{6,4},{7,5},{8,10},{9,11},{10,... | collective-permute-start | bytes 196616 | tf_op jit(solution)/shard_map/ppermute | solution.py:456
  60.9 4.6 %collective-permute-start.12 = (bf16[4,2,32,128]{3,2,1,0:T(8,128)(2,1)}, bf16[4,2,32,128]{3,2,1,0:T(8,128)(2,1)S(1)}, u32[]{:S(2)}, u32[]{:S(2)}) collective-permute-start(bf16[4,2,32,128]{3,2,1,0:T(8,128)(2,1)} %get-tuple-element.83), channel_id=1, source_target_pairs={{0,3},{1,2},{2,1},{3,0},{4,7},{5,6},{6,5},{7,4},{8,11},{9,10},{10,... | collective-permute-start | bytes 196616 | tf_op jit(solution)/shard_map/ppermute | solution.py:456
  61.0 6.0 %collective-permute-start.13 = (bf16[4,2,32,128]{3,2,1,0:T(8,128)(2,1)}, bf16[4,2,32,128]{3,2,1,0:T(8,128)(2,1)S(1)}, u32[]{:S(2)}, u32[]{:S(2)}) collective-permute-start(bf16[4,2,32,128]{3,2,1,0:T(8,128)(2,1)} %get-tuple-element.84), channel_id=1, source_target_pairs={{0,4},{1,5},{2,6},{3,7},{4,0},{5,1},{6,2},{7,3},{8,12},{9,13},{10,... | collective-permute-start | bytes 196616 | tf_op jit(solution)/shard_map/ppermute | solution.py:456
  62.4 10.2 %collective-permute-start.14 = (bf16[4,2,32,128]{3,2,1,0:T(8,128)(2,1)}, bf16[4,2,32,128]{3,2,1,0:T(8,128)(2,1)S(1)}, u32[]{:S(2)}, u32[]{:S(2)}) collective-permute-start(bf16[4,2,32,128]{3,2,1,0:T(8,128)(2,1)} %get-tuple-element.85), channel_id=1, source_target_pairs={{0,5},{1,4},{2,7},{3,6},{4,1},{5,0},{6,3},{7,2},{8,13},{9,12},{10,... | collective-permute-start | bytes 196616 | tf_op jit(solution)/shard_map/ppermute | solution.py:456
  63.0 9.6 %copy-start.7 = (bf16[4,2,32,128]{3,2,1,0:T(8,128)(2,1)}, bf16[4,2,32,128]{3,2,1,0:T(8,128)(2,1)S(1)}, u32[]{:S(2)}) copy-start(bf16[4,2,32,128]{3,2,1,0:T(8,128)(2,1)S(1)} %collective-permute-done.10.refs_1_) | copy-start | bytes 196612
  63.0 9.6 %collective-permute-start.15 = (bf16[4,2,32,128]{3,2,1,0:T(8,128)(2,1)}, bf16[4,2,32,128]{3,2,1,0:T(8,128)(2,1)S(1)}, u32[]{:S(2)}, u32[]{:S(2)}) collective-permute-start(bf16[4,2,32,128]{3,2,1,0:T(8,128)(2,1)} %get-tuple-element.86), channel_id=1, source_target_pairs={{0,6},{1,7},{2,4},{3,5},{4,2},{5,3},{6,0},{7,1},{8,14},{9,15},{10,... | collective-permute-start | bytes 196616 | tf_op jit(solution)/shard_map/ppermute | solution.py:456
  64.2 8.5 %copy-start.8 = (bf16[4,2,32,128]{3,2,1,0:T(8,128)(2,1)}, bf16[4,2,32,128]{3,2,1,0:T(8,128)(2,1)S(1)}, u32[]{:S(2)}) copy-start(bf16[4,2,32,128]{3,2,1,0:T(8,128)(2,1)S(1)} %collective-permute-done.11.refs_2_) | copy-start | bytes 196612
  64.2 8.5 %collective-permute-start.16 = (bf16[4,2,32,128]{3,2,1,0:T(8,128)(2,1)}, bf16[4,2,32,128]{3,2,1,0:T(8,128)(2,1)S(1)}, u32[]{:S(2)}, u32[]{:S(2)}) collective-permute-start(bf16[4,2,32,128]{3,2,1,0:T(8,128)(2,1)} %get-tuple-element.87), channel_id=1, source_target_pairs={{0,7},{1,6},{2,5},{3,4},{4,3},{5,2},{6,1},{7,0},{8,15},{9,14},{10,... | collective-permute-start | bytes 196616 | tf_op jit(solution)/shard_map/ppermute | solution.py:456
  65.5 7.2 %copy-start.9 = (bf16[4,2,32,128]{3,2,1,0:T(8,128)(2,1)}, bf16[4,2,32,128]{3,2,1,0:T(8,128)(2,1)S(1)}, u32[]{:S(2)}) copy-start(bf16[4,2,32,128]{3,2,1,0:T(8,128)(2,1)S(1)} %collective-permute-done.12.refs_3_) | copy-start | bytes 196612
  67.0 5.7 %copy-start.10 = (bf16[4,2,32,128]{3,2,1,0:T(8,128)(2,1)}, bf16[4,2,32,128]{3,2,1,0:T(8,128)(2,1)S(1)}, u32[]{:S(2)}) copy-start(bf16[4,2,32,128]{3,2,1,0:T(8,128)(2,1)S(1)} %collective-permute-done.13.refs_4_) | copy-start | bytes 196612
  72.6 0.6 copy-start.11
  72.6 0.6 copy-start.12
  72.6 0.7 copy-start.13
  77.8 13.9 %collective-permute-start.17 = (bf16[2,8,32,128]{3,2,1,0:T(8,128)(2,1)}, bf16[2,8,32,128]{3,2,1,0:T(8,128)(2,1)S(1)}, u32[]{:S(2)}, u32[]{:S(2)}) collective-permute-start(bf16[2,8,32,128]{3,2,1,0:T(8,128)(2,1)} %get-tuple-element.95), channel_id=1, source_target_pairs={{0,8},{8,0},{16,24},{24,16},{1,9},{9,1},{17,25},{25,17},{2,10},{10... | collective-permute-start | bytes 393224 | tf_op jit(solution)/shard_map/ppermute | solution.py:453
  77.8 13.9 %collective-permute-start.18 = (bf16[2,8,32,128]{3,2,1,0:T(8,128)(2,1)}, bf16[2,8,32,128]{3,2,1,0:T(8,128)(2,1)S(1)}, u32[]{:S(2)}, u32[]{:S(2)}) collective-permute-start(bf16[2,8,32,128]{3,2,1,0:T(8,128)(2,1)} %get-tuple-element.96), channel_id=1, source_target_pairs={{0,16},{8,24},{16,0},{24,8},{1,17},{9,25},{17,1},{25,9},{2,18},{10... | collective-permute-start | bytes 393224 | tf_op jit(solution)/shard_map/ppermute | solution.py:453
  80.2 11.5 %collective-permute-start.19 = (bf16[2,8,32,128]{3,2,1,0:T(8,128)(2,1)}, bf16[2,8,32,128]{3,2,1,0:T(8,128)(2,1)}, u32[]{:S(2)}, u32[]{:S(2)}) collective-permute-start(bf16[2,8,32,128]{3,2,1,0:T(8,128)(2,1)} %get-tuple-element.97), channel_id=1, source_target_pairs={{0,24},{8,16},{16,8},{24,0},{1,25},{9,17},{17,9},{25,1},{2,26},{10... | collective-permute-start | bytes 393224 | tf_op jit(solution)/shard_map/ppermute | solution.py:453
  87.2 4.5 %copy-start.1 = (bf16[6,128,4,258]{1,2,3,0:T(4,128)(2,1)S(1)}, bf16[6,128,4,258]{1,2,3,0:T(4,128)(2,1)}, u32[]{:S(2)}) copy-start(bf16[6,128,4,258]{1,2,3,0:T(4,128)(2,1)} %param.21) | copy-start | bytes 4755460
  87.2 64.6 %all-to-all-start.1 = ((bf16[32,2,32,640]{3,2,1,0:T(8,128)(2,1)}), bf16[32,2,32,640]{3,2,1,0:T(8,128)(2,1)}, u32[]{:S(2)}, u32[]{:S(2)}) async-start(bf16[32,2,32,640]{3,2,1,0:T(8,128)(2,1)} %latitudinal_wide.1), calls=%async_computation.1 | async-start | bytes 5242880 | tf_op jit(solution)/shard_map/all_to_all | solution.py:485
  91.7 1.1 copy-start.3
  91.7 0.7 copy-start.21
  91.7 0.7 copy-start.22
  105.0 1.5 copy-start.19
  105.0 2.0 %copy-start.14 = (bf16[768,8]{0,1:T(8,128)(2,1)S(1)}, bf16[768,8]{0,1:T(8,128)(2,1)}, u32[]{:S(2)}) copy-start(bf16[768,8]{0,1:T(8,128)(2,1)} %param.19) | copy-start | bytes 36868
  107.0 17.5 %copy-start.16 = (f32[8,128]{1,0:T(8,128)S(1)}, f32[8,128]{1,0:T(8,128)}, u32[]{:S(2)}) copy-start(f32[8,128]{1,0:T(8,128)} %param.24) | copy-start | bytes 12292
  107.0 17.6 %copy-start.18 = (bf16[8,128]{1,0:T(8,128)(2,1)S(1)}, bf16[8,128]{1,0:T(8,128)(2,1)}, u32[]{:S(2)}) copy-start(bf16[8,128]{1,0:T(8,128)(2,1)} %param.23) | copy-start | bytes 6148
  107.0 17.6 %copy-start.20 = (f32[128]{0:T(128)S(1)}, f32[128]{0:T(128)}, u32[]{:S(2)}) copy-start(f32[128]{0:T(128)} %param.25) | copy-start | bytes 1540
  131.4 9.1 %copy-start.17 = (f32[768]{0:T(1024)S(1)}, f32[768]{0:T(1024)}, u32[]{:S(2)}) copy-start(f32[768]{0:T(1024)} %param.20) | copy-start | bytes 9220

commit v7 on v6

--- a/solution.py
+++ b/solution.py
@@ -315,7 +315,7 @@
 
     def body(sec_ref, table_ref, air_ref, sea_ref, warmth_ref, *refs):
         part_refs, out_ref, gathered = refs[:sections], refs[-2], refs[-1]
-        for o, part_ref in enumerate(part_refs):
+        for o, part_ref in enumerate(part_refs[::-1]):
             for a in range(lines):
                 for odd in range(2):
                     gathered[odd, sec_ref[0] ^ o, :, :, a * width : (a + 1) * width] = part_ref[
@@ -352,7 +352,7 @@
         compiler_params=compiler_params(),
         cost_estimate=pl.CostEstimate(flops=10**11, bytes_accessed=3 * 10**8, transcendentals=0),
         name="synthesise_slim",
-    )(sec, table, air, sea, warmth, *parts)
+    )(sec, table, air, sea, warmth, *parts[::-1])
 
 
 def synthesise_wide(coeffs, table, air, sea, warmth, begun):

time: 158 us -> 158 us (level)
  no operation moved by 1% of the time
where the time goes in v7:
time: 158 us
  waiting for transfers between devices  37.9 us (24%)
  starting transfers between devices  33.5 us (21%)
  Pallas kernels  31.1 us (20%)
  matrix products  24.8 us (16%)
  blocking collectives  20.7 us (13%)
  local copies, waits for them, and re-layouts  7.45 us (5%)
    ppermute x14, waiting for transfers between devices, over_plane(): lax.ppermute(blocks[p], ('band', 'ch'), twists[p])  26 us
    all_gather x1, blocking collectives, gather_flux(): return lax.all_gather(flux_local, 'band', axis=1, tiled=True)  14.1 us
    dot_general x9, matrix products, ocean_update(): jnp.einsum('io,sirw->sorw', kernel_coefficients[shift_row, shift_col], wi...  13.8 us
    ppermute x14, starting transfers between devices, over_plane(): lax.ppermute(blocks[p], ('band', 'ch'), twists[p])  12.9 us
    all_to_all x2, starting transfers between devices, shards(): lax.all_to_all(wide_coeffs, AXES, split_axis=0, concat_axis=0, tiled=True)  10.6 us
    ppermute x6, starting transfers between devices, over_sections(): lax.ppermute(x, 'sec', hops[o])  10 us
    all_to_all x2, waiting for transfers between devices, shards(): lax.all_to_all(wide_coeffs, AXES, split_axis=0, concat_axis=0, tiled=True)  8.97 us
    dot_general x1, matrix products, ocean_update(): jnp.einsum('io,sirw->sorw', water_readout_matrix, hidden, preferred_eleme...  6.79 us
  transfers between devices with their start and end apart: 22, of which 11 were waited for; matrix products, arithmetic and copies ran while one was open for 19% of the time, Pallas kernels for 14%

profile of v7, /device:TPU:0, one launch (start us, length us, event | category | flops | bytes accessed | tf_op | source)
XLA Modules:
  0.0 157.6 jit_solution(8524038762661977388)
XLA Ops:
  0.7 3.7 %analyse_slim.1 = (bf16[3,8,32,128]{3,2,1,0:T(8,128)(2,1)}, bf16[3,8,32,128]{3,2,1,0:T(8,128)(2,1)}, bf16[3,8,32,128]{3,2,1,0:T(8,128)(2,1)}, bf16[3,8,32,128]{3,2,1,0:T(8,128)(2,1)}) custom-call(s32[1]{0:T(128)} %bitcast.sec_ref, bf16[1024,1024]{1,0:T(8,128)(2,1)} %constant.153.clone.table_ref, bf16[2,1024,768]{2,1,0:T(8,128)(2,1)} %air_ref.2, ...), custom_call_target="tpu_custom_call" | custom-call | flops 805306368 | bytes 3670016 | tf_op jit(solution)/shard_map/analyse_slim/pallas_call | solution.py:143
  4.4 5.0 %collective-permute-start = (bf16[3,8,32,128]{3,2,1,0:T(8,128)(2,1)}, bf16[3,8,32,128]{3,2,1,0:T(8,128)(2,1)S(1)}, u32[]{:S(2)}, u32[]{:S(2)}) collective-permute-start(bf16[3,8,32,128]{3,2,1,0:T(8,128)(2,1)} %get-tuple-element.59), channel_id=1, source_target_pairs={{0,24},{8,16},{16,8},{24,0},{1,25},{9,17},{17,9},{25,1},{2,26},{10... | collective-permute-start | bytes 589832 | tf_op jit(solution)/shard_map/ppermute | solution.py:453
  9.4 0.6 collective-permute-start.2
  10.0 6.6 %analyse_wide.1 = bf16[32,32,1152]{2,1,0:T(8,128)(2,1)} custom-call(bf16[1024,1024]{1,0:T(8,128)(2,1)} %constant.153.clone.table_ref, bf16[2,1024,768]{2,1,0:T(8,128)(2,1)} %air_ref.2), custom_call_target="tpu_custom_call" | custom-call | flops 2684354560 | bytes 7602176 | tf_op jit(solution)/shard_map/analyse_wide/pallas_call | solution.py:111
  16.6 6.2 %all-to-all-start = ((bf16[32,32,1152]{2,1,0:T(8,128)(2,1)}), bf16[32,32,1152]{2,1,0:T(8,128)(2,1)}, u32[]{:S(2)}, u32[]{:S(2)}) async-start(bf16[32,32,1152]{2,1,0:T(8,128)(2,1)} %analyse_wide.1), calls=%async_computation | async-start | bytes 4718592 | tf_op jit(solution)/shard_map/all_to_all | solution.py:463
  22.8 0.7 pad_add_fusion.position_ref
  23.5 2.9 %collective-permute-done.1.refs_1_ = bf16[3,8,32,128]{3,2,1,0:T(8,128)(2,1)S(1)} collective-permute-done((bf16[3,8,32,128]{3,2,1,0:T(8,128)(2,1)}, bf16[3,8,32,128]{3,2,1,0:T(8,128)(2,1)S(1)}, u32[]{:S(2)}, u32[]{:S(2)}) %collective-permute-start.1) | collective-permute-done | bytes 196640 | tf_op jit(solution)/shard_map/ppermute | solution.py:453
  26.4 0.7 copy-done.5
  27.1 0.7 copy-done.6
  27.8 2.2 %to_plane.1 = (bf16[4,3,32,128]{3,2,1,0:T(8,128)(2,1)}, bf16[4,3,32,128]{3,2,1,0:T(8,128)(2,1)}, bf16[4,3,32,128]{3,2,1,0:T(8,128)(2,1)}, bf16[4,3,32,128]{3,2,1...) custom-call(s32[1]{0:T(128)} %bitcast.1.place_ref, ...), custom_call_target="tpu_custom_call" | custom-call | bytes 1572864 | tf_op jit(solution)/shard_map/to_plane/pallas_call | solution.py:222
  30.0 1.5 collective-permute-start.4
  31.5 0.3 collective-permute-start.5
  31.8 1.5 collective-permute-start.6
  33.4 0.2 collective-permute-start.7
  33.5 2.5 %collective-permute-start.8 = (bf16[4,3,32,128]{3,2,1,0:T(8,128)(2,1)}, bf16[4,3,32,128]{3,2,1,0:T(8,128)(2,1)S(1)}, u32[]{:S(2)}, u32[]{:S(2)}) collective-permute-start(bf16[4,3,32,128]{3,2,1,0:T(8,128)(2,1)} %get-tuple-element.78), channel_id=1, source_target_pairs={{0,6},{1,7},{2,4},{3,5},{4,2},{5,3},{6,0},{7,1},{8,14},{9,15},{10,... | collective-permute-start | bytes 294920 | tf_op jit(solution)/shard_map/ppermute | solution.py:456
  36.0 6.9 %collective-permute-done.4.refs_2_ = bf16[4,3,32,128]{3,2,1,0:T(8,128)(2,1)S(1)} collective-permute-done((bf16[4,3,32,128]{3,2,1,0:T(8,128)(2,1)}, bf16[4,3,32,128]{3,2,1,0:T(8,128)(2,1)S(1)}, u32[]{:S(2)}, u32[]{:S(2)}) %collective-permute-start.4) | collective-permute-done | bytes 98336 | tf_op jit(solution)/shard_map/ppermute | solution.py:456
  42.9 0.5 collective-permute-start.9
  43.4 0.9 convolution_convert_fusion.matrix_ref
  44.4 3.1 %collective-permute-done.7.refs_5_ = bf16[4,3,32,128]{3,2,1,0:T(8,128)(2,1)S(1)} collective-permute-done((bf16[4,3,32,128]{3,2,1,0:T(8,128)(2,1)}, bf16[4,3,32,128]{3,2,1,0:T(8,128)(2,1)S(1)}, u32[]{:S(2)}, u32[]{:S(2)}) %collective-permute-start.7) | collective-permute-done | bytes 98336 | tf_op jit(solution)/shard_map/ppermute | solution.py:456
  47.5 6.9 %collective-permute-done.8.refs_6_ = bf16[4,3,32,128]{3,2,1,0:T(8,128)(2,1)S(1)} collective-permute-done((bf16[4,3,32,128]{3,2,1,0:T(8,128)(2,1)}, bf16[4,3,32,128]{3,2,1,0:T(8,128)(2,1)S(1)}, u32[]{:S(2)}, u32[]{:S(2)}) %collective-permute-start.8) | collective-permute-done | bytes 98336 | tf_op jit(solution)/shard_map/ppermute | solution.py:456
  54.4 1.7 %collective-permute-done.9.refs_7_ = bf16[4,3,32,128]{3,2,1,0:T(8,128)(2,1)} collective-permute-done((bf16[4,3,32,128]{3,2,1,0:T(8,128)(2,1)}, bf16[4,3,32,128]{3,2,1,0:T(8,128)(2,1)}, u32[]{:S(2)}, u32[]{:S(2)}) %collective-permute-start.9) | collective-permute-done | bytes 98336 | tf_op jit(solution)/shard_map/ppermute | solution.py:456
  56.2 2.8 %latitudinal_slim.1 = (bf16[32,32,128]{2,1,0:T(8,128)(2,1)}, bf16[4,2,32,128]{3,2,1,0:T(8,128)(2,1)}, bf16[4,2,32,128]{3,2,1,0:T(8,128)(2,1)}, bf16[4,2,32,128]{...) custom-call(s32[2]{0:T(128)} %pad_add_fusion.position_ref, ...), custom_call_target="tpu_custom_call" | custom-call | flops 99999997952 | bytes 300000000 | tf_op jit(solution)/shard_map/latitudinal_slim/pallas_call | solution.py:280
  58.9 0.6 collective-permute-start.10
  59.5 1.4 collective-permute-start.11
  61.0 1.5 collective-permute-start.13
  62.4 0.6 collective-permute-start.14
  63.0 1.1 collective-permute-start.15
  64.2 1.2 collective-permute-start.16
  65.4 0.1 collective-permute-done.12.refs_3_
  65.5 1.5 collective-permute-done.13.refs_4_
  67.0 5.6 %collective-permute-done.14.refs_5_ = bf16[4,2,32,128]{3,2,1,0:T(8,128)(2,1)S(1)} collective-permute-done((bf16[4,2,32,128]{3,2,1,0:T(8,128)(2,1)}, bf16[4,2,32,128]{3,2,1,0:T(8,128)(2,1)S(1)}, u32[]{:S(2)}, u32[]{:S(2)}) %collective-permute-start.14) | collective-permute-done | bytes 65568 | tf_op jit(solution)/shard_map/ppermute | solution.py:456
  72.7 0.6 copy-done.11
  73.3 1.9 %from_plane.1 = (bf16[2,8,32,128]{3,2,1,0:T(8,128)(2,1)}, bf16[2,8,32,128]{3,2,1,0:T(8,128)(2,1)}, bf16[2,8,32,128]{3,2,1,0:T(8,128)(2,1)}, bf16[2,8,32,128]{3,2,1,0:T(8,128)(2,1)}) custom-call(s32[1]{0:T(128)} %bitcast.1.place_ref, bf16[4,2,32,128]{3,2,1,0:T(8,128)(2,1)} %get-tuple-element.80.refs_0_, bf16[4,2,32,128]{3,2,1,0:T(8,128)(2,1)} %copy-done.7, ...), custom_call_target="tpu_custom_call" | custom-call | bytes 1048576 | tf_op jit(solution)/shard_map/from_plane/pallas_call | solution.py:245
  75.2 2.6 %all-to-all-done.x_ref = bf16[32,32,1152]{2,1,0:T(8,128)(2,1)} async-done(((bf16[32,32,1152]{2,1,0:T(8,128)(2,1)}), bf16[32,32,1152]{2,1,0:T(8,128)(2,1)}, u32[]{:S(2)}, u32[]{:S(2)}) %all-to-all-start) | async-done | bytes 2359328 | tf_op jit(solution)/shard_map/all_to_all | solution.py:463
  77.8 2.4 %collective-permute-start.18 = (bf16[2,8,32,128]{3,2,1,0:T(8,128)(2,1)}, bf16[2,8,32,128]{3,2,1,0:T(8,128)(2,1)S(1)}, u32[]{:S(2)}, u32[]{:S(2)}) collective-permute-start(bf16[2,8,32,128]{3,2,1,0:T(8,128)(2,1)} %get-tuple-element.96), channel_id=1, source_target_pairs={{0,16},{8,24},{16,0},{24,8},{1,17},{9,25},{17,1},{25,9},{2,18},{10... | collective-permute-start | bytes 393224 | tf_op jit(solution)/shard_map/ppermute | solution.py:453
  80.2 1.9 %collective-permute-start.19 = (bf16[2,8,32,128]{3,2,1,0:T(8,128)(2,1)}, bf16[2,8,32,128]{3,2,1,0:T(8,128)(2,1)}, u32[]{:S(2)}, u32[]{:S(2)}) collective-permute-start(bf16[2,8,32,128]{3,2,1,0:T(8,128)(2,1)} %get-tuple-element.97), channel_id=1, source_target_pairs={{0,24},{8,16},{16,8},{24,0},{1,25},{9,17},{17,9},{25,1},{2,26},{10... | collective-permute-start | bytes 393224 | tf_op jit(solution)/shard_map/ppermute | solution.py:453
  82.2 5.0 %latitudinal_wide.1 = bf16[32,2,32,640]{3,2,1,0:T(8,128)(2,1)} custom-call(bf16[32,32,1152]{2,1,0:T(8,128)(2,1)} %all-to-all-done.x_ref, bf16[32,32,128]{2,1,0:T(8,128)(2,1)} %get-tuple-element.93.joined_ref, bf16[16,64,64]{2,1,0:T(8,128)(2,1)} %matrix_ref.1, f32[64,768]{1,0:T(8,128)} %damping_ref.3), custom_call_target="tpu_custom_call" | custom-call | flops 335544320 | bytes 4849664 | tf_op jit(solution)/shard_map/latitudinal_wide/pallas_call | solution.py:190
  87.2 4.4 %all-to-all-start.1 = ((bf16[32,2,32,640]{3,2,1,0:T(8,128)(2,1)}), bf16[32,2,32,640]{3,2,1,0:T(8,128)(2,1)}, u32[]{:S(2)}, u32[]{:S(2)}) async-start(bf16[32,2,32,640]{3,2,1,0:T(8,128)(2,1)} %latitudinal_wide.1), calls=%async_computation.1 | async-start | bytes 5242880 | tf_op jit(solution)/shard_map/all_to_all | solution.py:485
  91.7 0.2 copy.95
  92.0 0.4 copy-done.21
  92.4 0.3 copy-done.3
  92.7 1.5 fusion.14
  94.2 1.5 fusion.16
  95.8 1.6 %fusion.18 = f32[6,2,256,128]{3,2,1,0:T(8,128)} fusion(bf16[6,128,4,258]{1,3,2,0:T(8,128)(2,1)S(1)} %copy.95, bf16[3,3,128,128]{3,2,1,0:T(8,128)(2,1)S(1)} %copy-done.3), kind=kOutput, calls=%fused_computation.24 | convolution fusion | flops 100663296 | bytes 2392064 | tf_op jit(solution)/shard_map/io,sirw->sorw/dot_general | solution.py:65
  97.4 1.5 fusion.20
  98.9 1.5 fusion.36
  100.4 1.6 %fusion.22 = f32[6,2,256,128]{3,2,1,0:T(8,128)} fusion(bf16[6,128,4,258]{1,3,2,0:T(8,128)(2,1)S(1)} %copy.95, bf16[3,3,128,128]{3,2,1,0:T(8,128)(2,1)S(1)} %copy-done.3), kind=kOutput, calls=%fused_computation.28 | convolution fusion | flops 100663296 | bytes 2392064 | tf_op jit(solution)/shard_map/io,sirw->sorw/dot_general | solution.py:65
  102.0 1.5 fusion.24
  103.5 1.5 fusion.26
  105.0 1.5 fusion.28
  106.8 0.2 reduce_window_sum.11
  107.0 2.8 %fusion.12 = bf16[8,2,1024]{2,0,1:T(8,128)(2,1)S(1)} fusion(bf16[2,1024,768]{2,1,0:T(8,128)(2,1)} %air_ref.2, bf16[768,8]{0,1:T(8,128)(2,1)S(1)} %copy-done.14), kind=kOutput, calls=%fused_computation.17 | convolution fusion | flops 25182208 | bytes 3190784 | tf_op jit(solution)/shard_map/anc,cf->fan/dot_general | solution.py:398
  109.9 14.1 %all_gather.6 = bf16[8,8,1024]{2,0,1:T(8,128)(2,1)S(1)} all-gather(bf16[8,2,1024]{2,0,1:T(8,128)(2,1)S(1)} %fusion.12), channel_id=1, replica_groups=mesh['sec'=4,'band'=4,'ch'=2] {'band'}, dimensions={1}, use_global_device_ids=true | all-gather | bytes 163840 | tf_op jit(solution)/shard_map/all_gather | solution.py:404
  124.1 0.3 convert_reduce_fusion
  124.6 6.8 %fusion.9 = bf16[6,128,2,256]{1,3,2,0:T(8,128)(2,1)S(1)} fusion(f32[6,2,256,128]{3,2,1,0:T(8,128)} %fusion.14, f32[6,2,256,128]{3,2,1,0:T(8,128)} %fusion.16, f32[6,2,256,128]{3,2,1,0:T(8,128)} %fusion.18, f32[6,2,256,128]{3,2,1,0:T(8,128)} %fusion.20, f32[6,2,256,128]{3,2,1,0:T(8,128)} %fusion.36, f32[6,2,256,128]{3,2,1,0:T(8,128)} %fusion.22, ...), kind=kOutput, calls=%fused_computation.11 | convolution fusion | flops 116391936 | bytes 15828480 | tf_op jit(solution)/shard_map/io,sirw->sorw/dot_general | solution.py:74
  131.4 1.8 %copy.115 = bf16[6,128,2,256]{3,2,1,0:T(2,128)(2,1)} copy(bf16[6,128,2,256]{1,3,2,0:T(8,128)(2,1)S(1)} %fusion.9) | data formatting | bytes 1572864
  133.2 0.3 copy.113
  133.6 6.6 %all-gather = bf16[24,1,2,256]{3,2,1,0:T(2,128)(2,1)S(1)} all-gather(bf16[6,1,2,256]{3,2,1,0:T(2,128)(2,1)S(1)} %copy.113), channel_id=2, replica_groups=mesh['sec'=4,'band'=4,'ch'=2] {'band'}, dimensions={0}, use_global_device_ids=true | all-gather | bytes 30720 | tf_op jit(solution)/shard_map/all_gather | solution.py:542
  140.3 0.2 fusion.13
  140.6 1.2 stack.33.warmth_ref
  141.8 0.6 broadcast_in_dim.9.sea_ref
  142.4 3.0 %synthesise_slim.1.begun_ref = bf16[2,2,512,768]{3,2,1,0:T(8,128)(2,1)} custom-call(s32[1]{0:T(128)} %bitcast.sec_ref, bf16[2,512,512]{2,1,0:T(8,128)(2,1)} %constant.154.clone.table_ref, bf16[2,2,512,768]{3,2,1,0:T(8,128)(2,1)} %bitcast.125, bf16[2,2,16,512]{3,2,1,0:T(8,128)(2,1)} %broadcast_in_dim.9.sea_ref, bf16[16,768]{1,0:T(8,128)(2,1)} %stack.33.warmth_ref, ...), custom_call_target="tpu_custom_call" | custom-call | flops 99999997952 | bytes 300000000 | tf_op jit(solution)/shard_map/synthesise_slim/pallas_call | solution.py:338
  145.4 6.4 %all-to-all-done.1.coeff_ref = bf16[32,2,32,640]{3,2,1,0:T(8,128)(2,1)} async-done(((bf16[32,2,32,640]{3,2,1,0:T(8,128)(2,1)}), bf16[32,2,32,640]{3,2,1,0:T(8,128)(2,1)}, u32[]{:S(2)}, u32[]{:S(2)}) %all-to-all-start.1) | async-done | bytes 2621472 | tf_op jit(solution)/shard_map/all_to_all | solution.py:485
  151.8 5.8 %synthesise_wide.1 = bf16[2,2,512,768]{3,2,1,0:T(8,128)(2,1)} custom-call(bf16[2,512,512]{2,1,0:T(8,128)(2,1)} %constant.154.clone.table_ref, bf16[32,2,32,640]{3,2,1,0:T(8,128)(2,1)} %all-to-all-done.1.coeff_ref, bf16[2,2,512,768]{3,2,1,0:T(8,128)(2,1)} %bitcast.126, ...), custom_call_target="tpu_custom_call", output_to_operand_aliasing={{}: (5, {})} | custom-call | flops 1342177280 | bytes 8912896 | tf_op jit(solution)/shard_map/synthesise_wide/pallas_call | solution.py:377
  (96 shorter events, 1.1 us)
Async XLA Ops:
  0.6 124.0 %copy-start = (bf16[128,128]{1,0:T(8,128)(2,1)S(1)}, bf16[128,128]{1,0:T(8,128)(2,1)}, u32[]{:S(2)}) copy-start(bf16[128,128]{1,0:T(8,128)(2,1)} %param.26) | copy-start | bytes 98308
  4.4 19.1 %collective-permute-start = (bf16[3,8,32,128]{3,2,1,0:T(8,128)(2,1)}, bf16[3,8,32,128]{3,2,1,0:T(8,128)(2,1)S(1)}, u32[]{:S(2)}, u32[]{:S(2)}) collective-permute-start(bf16[3,8,32,128]{3,2,1,0:T(8,128)(2,1)} %get-tuple-element.59), channel_id=1, source_target_pairs={{0,24},{8,16},{16,8},{24,0},{1,25},{9,17},{17,9},{25,1},{2,26},{10... | collective-permute-start | bytes 589832 | tf_op jit(solution)/shard_map/ppermute | solution.py:453
  9.4 17.0 %collective-permute-start.1 = (bf16[3,8,32,128]{3,2,1,0:T(8,128)(2,1)}, bf16[3,8,32,128]{3,2,1,0:T(8,128)(2,1)S(1)}, u32[]{:S(2)}, u32[]{:S(2)}) collective-permute-start(bf16[3,8,32,128]{3,2,1,0:T(8,128)(2,1)} %get-tuple-element.60), channel_id=1, source_target_pairs={{0,16},{8,24},{16,0},{24,8},{1,17},{9,25},{17,1},{25,9},{2,18},{10... | collective-permute-start | bytes 589832 | tf_op jit(solution)/shard_map/ppermute | solution.py:453
  9.4 17.0 %collective-permute-start.2 = (bf16[3,8,32,128]{3,2,1,0:T(8,128)(2,1)}, bf16[3,8,32,128]{3,2,1,0:T(8,128)(2,1)S(1)}, u32[]{:S(2)}, u32[]{:S(2)}) collective-permute-start(bf16[3,8,32,128]{3,2,1,0:T(8,128)(2,1)} %get-tuple-element.61), channel_id=1, source_target_pairs={{0,8},{8,0},{16,24},{24,16},{1,9},{9,1},{17,25},{25,17},{2,10},{10... | collective-permute-start | bytes 589832 | tf_op jit(solution)/shard_map/ppermute | solution.py:453
  16.6 26.8 %copy-start.2 = (bf16[16,64,64]{2,1,0:T(8,128)(2,1)S(1)}, bf16[16,64,64]{2,1,0:T(8,128)(2,1)}, u32[]{:S(2)}) copy-start(bf16[16,64,64]{2,1,0:T(8,128)(2,1)} %matrix_ref.1) | copy-start | bytes 393220
  16.6 61.1 %all-to-all-start = ((bf16[32,32,1152]{2,1,0:T(8,128)(2,1)}), bf16[32,32,1152]{2,1,0:T(8,128)(2,1)}, u32[]{:S(2)}, u32[]{:S(2)}) async-start(bf16[32,32,1152]{2,1,0:T(8,128)(2,1)} %analyse_wide.1), calls=%async_computation | async-start | bytes 4718592 | tf_op jit(solution)/shard_map/all_to_all | solution.py:463
  23.5 2.9 %copy-start.4 = (bf16[3,8,32,128]{3,2,1,0:T(8,128)(2,1)}, bf16[3,8,32,128]{3,2,1,0:T(8,128)(2,1)S(1)}, u32[]{:S(2)}) copy-start(bf16[3,8,32,128]{3,2,1,0:T(8,128)(2,1)S(1)} %collective-permute-done.refs_0_) | copy-start | bytes 589828
  26.4 0.7 copy-start.5
  27.1 0.7 copy-start.6
  30.0 3.6 %collective-permute-start.3 = (bf16[4,3,32,128]{3,2,1,0:T(8,128)(2,1)}, bf16[4,3,32,128]{3,2,1,0:T(8,128)(2,1)S(1)}, u32[]{:S(2)}, u32[]{:S(2)}) collective-permute-start(bf16[4,3,32,128]{3,2,1,0:T(8,128)(2,1)} %get-tuple-element.73), channel_id=1, source_target_pairs={{0,1},{1,0},{2,3},{3,2},{4,5},{5,4},{6,7},{7,6},{8,9},{9,8},{10,11... | collective-permute-start | bytes 294920 | tf_op jit(solution)/shard_map/ppermute | solution.py:456
  30.0 12.9 %collective-permute-start.4 = (bf16[4,3,32,128]{3,2,1,0:T(8,128)(2,1)}, bf16[4,3,32,128]{3,2,1,0:T(8,128)(2,1)S(1)}, u32[]{:S(2)}, u32[]{:S(2)}) collective-permute-start(bf16[4,3,32,128]{3,2,1,0:T(8,128)(2,1)} %get-tuple-element.74), channel_id=1, source_target_pairs={{0,2},{1,3},{2,0},{3,1},{4,6},{5,7},{6,4},{7,5},{8,10},{9,11},{10,... | collective-permute-start | bytes 294920 | tf_op jit(solution)/shard_map/ppermute | solution.py:456
  31.5 12.9 %collective-permute-start.5 = (bf16[4,3,32,128]{3,2,1,0:T(8,128)(2,1)}, bf16[4,3,32,128]{3,2,1,0:T(8,128)(2,1)S(1)}, u32[]{:S(2)}, u32[]{:S(2)}) collective-permute-start(bf16[4,3,32,128]{3,2,1,0:T(8,128)(2,1)} %get-tuple-element.75), channel_id=1, source_target_pairs={{0,3},{1,2},{2,1},{3,0},{4,7},{5,6},{6,5},{7,4},{8,11},{9,10},{10,... | collective-permute-start | bytes 294920 | tf_op jit(solution)/shard_map/ppermute | solution.py:456
  31.8 12.6 %collective-permute-start.6 = (bf16[4,3,32,128]{3,2,1,0:T(8,128)(2,1)}, bf16[4,3,32,128]{3,2,1,0:T(8,128)(2,1)S(1)}, u32[]{:S(2)}, u32[]{:S(2)}) collective-permute-start(bf16[4,3,32,128]{3,2,1,0:T(8,128)(2,1)} %get-tuple-element.76), channel_id=1, source_target_pairs={{0,4},{1,5},{2,6},{3,7},{4,0},{5,1},{6,2},{7,3},{8,12},{9,13},{10,... | collective-permute-start | bytes 294920 | tf_op jit(solution)/shard_map/ppermute | solution.py:456
  33.4 14.1 %collective-permute-start.7 = (bf16[4,3,32,128]{3,2,1,0:T(8,128)(2,1)}, bf16[4,3,32,128]{3,2,1,0:T(8,128)(2,1)S(1)}, u32[]{:S(2)}, u32[]{:S(2)}) collective-permute-start(bf16[4,3,32,128]{3,2,1,0:T(8,128)(2,1)} %get-tuple-element.77), channel_id=1, source_target_pairs={{0,5},{1,4},{2,7},{3,6},{4,1},{5,0},{6,3},{7,2},{8,13},{9,12},{10,... | collective-permute-start | bytes 294920 | tf_op jit(solution)/shard_map/ppermute | solution.py:456
  33.5 22.6 %copy-start.23 = (bf16[4,3,32,128]{3,2,1,0:T(8,128)(2,1)}, bf16[4,3,32,128]{3,2,1,0:T(8,128)(2,1)S(1)}, u32[]{:S(2)}) copy-start(bf16[4,3,32,128]{3,2,1,0:T(8,128)(2,1)S(1)} %collective-permute-done.3.refs_1_) | copy-start | bytes 294916
  33.5 20.9 %collective-permute-start.8 = (bf16[4,3,32,128]{3,2,1,0:T(8,128)(2,1)}, bf16[4,3,32,128]{3,2,1,0:T(8,128)(2,1)S(1)}, u32[]{:S(2)}, u32[]{:S(2)}) collective-permute-start(bf16[4,3,32,128]{3,2,1,0:T(8,128)(2,1)} %get-tuple-element.78), channel_id=1, source_target_pairs={{0,6},{1,7},{2,4},{3,5},{4,2},{5,3},{6,0},{7,1},{8,14},{9,15},{10,... | collective-permute-start | bytes 294920 | tf_op jit(solution)/shard_map/ppermute | solution.py:456
  42.9 13.2 %copy-start.24 = (bf16[4,3,32,128]{3,2,1,0:T(8,128)(2,1)}, bf16[4,3,32,128]{3,2,1,0:T(8,128)(2,1)S(1)}, u32[]{:S(2)}) copy-start(bf16[4,3,32,128]{3,2,1,0:T(8,128)(2,1)S(1)} %collective-permute-done.4.refs_2_) | copy-start | bytes 294916
  42.9 13.2 %collective-permute-start.9 = (bf16[4,3,32,128]{3,2,1,0:T(8,128)(2,1)}, bf16[4,3,32,128]{3,2,1,0:T(8,128)(2,1)}, u32[]{:S(2)}, u32[]{:S(2)}) collective-permute-start(bf16[4,3,32,128]{3,2,1,0:T(8,128)(2,1)} %get-tuple-element.79), channel_id=1, source_target_pairs={{0,7},{1,6},{2,5},{3,4},{4,3},{5,2},{6,1},{7,0},{8,15},{9,14},{10,... | collective-permute-start | bytes 294920 | tf_op jit(solution)/shard_map/ppermute | solution.py:456
  44.3 21.1 %copy-start.15 = (s32[6,2,256]{2,1,0:T(2,128)S(1)}, s32[6,2,256]{2,1,0:T(2,128)}, u32[]{:S(2)}) copy-start(s32[6,2,256]{2,1,0:T(2,128)} %param.28) | copy-start | bytes 36868
  44.3 37.9 %copy-start.29 = (s32[6]{0:T(128)S(1)}, s32[6]{0:T(128)}, u32[]{:S(2)}) copy-start(s32[6]{0:T(128)} %param.29) | copy-start | bytes 76
  44.4 11.7 %copy-start.25 = (bf16[4,3,32,128]{3,2,1,0:T(8,128)(2,1)}, bf16[4,3,32,128]{3,2,1,0:T(8,128)(2,1)S(1)}, u32[]{:S(2)}) copy-start(bf16[4,3,32,128]{3,2,1,0:T(8,128)(2,1)S(1)} %collective-permute-done.5.refs_3_) | copy-start | bytes 294916
  44.4 11.7 %copy-start.26 = (bf16[4,3,32,128]{3,2,1,0:T(8,128)(2,1)}, bf16[4,3,32,128]{3,2,1,0:T(8,128)(2,1)S(1)}, u32[]{:S(2)}) copy-start(bf16[4,3,32,128]{3,2,1,0:T(8,128)(2,1)S(1)} %collective-permute-done.6.refs_4_) | copy-start | bytes 294916
  47.5 8.7 %copy-start.27 = (bf16[4,3,32,128]{3,2,1,0:T(8,128)(2,1)}, bf16[4,3,32,128]{3,2,1,0:T(8,128)(2,1)S(1)}, u32[]{:S(2)}) copy-start(bf16[4,3,32,128]{3,2,1,0:T(8,128)(2,1)S(1)} %collective-permute-done.7.refs_5_) | copy-start | bytes 294916
  54.4 1.8 %copy-start.28 = (bf16[4,3,32,128]{3,2,1,0:T(8,128)(2,1)}, bf16[4,3,32,128]{3,2,1,0:T(8,128)(2,1)S(1)}, u32[]{:S(2)}) copy-start(bf16[4,3,32,128]{3,2,1,0:T(8,128)(2,1)S(1)} %collective-permute-done.8.refs_6_) | copy-start | bytes 294916
  58.9 4.1 %collective-permute-start.10 = (bf16[4,2,32,128]{3,2,1,0:T(8,128)(2,1)}, bf16[4,2,32,128]{3,2,1,0:T(8,128)(2,1)S(1)}, u32[]{:S(2)}, u32[]{:S(2)}) collective-permute-start(bf16[4,2,32,128]{3,2,1,0:T(8,128)(2,1)} %get-tuple-element.81), channel_id=1, source_target_pairs={{0,1},{1,0},{2,3},{3,2},{4,5},{5,4},{6,7},{7,6},{8,9},{9,8},{10,11... | collective-permute-start | bytes 196616 | tf_op jit(solution)/shard_map/ppermute | solution.py:456
  59.5 4.6 %collective-permute-start.11 = (bf16[4,2,32,128]{3,2,1,0:T(8,128)(2,1)}, bf16[4,2,32,128]{3,2,1,0:T(8,128)(2,1)S(1)}, u32[]{:S(2)}, u32[]{:S(2)}) collective-permute-start(bf16[4,2,32,128]{3,2,1,0:T(8,128)(2,1)} %get-tuple-element.82), channel_id=1, source_target_pairs={{0,2},{1,3},{2,0},{3,1},{4,6},{5,7},{6,4},{7,5},{8,10},{9,11},{10,... | collective-permute-start | bytes 196616 | tf_op jit(solution)/shard_map/ppermute | solution.py:456
  60.9 4.6 %collective-permute-start.12 = (bf16[4,2,32,128]{3,2,1,0:T(8,128)(2,1)}, bf16[4,2,32,128]{3,2,1,0:T(8,128)(2,1)S(1)}, u32[]{:S(2)}, u32[]{:S(2)}) collective-permute-start(bf16[4,2,32,128]{3,2,1,0:T(8,128)(2,1)} %get-tuple-element.83), channel_id=1, source_target_pairs={{0,3},{1,2},{2,1},{3,0},{4,7},{5,6},{6,5},{7,4},{8,11},{9,10},{10,... | collective-permute-start | bytes 196616 | tf_op jit(solution)/shard_map/ppermute | solution.py:456
  61.0 6.0 %collective-permute-start.13 = (bf16[4,2,32,128]{3,2,1,0:T(8,128)(2,1)}, bf16[4,2,32,128]{3,2,1,0:T(8,128)(2,1)S(1)}, u32[]{:S(2)}, u32[]{:S(2)}) collective-permute-start(bf16[4,2,32,128]{3,2,1,0:T(8,128)(2,1)} %get-tuple-element.84), channel_id=1, source_target_pairs={{0,4},{1,5},{2,6},{3,7},{4,0},{5,1},{6,2},{7,3},{8,12},{9,13},{10,... | collective-permute-start | bytes 196616 | tf_op jit(solution)/shard_map/ppermute | solution.py:456
  62.4 10.2 %collective-permute-start.14 = (bf16[4,2,32,128]{3,2,1,0:T(8,128)(2,1)}, bf16[4,2,32,128]{3,2,1,0:T(8,128)(2,1)S(1)}, u32[]{:S(2)}, u32[]{:S(2)}) collective-permute-start(bf16[4,2,32,128]{3,2,1,0:T(8,128)(2,1)} %get-tuple-element.85), channel_id=1, source_target_pairs={{0,5},{1,4},{2,7},{3,6},{4,1},{5,0},{6,3},{7,2},{8,13},{9,12},{10,... | collective-permute-start | bytes 196616 | tf_op jit(solution)/shard_map/ppermute | solution.py:456
  63.0 9.6 %copy-start.7 = (bf16[4,2,32,128]{3,2,1,0:T(8,128)(2,1)}, bf16[4,2,32,128]{3,2,1,0:T(8,128)(2,1)S(1)}, u32[]{:S(2)}) copy-start(bf16[4,2,32,128]{3,2,1,0:T(8,128)(2,1)S(1)} %collective-permute-done.10.refs_1_) | copy-start | bytes 196612
  63.0 9.6 %collective-permute-start.15 = (bf16[4,2,32,128]{3,2,1,0:T(8,128)(2,1)}, bf16[4,2,32,128]{3,2,1,0:T(8,128)(2,1)S(1)}, u32[]{:S(2)}, u32[]{:S(2)}) collective-permute-start(bf16[4,2,32,128]{3,2,1,0:T(8,128)(2,1)} %get-tuple-element.86), channel_id=1, source_target_pairs={{0,6},{1,7},{2,4},{3,5},{4,2},{5,3},{6,0},{7,1},{8,14},{9,15},{10,... | collective-permute-start | bytes 196616 | tf_op jit(solution)/shard_map/ppermute | solution.py:456
  64.2 8.5 %copy-start.8 = (bf16[4,2,32,128]{3,2,1,0:T(8,128)(2,1)}, bf16[4,2,32,128]{3,2,1,0:T(8,128)(2,1)S(1)}, u32[]{:S(2)}) copy-start(bf16[4,2,32,128]{3,2,1,0:T(8,128)(2,1)S(1)} %collective-permute-done.11.refs_2_) | copy-start | bytes 196612
  64.2 8.5 %collective-permute-start.16 = (bf16[4,2,32,128]{3,2,1,0:T(8,128)(2,1)}, bf16[4,2,32,128]{3,2,1,0:T(8,128)(2,1)S(1)}, u32[]{:S(2)}, u32[]{:S(2)}) collective-permute-start(bf16[4,2,32,128]{3,2,1,0:T(8,128)(2,1)} %get-tuple-element.87), channel_id=1, source_target_pairs={{0,7},{1,6},{2,5},{3,4},{4,3},{5,2},{6,1},{7,0},{8,15},{9,14},{10,... | collective-permute-start | bytes 196616 | tf_op jit(solution)/shard_map/ppermute | solution.py:456
  65.5 7.2 %copy-start.9 = (bf16[4,2,32,128]{3,2,1,0:T(8,128)(2,1)}, bf16[4,2,32,128]{3,2,1,0:T(8,128)(2,1)S(1)}, u32[]{:S(2)}) copy-start(bf16[4,2,32,128]{3,2,1,0:T(8,128)(2,1)S(1)} %collective-permute-done.12.refs_3_) | copy-start | bytes 196612
  67.0 5.7 %copy-start.10 = (bf16[4,2,32,128]{3,2,1,0:T(8,128)(2,1)}, bf16[4,2,32,128]{3,2,1,0:T(8,128)(2,1)S(1)}, u32[]{:S(2)}) copy-start(bf16[4,2,32,128]{3,2,1,0:T(8,128)(2,1)S(1)} %collective-permute-done.13.refs_4_) | copy-start | bytes 196612
  72.6 0.6 copy-start.11
  72.6 0.6 copy-start.12
  72.6 0.7 copy-start.13
  77.8 13.9 %collective-permute-start.17 = (bf16[2,8,32,128]{3,2,1,0:T(8,128)(2,1)}, bf16[2,8,32,128]{3,2,1,0:T(8,128)(2,1)S(1)}, u32[]{:S(2)}, u32[]{:S(2)}) collective-permute-start(bf16[2,8,32,128]{3,2,1,0:T(8,128)(2,1)} %get-tuple-element.95), channel_id=1, source_target_pairs={{0,8},{8,0},{16,24},{24,16},{1,9},{9,1},{17,25},{25,17},{2,10},{10... | collective-permute-start | bytes 393224 | tf_op jit(solution)/shard_map/ppermute | solution.py:453
  77.8 13.9 %collective-permute-start.18 = (bf16[2,8,32,128]{3,2,1,0:T(8,128)(2,1)}, bf16[2,8,32,128]{3,2,1,0:T(8,128)(2,1)S(1)}, u32[]{:S(2)}, u32[]{:S(2)}) collective-permute-start(bf16[2,8,32,128]{3,2,1,0:T(8,128)(2,1)} %get-tuple-element.96), channel_id=1, source_target_pairs={{0,16},{8,24},{16,0},{24,8},{1,17},{9,25},{17,1},{25,9},{2,18},{10... | collective-permute-start | bytes 393224 | tf_op jit(solution)/shard_map/ppermute | solution.py:453
  80.2 11.5 %collective-permute-start.19 = (bf16[2,8,32,128]{3,2,1,0:T(8,128)(2,1)}, bf16[2,8,32,128]{3,2,1,0:T(8,128)(2,1)}, u32[]{:S(2)}, u32[]{:S(2)}) collective-permute-start(bf16[2,8,32,128]{3,2,1,0:T(8,128)(2,1)} %get-tuple-element.97), channel_id=1, source_target_pairs={{0,24},{8,16},{16,8},{24,0},{1,25},{9,17},{17,9},{25,1},{2,26},{10... | collective-permute-start | bytes 393224 | tf_op jit(solution)/shard_map/ppermute | solution.py:453
  87.2 4.5 %copy-start.1 = (bf16[6,128,4,258]{1,2,3,0:T(4,128)(2,1)S(1)}, bf16[6,128,4,258]{1,2,3,0:T(4,128)(2,1)}, u32[]{:S(2)}) copy-start(bf16[6,128,4,258]{1,2,3,0:T(4,128)(2,1)} %param.21) | copy-start | bytes 4755460
  87.2 64.6 %all-to-all-start.1 = ((bf16[32,2,32,640]{3,2,1,0:T(8,128)(2,1)}), bf16[32,2,32,640]{3,2,1,0:T(8,128)(2,1)}, u32[]{:S(2)}, u32[]{:S(2)}) async-start(bf16[32,2,32,640]{3,2,1,0:T(8,128)(2,1)} %latitudinal_wide.1), calls=%async_computation.1 | async-start | bytes 5242880 | tf_op jit(solution)/shard_map/all_to_all | solution.py:485
  91.7 1.1 copy-start.3
  91.7 0.7 copy-start.21
  91.7 0.7 copy-start.22
  105.0 1.5 copy-start.19
  105.0 2.0 %copy-start.14 = (bf16[768,8]{0,1:T(8,128)(2,1)S(1)}, bf16[768,8]{0,1:T(8,128)(2,1)}, u32[]{:S(2)}) copy-start(bf16[768,8]{0,1:T(8,128)(2,1)} %param.19) | copy-start | bytes 36868
  107.0 17.5 %copy-start.16 = (f32[8,128]{1,0:T(8,128)S(1)}, f32[8,128]{1,0:T(8,128)}, u32[]{:S(2)}) copy-start(f32[8,128]{1,0:T(8,128)} %param.24) | copy-start | bytes 12292
  107.0 17.6 %copy-start.18 = (bf16[8,128]{1,0:T(8,128)(2,1)S(1)}, bf16[8,128]{1,0:T(8,128)(2,1)}, u32[]{:S(2)}) copy-start(bf16[8,128]{1,0:T(8,128)(2,1)} %param.23) | copy-start | bytes 6148
  107.0 17.6 %copy-start.20 = (f32[128]{0:T(128)S(1)}, f32[128]{0:T(128)}, u32[]{:S(2)}) copy-start(f32[128]{0:T(128)} %param.25) | copy-start | bytes 1540
  131.4 9.1 %copy-start.17 = (f32[768]{0:T(1024)S(1)}, f32[768]{0:T(1024)}, u32[]{:S(2)}) copy-start(f32[768]{0:T(1024)} %param.20) | copy-start | bytes 9220
